TPU v7x, 256 devices: a whole 4x4x8 slice. The times are simulated.
256 devices in a mesh: tm: 16 (over y, x), tile: 16 (over z, core).
Axes of the slice: x: 4, y: 4, z: 8, core: 2. Of those that a mesh axis runs over, the one named last changes fastest.
Arguments:
- activations: bfloat16 [128, 64, 16, 256], P('tm', 'tile'), may hold values from -6 to 6
- grad_output: bfloat16 [128, 128, 32, 128], P('tm', 'tile'), may hold values from -6 to 6
- conv_weight: bfloat16 [27, 256, 128], replicated, may hold values from -0.078125 to 0.078125
- frame_counts: int32 [16], P('tm'), may hold values from 2 to 8, as said below
Outputs:
- grad_input: bfloat16 [128, 64, 16, 256], P('tm', 'tile')
- grad_weight: float32 [27, 256, 128], replicated
Inputs may be any that keep to these rules, and one draw needn't show every extreme that they name: `frame_counts`: every device uses at least 2 of its 8 slots, and in every draw some device uses all 8.
All inputs are finite; a program needn't handle non-finite values.
Results may differ from a plain program's by a relative error of at most 0.001.
Values may be sent and summed in bfloat16 or wider, within the bound.
No kernel may reach another device: no remote copies, remote signals or barrier semaphores. Data moves between devices by JAX's collectives and lax.ppermute only.
A program may use at most 192 MiB of HBM per device.

v0:
```python
import math

import jax
import jax.numpy as jnp
from jax import lax
from jax.sharding import PartitionSpec as P


def padded(cells, sides, width):
    for axis, dim in sides:
        count = lax.axis_size(axis)
        ends = count - 1
        head = lax.slice_in_dim(cells, 0, width, axis=dim)
        tail = lax.slice_in_dim(cells, cells.shape[dim] - width, cells.shape[dim], axis=dim)
        cells = jnp.concatenate(
            [
                lax.ppermute(tail, axis, [(i, (i + 1) % count) for i in range(ends)]),
                cells,
                lax.ppermute(head, axis, [((i + 1) % count, i) for i in range(ends)]),
            ],
            axis=dim,
        )
    return cells


def passed_along(value, axis, steps):
    count = lax.axis_size(axis)
    leading, last = (max(0, -steps), min(count, count - steps))
    return lax.ppermute(value, axis, [(source, source + steps) for source in range(leading, last)])


def shards(activations, grad_output, conv_weight, frame_counts):
    slot_cap, rows_latent, cols_latent, chan_in = activations.shape
    frames_used = frame_counts[0]
    high = 2 * rows_latent
    wide = 2 * cols_latent
    latent_rim = padded(activations, (("tile", 1),), 1)
    last_two = lax.dynamic_slice_in_dim(latent_rim, frames_used - 2, 2, 0)
    earlier = passed_along(last_two, "tm", 1)
    latent_ext = jnp.concatenate([earlier, latent_rim], axis=0)
    upsampled = jnp.repeat(jnp.repeat(latent_ext, 2, axis=1), 2, axis=2)[:, 1:-1]
    upsampled = jnp.pad(upsampled, ((0, 0), (0, 0), (1, 1), (0, 0)))
    live_slots = jnp.arange(slot_cap, dtype=jnp.int32) < frames_used
    grad_masked = jnp.where(
        live_slots[:, None, None, None], grad_output, jnp.zeros((), jnp.bfloat16)
    )
    output_rim = padded(grad_masked, (("tile", 1),), 1)
    first_two = output_rim[:2]
    later = passed_along(first_two, "tm", -1)
    grad_ext = jnp.concatenate(
        [output_rim, jnp.zeros((2,) + output_rim.shape[1:], jnp.bfloat16)], axis=0
    )
    grad_ext = lax.dynamic_update_slice_in_dim(grad_ext, later, frames_used, 0)
    grad_ext = jnp.pad(grad_ext, ((0, 0), (0, 0), (1, 1), (0, 0)))
    weight_terms = []
    grad_up = jnp.zeros((slot_cap, high, wide, chan_in), jnp.float32)
    for depth_tap in range(3):
        for row_tap in range(3):
            for col_tap in range(3):
                tap_index = 9 * depth_tap + 3 * row_tap + col_tap
                u_piece = upsampled[
                    depth_tap : depth_tap + slot_cap,
                    row_tap : row_tap + high,
                    col_tap : col_tap + wide,
                ]
                weight_terms.append(
                    jnp.einsum(
                        "thwc,thwo->co", u_piece, grad_masked, preferred_element_type=jnp.float32
                    )
                )
                g_piece = grad_ext[
                    2 - depth_tap : 2 - depth_tap + slot_cap,
                    2 - row_tap : 2 - row_tap + high,
                    2 - col_tap : 2 - col_tap + wide,
                ]
                grad_up = grad_up + jnp.einsum(
                    "thwo,co->thwc",
                    g_piece,
                    conv_weight[tap_index],
                    preferred_element_type=jnp.float32,
                )
    local_weight = jnp.stack(weight_terms, axis=0)
    summed = lax.psum(local_weight, ("tm", "tile"))
    full_positions = (
        lax.axis_size("tm") * slot_cap * 4 * rows_latent * lax.axis_size("tile") * cols_latent
    )
    grad_weight = summed * (1.0 / math.sqrt(full_positions))
    blocked = grad_up.reshape(slot_cap, rows_latent, 2, cols_latent, 2, chan_in)
    grad_latent = jnp.sum(blocked, axis=(2, 4))
    grad_input = jnp.where(live_slots[:, None, None, None], grad_latent, jnp.zeros((), jnp.float32))
    return (grad_input.astype(jnp.bfloat16), grad_weight)


def solution(mesh):
    placed = (P("tm", "tile", None, None), P("tm", "tile", None, None), P(), P("tm"))
    return jax.shard_map(
        shards,
        mesh=mesh,
        in_specs=placed,
        out_specs=(P("tm", "tile", None, None), P()),
        check_vma=False,
    )
```

profile of v0, /device:TPU:1, one launch (start us, length us, event | category | flops | bytes accessed | tf_op | source)
XLA Modules:
  0.0 349.8 jit_solution(4906643997433646999)
XLA Ops:
  8.1 4.9 %collective-permute-start.3 = (bf16[8,1,16,256]{3,2,1,0:T(8,128)(2,1)S(1)}, bf16[8,1,16,256]{3,2,1,0:T(8,128)(2,1)S(1)}, u32[]{:S(2)}, u32[]{:S(2)}) collective-permute-start(bf16[8,1,16,256]{3,2,1,0:T(8,128)(2,1)S(1)} %get-tuple-element.5), channel_id=1, source_target_pairs={{0,1},{1,2},{2,3},{3,4},{4,5},{5,6},{6,7},{7,8},{8,9},{9,10},{10,1... | collective-permute-start | bytes 196616 | tf_op jit(solution)/shard_map/ppermute | solution.py:17
  13.7 1.1 broadcast_select_fusion
  14.9 1.9 collective-permute-start.1
  16.8 3.6 %collective-permute-start = (bf16[8,1,32,128]{3,2,1,0:T(8,128)(2,1)S(1)}, bf16[8,1,32,128]{3,2,1,0:T(8,128)(2,1)S(1)}, u32[]{:S(2)}, u32[]{:S(2)}) collective-permute-start(bf16[8,1,32,128]{3,2,1,0:T(8,128)(2,1)S(1)} %get-tuple-element.2), channel_id=1, source_target_pairs={{0,1},{1,2},{2,3},{3,4},{4,5},{5,6},{6,7},{7,8},{8,9},{9,10},{10,1... | collective-permute-start | bytes 196616 | tf_op jit(solution)/shard_map/ppermute | solution.py:17
  20.5 1.9 collective-permute-start.4
  23.4 2.6 collective-permute-done.4
  26.1 3.1 collective-permute-start.5
  29.4 1.3 collective-permute-start.2
  31.0 2.3 broadcast_in_dim.38
  33.3 2.2 reshape.19
  35.5 1.6 slice.378
  37.1 1.1 fusion.26
  44.3 1.1 fusion.22
  51.1 1.1 fusion.18
  58.0 1.1 fusion.14
  64.8 1.1 fusion.10
  67.1 1.4 fusion.9
  69.5 1.3 fusion.46
  70.8 1.7 fusion.43
  72.6 1.8 fusion.42
  74.3 1.8 fusion.50
  76.1 1.8 fusion.41
  77.9 1.7 fusion.40
  79.7 1.8 fusion.54
  81.5 1.8 fusion.39
  83.3 1.8 fusion.38
  85.0 1.8 fusion.58
  86.8 1.8 fusion.37
  88.6 1.8 fusion.36
  90.3 1.8 fusion.62
  92.1 1.7 fusion.35
  93.9 1.8 fusion.34
  95.7 1.8 fusion.66
  97.5 1.7 fusion.33
  99.2 1.7 fusion.32
  100.9 1.7 fusion.70
  102.7 1.7 fusion.31
  104.4 1.8 fusion.30
  106.2 1.7 fusion.74
  107.9 1.8 fusion.29
  109.7 1.7 fusion.28
  111.4 1.7 fusion.27
  113.2 1.7 fusion.78
  114.9 19.1 %add_add_fusion = f32[8,8,32,256]{3,2,1,0:T(8,128)} fusion(f32[8,8,32,256]{3,2,1,0:T(8,128)S(1)} %fusion.46, f32[8,8,32,256]{3,2,1,0:T(8,128)} %fusion.43, f32[8,8,32,256]{3,2,1,0:T(8,128)} %fusion.42, f32[8,8,32,256]{3,2,1,0:T(8,128)} %fusion.50, f32[8,8,32,256]{3,2,1,0:T(8,128)} %fusion.41, f32[8,8,32,256]{3,2,1,0:T(8,128)} %fusion.40, ...), kind=kOutput, calls=%fused_computation | convolution fusion | flops 147849216 | bytes 57507840 | tf_op jit(solution)/shard_map/thwo,co->thwc/dot_general | solution.py:76
  134.0 2.8 reshape.17
  136.7 1.9 reduce_sum.9
  139.5 199.2 %all-reduce.5.cloned.1.call-done = f32[27,256,128]{2,1,0:T(8,128)} async-done(((f32[27,256,128]{2,1,0:T(8,128)}), f32[27,256,128]{2,1,0:T(8,128)}) %all-reduce.5.cloned.1.call-update) | async-done | bytes 3538960 | tf_op jit(solution)/shard_map/psum | solution.py:83
  338.7 4.3 %broadcast_multiply_fusion = f32[27,256,128]{2,1,0:T(8,128)} fusion(f32[27,256,128]{2,1,0:T(8,128)} %all-reduce.5.cloned.1.call-done), kind=kLoop, calls=%fused_computation.1 | loop fusion | flops 884736 | bytes 7077888 | tf_op jit(solution)/shard_map/mul | solution.py:87
  (47 shorter events, 28.6 us)
Async XLA Ops:
  7.2 331.5 %all-reduce.5.cloned.1.call-start = ((), (), s32[]{:S(2)}) async-start(), calls=%async_computation | async-start | bytes 7077888 | tf_op jit(solution)/shard_map/psum | solution.py:83
  8.1 14.3 %collective-permute-start.3 = (bf16[8,1,16,256]{3,2,1,0:T(8,128)(2,1)S(1)}, bf16[8,1,16,256]{3,2,1,0:T(8,128)(2,1)S(1)}, u32[]{:S(2)}, u32[]{:S(2)}) collective-permute-start(bf16[8,1,16,256]{3,2,1,0:T(8,128)(2,1)S(1)} %get-tuple-element.5), channel_id=1, source_target_pairs={{0,1},{1,2},{2,3},{3,4},{4,5},{5,6},{6,7},{7,8},{8,9},{9,10},{10,1... | collective-permute-start | bytes 196616 | tf_op jit(solution)/shard_map/ppermute | solution.py:17
  14.9 14.3 %collective-permute-start.1 = (bf16[8,1,32,128]{3,2,1,0:T(8,128)(2,1)S(1)}, bf16[8,1,32,128]{3,2,1,0:T(8,128)(2,1)S(1)}, u32[]{:S(2)}, u32[]{:S(2)}) collective-permute-start(bf16[8,1,32,128]{3,2,1,0:T(8,128)(2,1)S(1)} %get-tuple-element.3), channel_id=1, source_target_pairs={{1,0},{2,1},{3,2},{4,3},{5,4},{6,5},{7,6},{8,7},{9,8},{10,9},{11,1... | collective-permute-start | bytes 196616 | tf_op jit(solution)/shard_map/ppermute | solution.py:19
  16.8 12.4 %collective-permute-start = (bf16[8,1,32,128]{3,2,1,0:T(8,128)(2,1)S(1)}, bf16[8,1,32,128]{3,2,1,0:T(8,128)(2,1)S(1)}, u32[]{:S(2)}, u32[]{:S(2)}) collective-permute-start(bf16[8,1,32,128]{3,2,1,0:T(8,128)(2,1)S(1)} %get-tuple-element.2), channel_id=1, source_target_pairs={{0,1},{1,2},{2,3},{3,4},{4,5},{5,6},{6,7},{7,8},{8,9},{9,10},{10,1... | collective-permute-start | bytes 196616 | tf_op jit(solution)/shard_map/ppermute | solution.py:17
  20.5 5.6 %collective-permute-start.4 = (bf16[8,1,16,256]{3,2,1,0:T(8,128)(2,1)S(1)}, bf16[8,1,16,256]{3,2,1,0:T(8,128)(2,1)S(1)}, u32[]{:S(2)}, u32[]{:S(2)}) collective-permute-start(bf16[8,1,16,256]{3,2,1,0:T(8,128)(2,1)S(1)} %get-tuple-element.4), channel_id=1, source_target_pairs={{1,0},{2,1},{3,2},{4,3},{5,4},{6,5},{7,6},{8,7},{9,8},{10,9},{11,1... | collective-permute-start | bytes 196616 | tf_op jit(solution)/shard_map/ppermute | solution.py:19
  26.1 4.7 %collective-permute-start.5 = (bf16[2,6,16,256]{3,2,1,0:T(8,128)(2,1)S(1)}, bf16[2,6,16,256]{3,2,1,0:T(8,128)(2,1)S(1)}, u32[]{:S(2)}, u32[]{:S(2)}) collective-permute-start(bf16[2,6,16,256]{3,2,1,0:T(8,128)(2,1)S(1)} %constant_dynamic-slice_fusion), channel_id=1, source_target_pairs={{0,16},{16,32},{32,48},{48,64},{64,80},{80,96},{96,112},{112,128},... | collective-permute-start | bytes 294920 | tf_op jit(solution)/shard_map/ppermute | solution.py:29
  29.4 39.1 %collective-permute-start.2 = (bf16[2,10,32,128]{3,2,1,0:T(8,128)(2,1)S(1)}, bf16[2,10,32,128]{3,2,1,0:T(8,128)(2,1)}, u32[]{:S(2)}, u32[]{:S(2)}) collective-permute-start(bf16[2,10,32,128]{3,2,1,0:T(8,128)(2,1)S(1)} %slice.377), channel_id=1, source_target_pairs={{16,0},{32,16},{48,32},{64,48},{80,64},{96,80},{112,96},{128,112},... | collective-permute-start | bytes 491528 | tf_op jit(solution)/shard_map/ppermute | solution.py:29
  37.1 1.6 copy-start
  68.4 2.4 copy-start.1
Sparse Core Ops, SparseCore 0:
  68.6 270.0 all-reduce.4
where the time goes:
time: 351 us; the launch traced here: 350 us
  waiting for transfers between devices  202 us (58%)
  matrix products  95.3 us (27%)
  starting transfers between devices  16.9 us (5%)
  between operations  14.9 us (4%)
  local copies, waits for them, and re-layouts  12.4 us (4%)
  other arithmetic  8.27 us (2%)
    psum x1, waiting for transfers between devices, shards(): summed = lax.psum(local_weight, ('tm', 'tile'))  199 us
    dot_general x27, matrix products, shards(): jnp.einsum('thwo,co->thwc', g_piece, conv_weight[tap_index], preferred_el...  64.4 us
    dot_general x27, matrix products, shards(): jnp.einsum('thwc,thwo->co', u_piece, grad_masked, preferred_element_type=...  30.9 us
    ppermute x2, starting transfers between devices, padded(): lax.ppermute(tail, axis, [(i, (i + 1) % count) for i in range(ends)])  8.58 us
  transfers between devices with their start and end apart: 7, of which 3 were waited for; matrix products, arithmetic and copies ran while one was open for 32% of the time, Pallas kernels for 0%

commit v1 on v0

v1 whole, which is shorter than its diff:
```python
import math

import jax
import jax.numpy as jnp
import numpy as np
from jax import lax
from jax.experimental import pallas as pl
from jax.experimental.pallas import tpu as pltpu
from jax.sharding import PartitionSpec as P

BOTH = ("tm", "tile")
F32 = jnp.float32
BF16 = jnp.bfloat16
F16 = jnp.float16


def moved(rank, kind, step):
    tm, tile = divmod(rank, 16)
    y, x = divmod(tm, 4)
    z, core = divmod(tile, 2)
    if kind == "core":
        core ^= 1
    elif kind == "z":
        z ^= step
    elif (kind == "first") == (core == 0):
        x ^= step
    else:
        y ^= step
    return (y * 4 + x) * 16 + z * 2 + core


def swapped(value, kind, step=1):
    return lax.ppermute(value, BOTH, [(rank, moved(rank, kind, step)) for rank in range(256)])


def shifted(value, tm_step, tile_step):
    pairs = []
    for rank in range(256):
        tm, tile = divmod(rank, 16)
        tm, tile = tm + tm_step, tile + tile_step
        if 0 <= tm < 16 and 0 <= tile < 16:
            pairs.append((rank, tm * 16 + tile))
    return lax.ppermute(value, BOTH, pairs)


def power(exponent):
    whole = exponent.astype(jnp.int32)
    size = jnp.abs(whole)
    result = jnp.ones_like(exponent)
    for bit in range(7):
        factor = jnp.where(whole >= 0, F32(2.0 ** (2**bit)), F32(2.0 ** -(2**bit)))
        result = result * jnp.where((size >> bit) & 1 == 1, factor, F32(1))
    return lax.optimization_barrier(result)


def packed(value, exponent, scale):
    tail = jnp.broadcast_to(exponent.astype(F16), (8, 128))
    return jnp.concatenate([(value * scale).astype(F16), tail], axis=0)


def opened(message):
    exponent = message[-8:-7].astype(F32)
    return message[:-8].astype(F32) * power(-exponent), exponent


def scattered(total, exponent, place, kind):
    rows = total.shape[0] // 4
    scale = power(exponent)
    parts = []
    lowest = exponent
    for step in (1, 3, 2):
        piece = lax.dynamic_slice_in_dim(total, (place ^ step) * rows, rows, 0)
        part, theirs = opened(swapped(packed(piece, exponent, scale), kind, step))
        parts.append(part)
        lowest = jnp.minimum(lowest, theirs)
    mine = lax.dynamic_slice_in_dim(total, place * rows, rows, 0)
    return (mine + parts[0]) + (parts[1] + parts[2]), lowest - 2


def gathered(message, place, kind):
    buffer = jnp.zeros((4,) + message.shape, F16)
    for step in (0, 1, 3, 2):
        theirs = swapped(message, kind, step) if step else message
        buffer = lax.dynamic_update_index_in_dim(buffer, theirs, place ^ step, 0)
    return buffer.reshape((-1,) + message.shape[-2:])


def summed_everywhere(own, received, bound, factor):
    tm, tile = lax.axis_index("tm"), lax.axis_index("tile")
    y, x, core = tm // 4, tm % 4, tile % 2
    first = jnp.where(core == 0, x, y)
    second = jnp.where(core == 0, y, x)
    exponent = jnp.floor(13 - jnp.log2(jnp.maximum(bound, F32(1e-30))))
    total, exponent = scattered(own + received, exponent, first, "first")
    total, exponent = scattered(total, exponent, second, "second")
    for steps in ((1,), (2, 4, 6)):
        message = packed(total, exponent, power(exponent))
        parts = [opened(message)] + [opened(swapped(message, "z", step)) for step in steps]
        while len(parts) > 1:
            parts = [
                (a + b, jnp.minimum(e, f) - 1)
                for (a, e), (b, f) in zip(parts[::2], parts[1::2])
            ]
        total, exponent = parts[0]
    message = packed(total, exponent, power(exponent))[None]
    message = gathered(message, second, "second")
    message = gathered(message, first, "first")
    other = swapped(message, "core")

    def restored(pieces):
        scale = power(-pieces[:, -8:-7].astype(F32)) * F32(factor)
        return pieces[:, :-8].astype(F32) * scale

    mine, theirs = restored(message), restored(other)
    return jnp.stack([jnp.where(core == 0, mine, theirs), jnp.where(core == 0, theirs, mine)])


def box_matrix():
    box = np.zeros((9, 4, 16, 320), np.float32)
    for dh in range(3):
        for dw in range(3):
            for i in range(4):
                for j in range(16):
                    for h in (2 * i + 1 - dh, 2 * i + 2 - dh):
                        for w in (2 * j + 1 - dw, 2 * j + 2 - dw):
                            if 0 <= w < 32:
                                row = 256 if h < 0 else 288 if h > 7 else 32 * h
                                box[3 * dh + dw, i, j, row + w] = 1
    return box.reshape(576, 320)


def weight_kernel(
    info, x_ref, g_ref, top_ref, bottom_ref, later_ref, later_top_ref, later_bottom_ref, box_ref,
    own_ref, sent_ref, bound_ref, high_ref, low_ref, frames, terms,
):
    used, core = info[0], info[1]
    frames[0:8, 0:256] = g_ref[...]
    frames[0:8, 256:288] = top_ref[...]
    frames[0:8, 288:320] = bottom_ref[...]
    frames[8:10] = jnp.zeros((2, 320, 128), BF16)
    for k in range(2):
        frames[used + k, 0:256] = later_ref[k]
        frames[used + k, 256:288] = later_top_ref[k]
        frames[used + k, 288:320] = later_bottom_ref[k]
    for pair in range(5):
        two = jnp.concatenate([frames[2 * pair], frames[2 * pair + 1]], axis=1)
        sums = jnp.dot(box_ref[...], two, preferred_element_type=F32)
        high = sums.astype(BF16)
        low = (sums - high.astype(F32)).astype(BF16)
        for k in range(2):
            rows = slice(64 * (2 * pair + k), 64 * (2 * pair + k + 1))
            for tap in range(9):
                block = (slice(64 * tap, 64 * tap + 64), slice(128 * k, 128 * k + 128))
                high_ref[rows, 128 * tap : 128 * tap + 128] = high[block]
                low_ref[rows, 128 * tap : 128 * tap + 128] = low[block]
    slot = lax.broadcasted_iota(jnp.int32, (512, 256), 0) // 64
    x = jnp.where(slot < used, x_ref[...], jnp.zeros((), BF16)).T
    for dt in range(3):
        rows = slice(64 * (2 - dt), 64 * (2 - dt) + 512)
        for at in range(0, 1152, 256):
            columns = slice(at, min(at + 256, 1152))
            term = jnp.dot(x, high_ref[rows, columns], preferred_element_type=F32)
            term = term + jnp.dot(x, low_ref[rows, columns], preferred_element_type=F32)
            for k in range(0, term.shape[1], 128):
                tap = 9 * dt + (at + k) // 128
                terms[256 * tap : 256 * tap + 256] = term[:, k : k + 128]
    own = terms[pl.ds(pl.multiple_of(core * 3456, 8), 3456)]
    own_ref[...] = own
    sent = terms[pl.ds(pl.multiple_of((1 - core) * 3456, 8), 3456)]
    sent_ref[0:3456] = sent
    bound_ref[...] = jnp.broadcast_to(jnp.max(jnp.abs(own)), (8, 128))
    sent_ref[3456:3464] = jnp.broadcast_to(jnp.max(jnp.abs(sent)), (8, 128))


def input_kernel(info, high_ref, low_ref, weight_ref, out_ref):
    total = jnp.zeros((512, 256), F32)
    for dt in range(3):
        rows = slice(64 * (2 - dt), 64 * (2 - dt) + 512)
        weight = weight_ref[1152 * dt : 1152 * dt + 1152]
        total = total + jnp.dot(high_ref[rows], weight, preferred_element_type=F32)
        total = total + jnp.dot(low_ref[rows], weight, preferred_element_type=F32)
    slot = lax.broadcasted_iota(jnp.int32, (512, 256), 0) // 64
    out_ref[...] = jnp.where(slot < info[0], total, F32(0)).astype(BF16)


def shards(activations, grad_output, conv_weight, frame_counts):
    info = jnp.concatenate([frame_counts, (lax.axis_index("tile") % 2)[None].astype(jnp.int32)])
    cotangent = grad_output.reshape(8, 256, 128)
    first_row, last_row = cotangent[:, :32], cotangent[:, 224:]
    with jax.named_scope("edges"):
        top = shifted(last_row, 0, 1)
        bottom = shifted(first_row, 0, -1)
        later = shifted(cotangent[:2], -1, 0)
        later_top = shifted(last_row[:2], -1, 1)
        later_bottom = shifted(first_row[:2], -1, -1)
    whole = pl.BlockSpec(memory_space=pltpu.VMEM)
    scalars = pl.BlockSpec(memory_space=pltpu.SMEM)
    with jax.named_scope("weight_terms"):
        own, sent, bound, high, low = pl.pallas_call(
            weight_kernel,
            out_shape=(
                jax.ShapeDtypeStruct((3456, 128), F32),
                jax.ShapeDtypeStruct((3464, 128), F32),
                jax.ShapeDtypeStruct((8, 128), F32),
                jax.ShapeDtypeStruct((640, 1152), BF16),
                jax.ShapeDtypeStruct((640, 1152), BF16),
            ),
            in_specs=[scalars] + [whole] * 8,
            out_specs=(whole,) * 5,
            scratch_shapes=[pltpu.VMEM((10, 320, 128), BF16), pltpu.VMEM((6912, 128), F32)],
            compiler_params=pltpu.CompilerParams(vmem_limit_bytes=40 * 2**20),
            cost_estimate=pl.CostEstimate(
                flops=3 * 10**9, bytes_accessed=10**7, transcendentals=0
            ),
        )(
            info, activations.reshape(512, 256), cotangent, top, bottom, later, later_top,
            later_bottom, jnp.asarray(box_matrix(), BF16),
        )
    with jax.named_scope("halves"):
        received = swapped(sent, "core")
    weight = jnp.transpose(conv_weight, (0, 2, 1)).reshape(3456, 256)
    with jax.named_scope("input_terms"):
        grad_input = pl.pallas_call(
            input_kernel,
            out_shape=jax.ShapeDtypeStruct((512, 256), BF16),
            in_specs=[scalars] + [whole] * 3,
            out_specs=whole,
            compiler_params=pltpu.CompilerParams(vmem_limit_bytes=40 * 2**20),
            cost_estimate=pl.CostEstimate(
                flops=2 * 10**9, bytes_accessed=5 * 10**6, transcendentals=0
            ),
        )(info, high, low, weight)
    with jax.named_scope("weight_sum"):
        factor = 1.0 / math.sqrt(16 * 16 * 2048)
        grad_weight = summed_everywhere(
            own, received[:3456], bound[:1] + received[3456:3457], factor
        )
    return grad_input.reshape(8, 4, 16, 256), grad_weight.reshape(27, 256, 128)


def solution(mesh):
    placed = (P("tm", "tile", None, None), P("tm", "tile", None, None), P(), P("tm"))
    return jax.shard_map(
        shards,
        mesh=mesh,
        in_specs=placed,
        out_specs=(P("tm", "tile", None, None), P()),
        check_vma=False,
    )
```

time: 351 us -> 123 us (0.35)
  waiting for transfers between devices: 202 us -> 30.1 us
  matrix products: 95.3 us -> 0 us
  starting transfers between devices: 16.9 us -> 49.8 us
  between operations: 14.9 us -> 1.61 us
  local copies, waits for them, and re-layouts: 12.4 us -> 23.2 us
  Pallas kernels: 0 us -> 7.69 us
    psum x1 -> x0, waiting for transfers between devices: 199 us -> none  [shards(): summed = lax.psum(local_weight, ('tm', 'tile'))]
    dot_general x54 -> x0, matrix products: 95.3 us -> none  [the longest x27 64.4 us: shards(): jnp.einsum('thwo,co->thwc', g_piece, conv_weight[tap_index], preferred_el...]
    ppermute x6 -> x23, starting transfers between devices: 16.8 us -> 49.8 us  [the longest x18 39.1 us: swapped(): lax.ppermute(value, BOTH, [(rank, moved(rank, kind, step)) for rank in ra...]
    ppermute x6 -> x23, waiting for transfers between devices: 2.76 us -> 30.1 us  [the longest x18 25 us: swapped(): lax.ppermute(value, BOTH, [(rank, moved(rank, kind, step)) for rank in ra...]
    unnamed x6 -> x34, local copies, waits for them, and re-layouts: 1.43 us -> 13.8 us
    pallas_call x0 -> x2, Pallas kernels: none -> 7.69 us  [the longest x1 4.27 us: shards(): pl.pallas_call(weight_kernel, out_shape=(jax.ShapeDtypeStruct((3456, 128)...]
    reshape x2 -> x1, local copies, waits for them, and re-layouts: 4.98 us -> 0.04 us  [gathered(): return buffer.reshape((-1,) + message.shape[-2:])]
    another operation x0 -> x2, other arithmetic: none -> 3.82 us  [summed_everywhere(): jnp.stack([jnp.where(core == 0, mine, theirs), jnp.where(core == 0, their...]
  transfers between devices with their start and end apart: 7 -> 23, of which waited for: 3 -> 16; matrix products, arithmetic and copies ran while one was open for 32% -> 7% of each run, Pallas kernels for 0% -> 3%
where the time goes in v1:
time: 123 us; the launch traced here: 122 us
  starting transfers between devices  49.8 us (40%)
  waiting for transfers between devices  30.1 us (24%)
  local copies, waits for them, and re-layouts  23.2 us (19%)
  other arithmetic  9.14 us (7%)
  Pallas kernels  7.69 us (6%)
  between operations  1.61 us (1%)
    ppermute x18, starting transfers between devices, swapped(): lax.ppermute(value, BOTH, [(rank, moved(rank, kind, step)) for rank in ra...  39.1 us
    ppermute x18, waiting for transfers between devices, swapped(): lax.ppermute(value, BOTH, [(rank, moved(rank, kind, step)) for rank in ra...  25 us
    unnamed x34, local copies, waits for them, and re-layouts  13.8 us
    ppermute x5, starting transfers between devices, shifted(): return lax.ppermute(value, BOTH, pairs)  10.7 us
    ppermute x5, waiting for transfers between devices, shifted(): return lax.ppermute(value, BOTH, pairs)  5.14 us
    pallas_call x1, Pallas kernels, shards(): pl.pallas_call(weight_kernel, out_shape=(jax.ShapeDtypeStruct((3456, 128)...  4.27 us
    another operation x2, other arithmetic, summed_everywhere(): jnp.stack([jnp.where(core == 0, mine, theirs), jnp.where(core == 0, their...  3.82 us
    pallas_call x1, Pallas kernels, shards(): pl.pallas_call(input_kernel, out_shape=jax.ShapeDtypeStruct((512, 256), B...  3.42 us
  transfers between devices with their start and end apart: 23, of which 16 were waited for; matrix products, arithmetic and copies ran while one was open for 7% of the time, Pallas kernels for 3%

profile of v1, /device:TPU:1, one launch (start us, length us, event | category | flops | bytes accessed | tf_op | source)
XLA Modules:
  0.0 121.5 jit_solution(9760476281475674694)
XLA Ops:
  0.6 0.9 fusion.139
  1.5 4.9 %collective-permute-start = (bf16[8,32,128]{2,1,0:T(8,128)(2,1)S(1)}, bf16[8,32,128]{2,1,0:T(8,128)(2,1)S(1)}, u32[]{:S(2)}, u32[]{:S(2)}) collective-permute-start(bf16[8,32,128]{2,1,0:T(8,128)(2,1)S(1)} %get-tuple-element.30), channel_id=1, source_target_pairs={{0,1},{1,2},{2,3},{3,4},{4,5},{5,6},{6,7},{7,8},{8,9},{9,10},{10,1... | collective-permute-start | bytes 196616 | tf_op jit(solution)/shard_map/edges/ppermute | solution.py:43
  6.5 1.9 %collective-permute-start.1 = (bf16[8,32,128]{2,1,0:T(8,128)(2,1)S(1)}, bf16[8,32,128]{2,1,0:T(8,128)(2,1)S(1)}, u32[]{:S(2)}, u32[]{:S(2)}) collective-permute-start(bf16[8,32,128]{2,1,0:T(8,128)(2,1)S(1)} %get-tuple-element.29), channel_id=1, source_target_pairs={{1,0},{2,1},{3,2},{4,3},{5,4},{6,5},{7,6},{8,7},{9,8},{10,9},{11,1... | collective-permute-start | bytes 196616 | tf_op jit(solution)/shard_map/edges/ppermute | solution.py:43
  8.4 0.9 slice.105
  9.3 1.3 %collective-permute-start.2 = (bf16[2,256,128]{2,1,0:T(8,128)(2,1)S(1)}, bf16[2,256,128]{2,1,0:T(8,128)(2,1)S(1)}, u32[]{:S(2)}, u32[]{:S(2)}) collective-permute-start(bf16[2,256,128]{2,1,0:T(8,128)(2,1)S(1)} %bitcast.61), channel_id=1, source_target_pairs={{16,0},{17,1},{18,2},{19,3},{20,4},{21,5},{22,6},{23,7},{24,8},{25... | collective-permute-start | bytes 393224 | tf_op jit(solution)/shard_map/edges/ppermute | solution.py:43
  11.4 1.3 %collective-permute-start.3 = (bf16[2,32,128]{2,1,0:T(8,128)(2,1)S(1)}, bf16[2,32,128]{2,1,0:T(8,128)(2,1)S(1)}, u32[]{:S(2)}, u32[]{:S(2)}) collective-permute-start(bf16[2,32,128]{2,1,0:T(8,128)(2,1)S(1)} %get-tuple-element.28), channel_id=1, source_target_pairs={{16,1},{17,2},{18,3},{19,4},{20,5},{21,6},{22,7},{23,8},{24,9},{25... | collective-permute-start | bytes 49160 | tf_op jit(solution)/shard_map/edges/ppermute | solution.py:43
  12.6 1.3 %collective-permute-start.4 = (bf16[2,32,128]{2,1,0:T(8,128)(2,1)S(1)}, bf16[2,32,128]{2,1,0:T(8,128)(2,1)S(1)}, u32[]{:S(2)}, u32[]{:S(2)}) collective-permute-start(bf16[2,32,128]{2,1,0:T(8,128)(2,1)S(1)} %get-tuple-element.27), channel_id=1, source_target_pairs={{17,0},{18,1},{19,2},{20,3},{21,4},{22,5},{23,6},{24,7},{25,8},{26... | collective-permute-start | bytes 49160 | tf_op jit(solution)/shard_map/edges/ppermute | solution.py:43
  14.7 1.7 %collective-permute-done.3.later_top_ref = bf16[2,32,128]{2,1,0:T(8,128)(2,1)S(1)} collective-permute-done((bf16[2,32,128]{2,1,0:T(8,128)(2,1)S(1)}, bf16[2,32,128]{2,1,0:T(8,128)(2,1)S(1)}, u32[]{:S(2)}, u32[]{:S(2)}) %collective-permute-start.3) | collective-permute-done | bytes 16416 | tf_op jit(solution)/shard_map/edges/ppermute | solution.py:43
  17.0 3.4 %collective-permute-done.4.later_bottom_ref = bf16[2,32,128]{2,1,0:T(8,128)(2,1)S(1)} collective-permute-done((bf16[2,32,128]{2,1,0:T(8,128)(2,1)S(1)}, bf16[2,32,128]{2,1,0:T(8,128)(2,1)S(1)}, u32[]{:S(2)}, u32[]{:S(2)}) %collective-permute-start.4) | collective-permute-done | bytes 16416 | tf_op jit(solution)/shard_map/edges/ppermute | solution.py:43
  22.9 1.0 copy-done
  24.0 0.9 copy-done.1
  24.9 0.9 copy-done.3
  25.8 0.8 copy-done.5
  28.9 1.0 copy-done.12
  30.0 4.3 %weight_terms.1 = (f32[3456,128]{1,0:T(8,128)S(1)}, f32[3464,128]{1,0:T(8,128)S(1)}, f32[8,128]{1,0:T(8,128)S(1)}, bf16[640,1152]{1,0:T(8,128)(2,1)S(1)}, bf16[640,1152]{1,0:T(8,128)(2,1)S(1)}) custom-call(s32[2]{0:T(128)S(1)} %pad_add_fusion.info, bf16[512,256]{1,0:T(8,128)(2,1)S(1)} %bitcast.58, bf16[8,256,128]{2,1,0:T(8,128)(2,1)S(1)} %bitcast.57, ...), custom_call_target="tpu_custom_call" | custom-call | flops 3000000000 | bytes 10000000 | tf_op jit(solution)/shard_map/weight_terms/pallas_call | solution.py:199
  34.3 1.1 copy-done.13
  35.4 1.1 copy-done.15
  36.5 3.8 %collective-permute-done.5 = f32[3464,128]{1,0:T(8,128)} collective-permute-done((f32[3464,128]{1,0:T(8,128)S(1)}, f32[3464,128]{1,0:T(8,128)}, u32[]{:S(2)}, u32[]{:S(2)}) %collective-permute-start.5) | collective-permute-done | bytes 1773600 | tf_op jit(solution)/shard_map/halves/ppermute | solution.py:33
  41.0 1.8 %slice_add_fusion = f32[3456,128]{1,0:T(8,128)S(1)} fusion(f32[3456,128]{1,0:T(8,128)S(1)} %get-tuple-element.9, f32[3464,128]{1,0:T(8,128)} %collective-permute-done.5), kind=kLoop, calls=%fused_computation.1 | loop fusion | flops 442368 | bytes 5308416 | tf_op jit(solution)/shard_map/weight_sum/add | solution.py:94
  43.2 7.1 %collective-permute-start.8 = (f16[872,128]{1,0:T(8,128)(2,1)S(1)}, f16[872,128]{1,0:T(8,128)(2,1)S(1)}, u32[]{:S(2)}, u32[]{:S(2)}) collective-permute-start(f16[872,128]{1,0:T(8,128)(2,1)S(1)} %get-tuple-element.49), channel_id=1, source_target_pairs={{0,32},{1,129},{2,34},{3,131},{4,36},{5,133},{6,38},{7,135},{8,40}... | collective-permute-start | bytes 669704 | tf_op jit(solution)/shard_map/weight_sum/ppermute | solution.py:33
  51.0 2.6 %collective-permute-done.8 = f16[872,128]{1,0:T(8,128)(2,1)S(1)} collective-permute-done((f16[872,128]{1,0:T(8,128)(2,1)S(1)}, f16[872,128]{1,0:T(8,128)(2,1)S(1)}, u32[]{:S(2)}, u32[]{:S(2)}) %collective-permute-start.8) | collective-permute-done | bytes 223264 | tf_op jit(solution)/shard_map/weight_sum/ppermute | solution.py:33
  53.6 2.7 %collective-permute-done.7 = f16[872,128]{1,0:T(8,128)(2,1)S(1)} collective-permute-done((f16[872,128]{1,0:T(8,128)(2,1)S(1)}, f16[872,128]{1,0:T(8,128)(2,1)S(1)}, u32[]{:S(2)}, u32[]{:S(2)}) %collective-permute-start.7) | collective-permute-done | bytes 223264 | tf_op jit(solution)/shard_map/weight_sum/ppermute | solution.py:33
  57.5 3.0 %collective-permute-start.10 = (f16[224,128]{1,0:T(8,128)(2,1)S(1)}, f16[224,128]{1,0:T(8,128)(2,1)S(1)}, u32[]{:S(2)}, u32[]{:S(2)}) collective-permute-start(f16[224,128]{1,0:T(8,128)(2,1)S(1)} %get-tuple-element.45), channel_id=1, source_target_pairs={{0,192},{1,49},{2,194},{3,51},{4,196},{5,53},{6,198},{7,55},{8,200... | collective-permute-start | bytes 172040 | tf_op jit(solution)/shard_map/weight_sum/ppermute | solution.py:33
  60.5 1.6 %collective-permute-done.11 = f16[224,128]{1,0:T(8,128)(2,1)S(1)} collective-permute-done((f16[224,128]{1,0:T(8,128)(2,1)S(1)}, f16[224,128]{1,0:T(8,128)(2,1)S(1)}, u32[]{:S(2)}, u32[]{:S(2)}) %collective-permute-start.11) | collective-permute-done | bytes 57376 | tf_op jit(solution)/shard_map/weight_sum/ppermute | solution.py:33
  62.0 0.8 collective-permute-done.10
  63.6 1.7 %collective-permute-start.12 = (f16[224,128]{1,0:T(8,128)(2,1)S(1)}, f16[224,128]{1,0:T(8,128)(2,1)S(1)}, u32[]{:S(2)}, u32[]{:S(2)}) collective-permute-start(f16[224,128]{1,0:T(8,128)(2,1)S(1)} %pad_maximum_fusion.7), channel_id=1, source_target_pairs={{0,2},{1,3},{2,0},{3,1},{4,6},{5,7},{6,4},{7,5},{8,10},{9,11},{10,... | collective-permute-start | bytes 172040 | tf_op jit(solution)/shard_map/weight_sum/ppermute | solution.py:33
  65.4 1.6 %collective-permute-done.12 = f16[224,128]{1,0:T(8,128)(2,1)S(1)} collective-permute-done((f16[224,128]{1,0:T(8,128)(2,1)S(1)}, f16[224,128]{1,0:T(8,128)(2,1)S(1)}, u32[]{:S(2)}, u32[]{:S(2)}) %collective-permute-start.12) | collective-permute-done | bytes 57376 | tf_op jit(solution)/shard_map/weight_sum/ppermute | solution.py:33
  67.1 5.0 %collective-permute-start.15 = (f16[224,128]{1,0:T(8,128)(2,1)S(1)}, f16[224,128]{1,0:T(8,128)(2,1)S(1)}, u32[]{:S(2)}, u32[]{:S(2)}) collective-permute-start(f16[224,128]{1,0:T(8,128)(2,1)S(1)} %pad_maximum_fusion.8), channel_id=1, source_target_pairs={{0,12},{1,13},{2,14},{3,15},{4,8},{5,9},{6,10},{7,11},{8,4},{9,5},... | collective-permute-start | bytes 172040 | tf_op jit(solution)/shard_map/weight_sum/ppermute | solution.py:33
  72.1 5.0 %collective-permute-start.14 = (f16[224,128]{1,0:T(8,128)(2,1)S(1)}, f16[224,128]{1,0:T(8,128)(2,1)S(1)}, u32[]{:S(2)}, u32[]{:S(2)}) collective-permute-start(f16[224,128]{1,0:T(8,128)(2,1)S(1)} %pad_maximum_fusion.8), channel_id=1, source_target_pairs={{0,8},{1,9},{2,10},{3,11},{4,12},{5,13},{6,14},{7,15},{8,0},{9,1},... | collective-permute-start | bytes 172040 | tf_op jit(solution)/shard_map/weight_sum/ppermute | solution.py:33
  77.1 3.0 %collective-permute-done.14 = f16[224,128]{1,0:T(8,128)(2,1)S(1)} collective-permute-done((f16[224,128]{1,0:T(8,128)(2,1)S(1)}, f16[224,128]{1,0:T(8,128)(2,1)S(1)}, u32[]{:S(2)}, u32[]{:S(2)}) %collective-permute-start.14) | collective-permute-done | bytes 57376 | tf_op jit(solution)/shard_map/weight_sum/ppermute | solution.py:33
  80.1 1.6 %collective-permute-done.13 = f16[224,128]{1,0:T(8,128)(2,1)S(1)} collective-permute-done((f16[224,128]{1,0:T(8,128)(2,1)S(1)}, f16[224,128]{1,0:T(8,128)(2,1)S(1)}, u32[]{:S(2)}, u32[]{:S(2)}) %collective-permute-start.13) | collective-permute-done | bytes 57376 | tf_op jit(solution)/shard_map/weight_sum/ppermute | solution.py:33
  81.9 1.7 %collective-permute-start.17 = (f16[1,224,128]{2,1,0:T(8,128)(2,1)S(1)}, f16[1,224,128]{2,1,0:T(8,128)(2,1)S(1)}, u32[]{:S(2)}, u32[]{:S(2)}) collective-permute-start(f16[1,224,128]{2,1,0:T(8,128)(2,1)S(1)} %maximum_bitcast_fusion), channel_id=1, source_target_pairs={{0,192},{1,49},{2,194},{3,51},{4,196},{5,53},{6,198},{7,55},{8,200... | collective-permute-start | bytes 172040 | tf_op jit(solution)/shard_map/weight_sum/ppermute | solution.py:33
  83.6 1.6 %collective-permute-start.18 = (f16[1,224,128]{2,1,0:T(8,128)(2,1)S(1)}, f16[1,224,128]{2,1,0:T(8,128)(2,1)S(1)}, u32[]{:S(2)}, u32[]{:S(2)}) collective-permute-start(f16[1,224,128]{2,1,0:T(8,128)(2,1)S(1)} %maximum_bitcast_fusion), channel_id=1, source_target_pairs={{0,128},{1,33},{2,130},{3,35},{4,132},{5,37},{6,134},{7,39},{8,136... | collective-permute-start | bytes 172040 | tf_op jit(solution)/shard_map/weight_sum/ppermute | solution.py:33
  85.3 1.3 %collective-permute-done.17 = f16[1,224,128]{2,1,0:T(8,128)(2,1)S(1)} collective-permute-done((f16[1,224,128]{2,1,0:T(8,128)(2,1)S(1)}, f16[1,224,128]{2,1,0:T(8,128)(2,1)S(1)}, u32[]{:S(2)}, u32[]{:S(2)}) %collective-permute-start.17) | collective-permute-done | bytes 57376 | tf_op jit(solution)/shard_map/weight_sum/ppermute | solution.py:33
  86.6 1.5 %collective-permute-done.18 = f16[1,224,128]{2,1,0:T(8,128)(2,1)S(1)} collective-permute-done((f16[1,224,128]{2,1,0:T(8,128)(2,1)S(1)}, f16[1,224,128]{2,1,0:T(8,128)(2,1)S(1)}, u32[]{:S(2)}, u32[]{:S(2)}) %collective-permute-start.18) | collective-permute-done | bytes 57376 | tf_op jit(solution)/shard_map/weight_sum/ppermute | solution.py:33
  88.1 1.1 collective-permute-start.19
  89.2 1.9 %collective-permute-start.20 = (f16[4,224,128]{2,1,0:T(8,128)(2,1)S(1)}, f16[4,224,128]{2,1,0:T(8,128)(2,1)S(1)}, u32[]{:S(2)}, u32[]{:S(2)}) collective-permute-start(f16[4,224,128]{2,1,0:T(8,128)(2,1)S(1)} %constant_dynamic-update-slice_fusion), channel_id=1, source_target_pairs={{0,48},{1,193},{2,50},{3,195},{4,52},{5,197},{6,54},{7,199},{8,56}... | collective-permute-start | bytes 688136 | tf_op jit(solution)/shard_map/weight_sum/ppermute | solution.py:33
  91.1 1.1 collective-permute-start.21
  92.2 1.1 broadcast_in_dim.539
  94.7 2.4 %collective-permute-done.20 = f16[4,224,128]{2,1,0:T(8,128)(2,1)S(1)} collective-permute-done((f16[4,224,128]{2,1,0:T(8,128)(2,1)S(1)}, f16[4,224,128]{2,1,0:T(8,128)(2,1)S(1)}, u32[]{:S(2)}, u32[]{:S(2)}) %collective-permute-start.20) | collective-permute-done | bytes 229408 | tf_op jit(solution)/shard_map/weight_sum/ppermute | solution.py:33
  99.4 9.0 %collective-permute-start.22 = (f16[16,224,128]{2,1,0:T(8,128)(2,1)}, f16[16,224,128]{2,1,0:T(8,128)(2,1)}, u32[]{:S(2)}, u32[]{:S(2)}) collective-permute-start(f16[16,224,128]{2,1,0:T(8,128)(2,1)} %bitcast.34), channel_id=1, source_target_pairs={{0,1},{1,0},{2,3},{3,2},{4,5},{5,4},{6,7},{7,6},{8,9},{9,8},{10,11... | collective-permute-start | bytes 2752520 | tf_op jit(solution)/shard_map/weight_sum/ppermute | solution.py:33
  108.4 2.7 %copy.7 = bf16[27,128,256]{2,1,0:T(8,128)(2,1)S(1)} copy(bf16[27,128,256]{1,2,0:T(8,128)(2,1)} %bitcast.60) | data formatting | bytes 3538944 | tf_op jit(solution)/shard_map/transpose | solution.py:221
  111.1 1.4 %copy-done.16 = bf16[640,1152]{1,0:T(8,128)(2,1)S(1)} copy-done((bf16[640,1152]{1,0:T(8,128)(2,1)S(1)}, bf16[640,1152]{1,0:T(8,128)(2,1)}, u32[]{:S(2)}) %copy-start.16) | copy-done | bytes 1474584
  112.5 3.4 %input_terms.1 = bf16[512,256]{1,0:T(8,128)(2,1)} custom-call(s32[2]{0:T(128)S(1)} %pad_add_fusion.info, bf16[640,1152]{1,0:T(8,128)(2,1)S(1)} %copy-done.14, bf16[640,1152]{1,0:T(8,128)(2,1)S(1)} %copy-done.16, bf16[3456,256]{1,0:T(8,128)(2,1)S(1)} %bitcast.54), custom_call_target="tpu_custom_call" | custom-call | flops 2000000000 | bytes 5000000 | tf_op jit(solution)/shard_map/input_terms/pallas_call | solution.py:223
  115.9 0.9 fusion.5
  116.8 0.9 fusion.11
  117.7 1.8 %select_bitcast_fusion.1 = (f32[1,16,216,128]{3,2,1,0:T(8,128)S(1)}, f32[1,16,216,128]{3,2,1,0:T(8,128)S(1)}) fusion(f32[16,128]{1,0:T(8,128)S(1)} %bitcast.63, f32[16,128]{1,0:T(8,128)S(1)} %bitcast.62, pred[]{:T(512)S(6)} %eq.437, f16[16,224,128]{2,1,0:T(8,128)(2,1)} %collective-permute-done.22, f16[16,224,128]{2,1,0:T(8,128)(2,1)} %bitcast.34), kind=kLoop, calls=%fused_computation.3 | loop fusion | flops 2654208 | bytes 5324801 | tf_op jit(solution)/shard_map/weight_sum/stack | solution.py:115
  119.5 2.0 %pad_maximum_fusion = f32[2,16,216,128]{3,2,1,0:T(8,128)} fusion(f32[1,16,216,128]{3,2,1,0:T(8,128)S(1)} %get-tuple-element.23, f32[1,16,216,128]{3,2,1,0:T(8,128)S(1)} %get-tuple-element.22), kind=kLoop, calls=%fused_computation | loop fusion | flops 884736 | bytes 7077888 | tf_op jit(solution)/shard_map/weight_sum/stack | solution.py:115
  (82 shorter events, 14.2 us)
Async XLA Ops:
  1.5 19.5 %collective-permute-start = (bf16[8,32,128]{2,1,0:T(8,128)(2,1)S(1)}, bf16[8,32,128]{2,1,0:T(8,128)(2,1)S(1)}, u32[]{:S(2)}, u32[]{:S(2)}) collective-permute-start(bf16[8,32,128]{2,1,0:T(8,128)(2,1)S(1)} %get-tuple-element.30), channel_id=1, source_target_pairs={{0,1},{1,2},{2,3},{3,4},{4,5},{5,6},{6,7},{7,8},{8,9},{9,10},{10,1... | collective-permute-start | bytes 196616 | tf_op jit(solution)/shard_map/edges/ppermute | solution.py:43
  6.5 15.2 %collective-permute-start.1 = (bf16[8,32,128]{2,1,0:T(8,128)(2,1)S(1)}, bf16[8,32,128]{2,1,0:T(8,128)(2,1)S(1)}, u32[]{:S(2)}, u32[]{:S(2)}) collective-permute-start(bf16[8,32,128]{2,1,0:T(8,128)(2,1)S(1)} %get-tuple-element.29), channel_id=1, source_target_pairs={{1,0},{2,1},{3,2},{4,3},{5,4},{6,5},{7,6},{8,7},{9,8},{10,9},{11,1... | collective-permute-start | bytes 196616 | tf_op jit(solution)/shard_map/edges/ppermute | solution.py:43
  9.3 13.0 %collective-permute-start.2 = (bf16[2,256,128]{2,1,0:T(8,128)(2,1)S(1)}, bf16[2,256,128]{2,1,0:T(8,128)(2,1)S(1)}, u32[]{:S(2)}, u32[]{:S(2)}) collective-permute-start(bf16[2,256,128]{2,1,0:T(8,128)(2,1)S(1)} %bitcast.61), channel_id=1, source_target_pairs={{16,0},{17,1},{18,2},{19,3},{20,4},{21,5},{22,6},{23,7},{24,8},{25... | collective-permute-start | bytes 393224 | tf_op jit(solution)/shard_map/edges/ppermute | solution.py:43
  11.4 5.0 %collective-permute-start.3 = (bf16[2,32,128]{2,1,0:T(8,128)(2,1)S(1)}, bf16[2,32,128]{2,1,0:T(8,128)(2,1)S(1)}, u32[]{:S(2)}, u32[]{:S(2)}) collective-permute-start(bf16[2,32,128]{2,1,0:T(8,128)(2,1)S(1)} %get-tuple-element.28), channel_id=1, source_target_pairs={{16,1},{17,2},{18,3},{19,4},{20,5},{21,6},{22,7},{23,8},{24,9},{25... | collective-permute-start | bytes 49160 | tf_op jit(solution)/shard_map/edges/ppermute | solution.py:43
  12.6 7.8 %collective-permute-start.4 = (bf16[2,32,128]{2,1,0:T(8,128)(2,1)S(1)}, bf16[2,32,128]{2,1,0:T(8,128)(2,1)S(1)}, u32[]{:S(2)}, u32[]{:S(2)}) collective-permute-start(bf16[2,32,128]{2,1,0:T(8,128)(2,1)S(1)} %get-tuple-element.27), channel_id=1, source_target_pairs={{17,0},{18,1},{19,2},{20,3},{21,4},{22,5},{23,6},{24,7},{25,8},{26... | collective-permute-start | bytes 49160 | tf_op jit(solution)/shard_map/edges/ppermute | solution.py:43
  16.4 0.6 copy-start.8
  20.4 0.6 copy-start.10
  21.0 0.6 copy-start.4
  21.6 0.6 copy-start.6
  22.3 0.7 copy-start.2
  22.9 1.0 copy-start
  24.0 0.9 copy-start.1
  24.9 0.9 copy-start.3
  25.8 0.8 copy-start.5
  26.7 0.8 copy-start.7
  27.5 0.7 copy-start.9
  28.2 0.7 copy-start.11
  28.9 1.0 copy-start.12
  34.2 1.1 copy-start.13
  35.4 1.1 copy-start.15
  36.5 3.8 %collective-permute-start.5 = (f32[3464,128]{1,0:T(8,128)S(1)}, f32[3464,128]{1,0:T(8,128)}, u32[]{:S(2)}, u32[]{:S(2)}) collective-permute-start(f32[3464,128]{1,0:T(8,128)S(1)} %get-tuple-element.10), channel_id=1, source_target_pairs={{0,1},{1,0},{2,3},{3,2},{4,5},{5,4},{6,7},{7,6},{8,9},{9,8},{10,11... | collective-permute-start | bytes 5320712 | tf_op jit(solution)/shard_map/halves/ppermute | solution.py:33
  43.2 10.4 %collective-permute-start.8 = (f16[872,128]{1,0:T(8,128)(2,1)S(1)}, f16[872,128]{1,0:T(8,128)(2,1)S(1)}, u32[]{:S(2)}, u32[]{:S(2)}) collective-permute-start(f16[872,128]{1,0:T(8,128)(2,1)S(1)} %get-tuple-element.49), channel_id=1, source_target_pairs={{0,32},{1,129},{2,34},{3,131},{4,36},{5,133},{6,38},{7,135},{8,40}... | collective-permute-start | bytes 669704 | tf_op jit(solution)/shard_map/weight_sum/ppermute | solution.py:33
  50.3 6.0 %collective-permute-start.7 = (f16[872,128]{1,0:T(8,128)(2,1)S(1)}, f16[872,128]{1,0:T(8,128)(2,1)S(1)}, u32[]{:S(2)}, u32[]{:S(2)}) collective-permute-start(f16[872,128]{1,0:T(8,128)(2,1)S(1)} %get-tuple-element.48), channel_id=1, source_target_pairs={{0,48},{1,193},{2,50},{3,195},{4,52},{5,197},{6,54},{7,199},{8,56}... | collective-permute-start | bytes 669704 | tf_op jit(solution)/shard_map/weight_sum/ppermute | solution.py:33
  51.0 6.0 %collective-permute-start.6 = (f16[872,128]{1,0:T(8,128)(2,1)S(1)}, f16[872,128]{1,0:T(8,128)(2,1)S(1)}, u32[]{:S(2)}, u32[]{:S(2)}) collective-permute-start(f16[872,128]{1,0:T(8,128)(2,1)S(1)} %get-tuple-element.47), channel_id=1, source_target_pairs={{0,16},{1,65},{2,18},{3,67},{4,20},{5,69},{6,22},{7,71},{8,24},{9,... | collective-permute-start | bytes 669704 | tf_op jit(solution)/shard_map/weight_sum/ppermute | solution.py:33
  57.3 4.7 %collective-permute-start.11 = (f16[224,128]{1,0:T(8,128)(2,1)S(1)}, f16[224,128]{1,0:T(8,128)(2,1)S(1)}, u32[]{:S(2)}, u32[]{:S(2)}) collective-permute-start(f16[224,128]{1,0:T(8,128)(2,1)S(1)} %get-tuple-element.46), channel_id=1, source_target_pairs={{0,128},{1,33},{2,130},{3,35},{4,132},{5,37},{6,134},{7,39},{8,136... | collective-permute-start | bytes 172040 | tf_op jit(solution)/shard_map/weight_sum/ppermute | solution.py:33
  57.5 5.4 %collective-permute-start.10 = (f16[224,128]{1,0:T(8,128)(2,1)S(1)}, f16[224,128]{1,0:T(8,128)(2,1)S(1)}, u32[]{:S(2)}, u32[]{:S(2)}) collective-permute-start(f16[224,128]{1,0:T(8,128)(2,1)S(1)} %get-tuple-element.45), channel_id=1, source_target_pairs={{0,192},{1,49},{2,194},{3,51},{4,196},{5,53},{6,198},{7,55},{8,200... | collective-permute-start | bytes 172040 | tf_op jit(solution)/shard_map/weight_sum/ppermute | solution.py:33
  60.5 3.0 %collective-permute-start.9 = (f16[224,128]{1,0:T(8,128)(2,1)S(1)}, f16[224,128]{1,0:T(8,128)(2,1)S(1)}, u32[]{:S(2)}, u32[]{:S(2)}) collective-permute-start(f16[224,128]{1,0:T(8,128)(2,1)S(1)} %get-tuple-element.44), channel_id=1, source_target_pairs={{0,64},{1,17},{2,66},{3,19},{4,68},{5,21},{6,70},{7,23},{8,72},{9,... | collective-permute-start | bytes 172040 | tf_op jit(solution)/shard_map/weight_sum/ppermute | solution.py:33
  63.6 3.3 %collective-permute-start.12 = (f16[224,128]{1,0:T(8,128)(2,1)S(1)}, f16[224,128]{1,0:T(8,128)(2,1)S(1)}, u32[]{:S(2)}, u32[]{:S(2)}) collective-permute-start(f16[224,128]{1,0:T(8,128)(2,1)S(1)} %pad_maximum_fusion.7), channel_id=1, source_target_pairs={{0,2},{1,3},{2,0},{3,1},{4,6},{5,7},{6,4},{7,5},{8,10},{9,11},{10,... | collective-permute-start | bytes 172040 | tf_op jit(solution)/shard_map/weight_sum/ppermute | solution.py:33
  67.1 10.0 %collective-permute-start.15 = (f16[224,128]{1,0:T(8,128)(2,1)S(1)}, f16[224,128]{1,0:T(8,128)(2,1)S(1)}, u32[]{:S(2)}, u32[]{:S(2)}) collective-permute-start(f16[224,128]{1,0:T(8,128)(2,1)S(1)} %pad_maximum_fusion.8), channel_id=1, source_target_pairs={{0,12},{1,13},{2,14},{3,15},{4,8},{5,9},{6,10},{7,11},{8,4},{9,5},... | collective-permute-start | bytes 172040 | tf_op jit(solution)/shard_map/weight_sum/ppermute | solution.py:33
  72.1 8.0 %collective-permute-start.14 = (f16[224,128]{1,0:T(8,128)(2,1)S(1)}, f16[224,128]{1,0:T(8,128)(2,1)S(1)}, u32[]{:S(2)}, u32[]{:S(2)}) collective-permute-start(f16[224,128]{1,0:T(8,128)(2,1)S(1)} %pad_maximum_fusion.8), channel_id=1, source_target_pairs={{0,8},{1,9},{2,10},{3,11},{4,12},{5,13},{6,14},{7,15},{8,0},{9,1},... | collective-permute-start | bytes 172040 | tf_op jit(solution)/shard_map/weight_sum/ppermute | solution.py:33
  77.1 4.6 %collective-permute-start.13 = (f16[224,128]{1,0:T(8,128)(2,1)S(1)}, f16[224,128]{1,0:T(8,128)(2,1)S(1)}, u32[]{:S(2)}, u32[]{:S(2)}) collective-permute-start(f16[224,128]{1,0:T(8,128)(2,1)S(1)} %pad_maximum_fusion.8), channel_id=1, source_target_pairs={{0,4},{1,5},{2,6},{3,7},{4,0},{5,1},{6,2},{7,3},{8,12},{9,13},{10,... | collective-permute-start | bytes 172040 | tf_op jit(solution)/shard_map/weight_sum/ppermute | solution.py:33
  81.8 3.4 %collective-permute-start.16 = (f16[1,224,128]{2,1,0:T(8,128)(2,1)S(1)}, f16[1,224,128]{2,1,0:T(8,128)(2,1)S(1)}, u32[]{:S(2)}, u32[]{:S(2)}) collective-permute-start(f16[1,224,128]{2,1,0:T(8,128)(2,1)S(1)} %maximum_bitcast_fusion), channel_id=1, source_target_pairs={{0,64},{1,17},{2,66},{3,19},{4,68},{5,21},{6,70},{7,23},{8,72},{9,... | collective-permute-start | bytes 172040 | tf_op jit(solution)/shard_map/weight_sum/ppermute | solution.py:33
  81.9 4.6 %collective-permute-start.17 = (f16[1,224,128]{2,1,0:T(8,128)(2,1)S(1)}, f16[1,224,128]{2,1,0:T(8,128)(2,1)S(1)}, u32[]{:S(2)}, u32[]{:S(2)}) collective-permute-start(f16[1,224,128]{2,1,0:T(8,128)(2,1)S(1)} %maximum_bitcast_fusion), channel_id=1, source_target_pairs={{0,192},{1,49},{2,194},{3,51},{4,196},{5,53},{6,198},{7,55},{8,200... | collective-permute-start | bytes 172040 | tf_op jit(solution)/shard_map/weight_sum/ppermute | solution.py:33
  83.6 4.5 %collective-permute-start.18 = (f16[1,224,128]{2,1,0:T(8,128)(2,1)S(1)}, f16[1,224,128]{2,1,0:T(8,128)(2,1)S(1)}, u32[]{:S(2)}, u32[]{:S(2)}) collective-permute-start(f16[1,224,128]{2,1,0:T(8,128)(2,1)S(1)} %maximum_bitcast_fusion), channel_id=1, source_target_pairs={{0,128},{1,33},{2,130},{3,35},{4,132},{5,37},{6,134},{7,39},{8,136... | collective-permute-start | bytes 172040 | tf_op jit(solution)/shard_map/weight_sum/ppermute | solution.py:33
  88.1 5.9 %collective-permute-start.19 = (f16[4,224,128]{2,1,0:T(8,128)(2,1)S(1)}, f16[4,224,128]{2,1,0:T(8,128)(2,1)S(1)}, u32[]{:S(2)}, u32[]{:S(2)}) collective-permute-start(f16[4,224,128]{2,1,0:T(8,128)(2,1)S(1)} %constant_dynamic-update-slice_fusion), channel_id=1, source_target_pairs={{0,16},{1,65},{2,18},{3,67},{4,20},{5,69},{6,22},{7,71},{8,24},{9,... | collective-permute-start | bytes 688136 | tf_op jit(solution)/shard_map/weight_sum/ppermute | solution.py:33
  89.2 7.9 %collective-permute-start.20 = (f16[4,224,128]{2,1,0:T(8,128)(2,1)S(1)}, f16[4,224,128]{2,1,0:T(8,128)(2,1)S(1)}, u32[]{:S(2)}, u32[]{:S(2)}) collective-permute-start(f16[4,224,128]{2,1,0:T(8,128)(2,1)S(1)} %constant_dynamic-update-slice_fusion), channel_id=1, source_target_pairs={{0,48},{1,193},{2,50},{3,195},{4,52},{5,197},{6,54},{7,199},{8,56}... | collective-permute-start | bytes 688136 | tf_op jit(solution)/shard_map/weight_sum/ppermute | solution.py:33
  91.1 7.6 %collective-permute-start.21 = (f16[4,224,128]{2,1,0:T(8,128)(2,1)S(1)}, f16[4,224,128]{2,1,0:T(8,128)(2,1)S(1)}, u32[]{:S(2)}, u32[]{:S(2)}) collective-permute-start(f16[4,224,128]{2,1,0:T(8,128)(2,1)S(1)} %constant_dynamic-update-slice_fusion), channel_id=1, source_target_pairs={{0,32},{1,129},{2,34},{3,131},{4,36},{5,133},{6,38},{7,135},{8,40}... | collective-permute-start | bytes 688136 | tf_op jit(solution)/shard_map/weight_sum/ppermute | solution.py:33
  99.4 17.4 %collective-permute-start.22 = (f16[16,224,128]{2,1,0:T(8,128)(2,1)}, f16[16,224,128]{2,1,0:T(8,128)(2,1)}, u32[]{:S(2)}, u32[]{:S(2)}) collective-permute-start(f16[16,224,128]{2,1,0:T(8,128)(2,1)} %bitcast.34), channel_id=1, source_target_pairs={{0,1},{1,0},{2,3},{3,2},{4,5},{5,4},{6,7},{7,6},{8,9},{9,8},{10,11... | collective-permute-start | bytes 2752520 | tf_op jit(solution)/shard_map/weight_sum/ppermute | solution.py:33
  108.4 2.7 %copy-start.14 = (bf16[640,1152]{1,0:T(8,128)(2,1)S(1)}, bf16[640,1152]{1,0:T(8,128)(2,1)}, u32[]{:S(2)}) copy-start(bf16[640,1152]{1,0:T(8,128)(2,1)} %copy-done.13) | copy-start | bytes 4423684
  111.1 1.4 %copy-start.16 = (bf16[640,1152]{1,0:T(8,128)(2,1)S(1)}, bf16[640,1152]{1,0:T(8,128)(2,1)}, u32[]{:S(2)}) copy-start(bf16[640,1152]{1,0:T(8,128)(2,1)} %copy-done.15) | copy-start | bytes 4423684

commit v2 on v1

v2 whole, which is shorter than its diff:
```python
import math

import jax
import jax.numpy as jnp
import numpy as np
from jax import lax
from jax.experimental import pallas as pl
from jax.experimental.pallas import tpu as pltpu
from jax.sharding import PartitionSpec as P

BOTH = ("tm", "tile")
F32 = jnp.float32
BF16 = jnp.bfloat16
F16 = jnp.float16


def moved(rank, kind, step):
    tm, tile = divmod(rank, 16)
    y, x = divmod(tm, 4)
    z, core = divmod(tile, 2)
    if kind == "core":
        core ^= 1
    elif kind == "strip":
        tile += 1 if core else -1
        return tm * 16 + tile if 0 <= tile < 16 else None
    elif kind == "pair":
        z ^= 1
    elif kind == "z":
        z = (z + step if z % 2 else z - step) % 8
    elif (kind == "first") == (core == 0):
        x ^= step
    else:
        y ^= step
    return (y * 4 + x) * 16 + z * 2 + core


def swapped(value, kind, step=1):
    pairs = [(rank, moved(rank, kind, step)) for rank in range(256)]
    return lax.ppermute(value, BOTH, [pair for pair in pairs if pair[1] is not None])


def shifted(value, tm_step, tile_step):
    pairs = []
    for rank in range(256):
        tm, tile = divmod(rank, 16)
        tm, tile = tm + tm_step, tile + tile_step
        if 0 <= tm < 16 and 0 <= tile < 16:
            pairs.append((rank, tm * 16 + tile))
    return lax.ppermute(value, BOTH, pairs)


def position():
    tm, tile = lax.axis_index("tm"), lax.axis_index("tile")
    y, x, core = tm // 4, tm % 4, tile % 2
    return core, jnp.where(core == 0, x, y), jnp.where(core == 0, y, x)


def power(exponent):
    whole = exponent.astype(jnp.int32)
    size = jnp.abs(whole)
    result = jnp.ones_like(exponent)
    for bit in range(7):
        factor = jnp.where(whole >= 0, F32(2.0 ** (2**bit)), F32(2.0 ** -(2**bit)))
        result = result * jnp.where((size >> bit) & 1 == 1, factor, F32(1))
    return lax.optimization_barrier(result)


def packed(value, exponent, scale):
    tail = jnp.broadcast_to(exponent.astype(F16), (8, 128))
    return jnp.concatenate([(value * scale).astype(F16), tail], axis=0)


def opened(message):
    exponent = message[-8:-7].astype(F32)
    return message[:-8].astype(F32) * power(-exponent), exponent


def scattered(pieces, exponent, kind, after=None):
    scale = power(exponent)
    lowest = exponent
    parts = [pieces[0]]
    arrived = [swapped(packed(pieces[step], exponent, scale), kind, step) for step in (1, 3, 2)]
    if after is not None:
        *arrived, after = lax.optimization_barrier((*arrived, after))
    for message in arrived:
        part, theirs = opened(message)
        parts.append(part)
        lowest = jnp.minimum(lowest, theirs)
    return (parts[0] + parts[1]) + (parts[2] + parts[3]), lowest - 2, after


def placed_at(buffer, piece, place):
    return lax.dynamic_update_index_in_dim(buffer, piece, place, 0)


def summed_everywhere(own, received, grad_input, factor):
    core, first, second = position()
    bound = own[3456:3457] + received[3456:3457]
    exponent = jnp.floor(13 - jnp.log2(jnp.maximum(bound, F32(1e-30))))
    pieces = [own[r : r + 864] + received[r : r + 864] for r in range(0, 3456, 864)]
    total, exponent, grad_input = scattered(pieces, exponent, "first", grad_input)
    pieces = [total[r : r + 216] for r in range(0, 864, 216)]
    total, exponent, _ = scattered(pieces, exponent, "second")
    message = packed(total, exponent, power(exponent))
    (a, e), (b, f) = opened(message), opened(swapped(message, "pair"))
    total, exponent = a + b, jnp.minimum(e, f) - 1
    message = packed(total, exponent, power(exponent))
    parts = [opened(message)] + [opened(swapped(message, "z", step)) for step in (3, 2, 1)]
    total = (parts[0][0] + parts[1][0]) + (parts[2][0] + parts[3][0])
    exponent = jnp.stack([part[1] for part in parts]).min(axis=0) - 2
    message = packed(total, exponent, power(exponent))
    row = jnp.zeros((4, 224, 128), F16)
    for step in (0, 1, 3, 2):
        theirs = swapped(message, "second", step) if step else message
        row = placed_at(row, theirs, second ^ step)
    pieces = [row] + [swapped(row, "first", step) for step in (1, 3, 2)]
    mine = theirs = jnp.zeros((4, 4, 224, 128), F16)
    for pair, steps in ((pieces[:2], (0, 1)), (pieces[2:], (3, 2))):
        other = swapped(jnp.stack(pair), "core")
        for k, step in enumerate(steps):
            mine = placed_at(mine, pair[k], first ^ step)
            theirs = placed_at(theirs, other[k], second ^ step)
    result = jnp.zeros((2, 4, 4, 216, 128), F32)
    for half, pieces in ((core, mine), (1 - core, theirs)):
        scale = power(-pieces[:, :, -8:-7].astype(F32)) * F32(factor)
        result = placed_at(result, pieces[:, :, :-8].astype(F32) * scale, half)
    return result, grad_input


def box_matrix():
    box = np.zeros((9, 4, 16, 320), np.float32)
    for dh in range(3):
        for dw in range(3):
            for i in range(4):
                for j in range(16):
                    for h in (2 * i + 1 - dh, 2 * i + 2 - dh):
                        for w in (2 * j + 1 - dw, 2 * j + 2 - dw):
                            if 0 <= w < 32:
                                row = 256 if h < 0 else 288 if h > 7 else 32 * h
                                box[3 * dh + dw, i, j, row + w] = 1
    return box.reshape(576, 320)


def box_sums(box, frame, next_frame, high_ref, low_ref, row):
    two = jnp.concatenate([frame, next_frame], axis=1)
    sums = jnp.dot(box, two, preferred_element_type=F32)
    high = sums.astype(BF16)
    low = (sums - high.astype(F32)).astype(BF16)
    for k in range(2):
        rows = slice(row + 64 * k, row + 64 * k + 64)
        for tap in range(9):
            block = (slice(64 * tap, 64 * tap + 64), slice(128 * k, 128 * k + 128))
            columns = slice(128 * tap, 128 * tap + 128)
            high_ref[rows, columns] = high[block]
            low_ref[rows, columns] = low[block]


def most(value):
    return jnp.max(jnp.abs(value).reshape(-1, 8, 128), axis=0)


def edge_kernel(
    count, latent_in, g_in, previous_out, inner_out, outer_out, sems,
):
    core = lax.axis_index("tile") % 2
    inner, outer = 224 * (1 - core), 224 * core
    copies = [
        pltpu.make_async_copy(source, target, sems.at[k])
        for k, (source, target) in enumerate(
            (
                (latent_in.at[pl.ds(count[0] - 2, 2)], previous_out),
                (g_in.at[:, pl.ds(pl.multiple_of(inner, 32), 32)], inner_out),
                (g_in.at[:, pl.ds(pl.multiple_of(outer, 32), 32)], outer_out),
            )
        )
    ]
    for copy in copies:
        copy.start()
    for copy in copies:
        copy.wait()


def weight_kernel(
    count, x_ref, g_ref, box_ref, previous_ref, inner_ref, outer_ref,
    own_ref, sent_ref, high_ref, low_ref, later_ref,
    frames, terms,
):
    used = count[0]
    core, first, second = position()
    frames[:, 0:256] = g_ref[...]
    frames[:, pl.ds(pl.multiple_of(288 - 32 * core, 32), 32)] = inner_ref[...]
    frames[:, pl.ds(pl.multiple_of(256 + 32 * core, 32), 32)] = outer_ref[...]
    for t in range(2, 8):

        @pl.when(t >= used)
        def _():
            frames[t] = jnp.zeros((320, 128), BF16)

    later_ref[...] = frames[0:2]
    for pair in range(4):
        box_sums(
            box_ref[...], frames[2 * pair], frames[2 * pair + 1], high_ref, low_ref, 128 * pair
        )
    peak = [jnp.zeros((8, 128), F32)] * 2
    for dt in range(3):
        parts = [previous_ref[64 * dt :]] if dt < 2 else []
        parts.append(x_ref[: 384 + 64 * dt])
        x = jnp.concatenate(parts, axis=0).T
        for at in range(0, 1152, 256):
            columns = slice(at, min(at + 256, 1152))
            term = jnp.dot(x, high_ref[:, columns], preferred_element_type=F32)
            term = term + jnp.dot(x, low_ref[:, columns], preferred_element_type=F32)
            for k in range(0, term.shape[1], 128):
                tap = 9 * dt + (at + k) // 128
                block = term[:, k : k + 128]
                terms[256 * tap : 256 * tap + 256] = block
                if tap <= 13:
                    peak[0] = jnp.maximum(peak[0], most(block[: 128 if tap == 13 else 256]))
                if tap >= 13:
                    peak[1] = jnp.maximum(peak[1], most(block[128 if tap == 13 else 0 :]))
    for target, half, outer, inner in (
        (own_ref, core, first, second),
        (sent_ref, 1 - core, second, first),
    ):
        for j in range(16):
            start = 3456 * half + 864 * ((j // 4) ^ outer) + 216 * ((j % 4) ^ inner)
            rows = terms[pl.ds(pl.multiple_of(start, 8), 216)]
            target[216 * j : 216 * j + 216] = rows
    low_half = jnp.broadcast_to(jnp.max(peak[0]), (8, 128))
    high_half = jnp.broadcast_to(jnp.max(peak[1]), (8, 128))
    own_ref[3456:3464] = jnp.where(core == 0, low_half, high_half)
    sent_ref[3456:3464] = jnp.where(core == 0, high_half, low_half)


def times_taps(high, low, weight_ref, dt):
    total = None
    for at in range(0, 9, 2):
        taps = range(at, min(at + 2, 9))
        weight = jnp.concatenate([weight_ref[9 * dt + tap] for tap in taps], axis=1)
        columns = slice(128 * at, 128 * at + 128 * len(taps))
        for part in (high, low):
            term = lax.dot_general(
                part[:, columns], weight, (((1,), (1,)), ((), ())), preferred_element_type=F32
            )
            total = term if total is None else total + term
    return total


def input_kernel(
    count, weight_ref, box_ref, later_ref, high_ref, low_ref,
    grad_ref, later_high, later_low, total,
):
    used = count[0]
    for dt in (2, 1, 0):
        start = 64 * (2 - dt)
        term = times_taps(high_ref[start:512], low_ref[start:512], weight_ref, dt)
        if start:
            total[0 : 512 - start] += term
        else:
            total[...] = term
    box_sums(box_ref[...], later_ref[0], later_ref[1], later_high, later_low, 0)
    two = pl.ds(pl.multiple_of(64 * used - 128, 64), 128)
    total[two] += times_taps(later_high[...], later_low[...], weight_ref, 0)
    one = pl.ds(pl.multiple_of(64 * used - 64, 64), 64)
    total[one] += times_taps(later_high[0:64], later_low[0:64], weight_ref, 1)
    slot = lax.broadcasted_iota(jnp.int32, (512, 256), 0) // 64
    grad_ref[...] = jnp.where(slot < used, total[...], F32(0)).astype(BF16)


def shards(activations, grad_output, conv_weight, frame_counts):
    latent = activations.reshape(8, 64, 256)
    cotangent = grad_output.reshape(8, 256, 128)
    box = jnp.asarray(box_matrix(), BF16)
    far = pl.BlockSpec(memory_space=pltpu.HBM)
    near = pl.BlockSpec(memory_space=pltpu.VMEM)
    scalars = pl.BlockSpec(memory_space=pltpu.SMEM)
    params = pltpu.CompilerParams(vmem_limit_bytes=24 * 2**20)
    dma = pltpu.SemaphoreType.DMA
    with jax.named_scope("edges"):
        previous, inner, outer = pl.pallas_call(
            edge_kernel,
            out_shape=(
                jax.ShapeDtypeStruct((2, 64, 256), BF16),
                jax.ShapeDtypeStruct((8, 32, 128), BF16),
                jax.ShapeDtypeStruct((8, 32, 128), BF16),
            ),
            in_specs=[scalars] + [far] * 2,
            out_specs=(near,) * 3,
            scratch_shapes=[dma((3,))],
            compiler_params=pltpu.CompilerParams(vmem_limit_bytes=24 * 2**20),
        )(frame_counts, latent, cotangent)
        previous = shifted(previous, 1, 0).reshape(128, 256)
        inner = swapped(inner, "core")
        outer = swapped(outer, "strip")
    with jax.named_scope("weight_terms"):
        own, sent, high, low, later = pl.pallas_call(
            weight_kernel,
            out_shape=(
                jax.ShapeDtypeStruct((3464, 128), F32),
                jax.ShapeDtypeStruct((3464, 128), F32),
                jax.ShapeDtypeStruct((512, 1152), BF16),
                jax.ShapeDtypeStruct((512, 1152), BF16),
                jax.ShapeDtypeStruct((2, 320, 128), BF16),
            ),
            in_specs=[scalars] + [near] * 6,
            out_specs=(near,) * 5,
            scratch_shapes=[
                pltpu.VMEM((8, 320, 128), BF16),
                pltpu.VMEM((6912, 128), F32),
            ],
            compiler_params=params,
            cost_estimate=pl.CostEstimate(
                flops=3 * 10**9, bytes_accessed=10**7, transcendentals=0
            ),
        )(frame_counts, latent.reshape(512, 256), cotangent, box, previous, inner, outer)
    with jax.named_scope("halves"):
        later = shifted(later, -1, 0)
        received = swapped(sent, "core")
    with jax.named_scope("input_terms"):
        grad_input = pl.pallas_call(
            input_kernel,
            out_shape=jax.ShapeDtypeStruct((512, 256), BF16),
            in_specs=[scalars] + [near] * 5,
            out_specs=near,
            scratch_shapes=[
                pltpu.VMEM((128, 1152), BF16),
                pltpu.VMEM((128, 1152), BF16),
                pltpu.VMEM((512, 256), F32),
            ],
            compiler_params=params,
            cost_estimate=pl.CostEstimate(
                flops=2 * 10**9, bytes_accessed=5 * 10**6, transcendentals=0
            ),
        )(frame_counts, conv_weight, box, later, high, low)
    with jax.named_scope("weight_sum"):
        factor = 1.0 / math.sqrt(16 * 16 * 2048)
        grad_weight, grad_input = summed_everywhere(own, received, grad_input, factor)
    return grad_input.reshape(8, 4, 16, 256), grad_weight.reshape(27, 256, 128)


def solution(mesh):
    placed = (P("tm", "tile", None, None), P("tm", "tile", None, None), P(), P("tm"))
    return jax.shard_map(
        shards,
        mesh=mesh,
        in_specs=placed,
        out_specs=(P("tm", "tile", None, None), P()),
        check_vma=False,
    )
```

time: 123 us -> 88.3 us (0.72)
  local copies, waits for them, and re-layouts: 23.2 us -> 6.08 us
  other arithmetic: 9.14 us -> 2 us
  waiting for transfers between devices: 30.1 us -> 23.7 us
  starting transfers between devices: 49.8 us -> 47.8 us
    unnamed x34 -> x12, local copies, waits for them, and re-layouts: 13.8 us -> 4.8 us
    ppermute x5 -> x2, starting transfers between devices: 10.7 us -> 5.24 us  [shifted(): return lax.ppermute(value, BOTH, pairs)]
    ppermute x5 -> x2, waiting for transfers between devices: 5.14 us -> 0.01 us  [shifted(): return lax.ppermute(value, BOTH, pairs)]
    another operation x2, other arithmetic: 3.82 us -> 0.24 us  [summed_everywhere(): other = swapped(jnp.stack(pair), 'core')]
    ppermute x18 -> x21, starting transfers between devices: 39.1 us -> 42.5 us  [swapped(): lax.ppermute(value, BOTH, [pair for pair in pairs if pair[1] is not None])]
    transpose x1 -> x0, local copies, waits for them, and re-layouts: 2.73 us -> none  [shards(): weight = jnp.transpose(conv_weight, (0, 2, 1)).reshape(3456, 256)]
    slice x3 -> x0, local copies, waits for them, and re-layouts: 2.55 us -> none  [the longest x1 0.92 us: shards(): later = shifted(cotangent[:2], -1, 0)]
    dynamic_update_slice x7 -> x11, local copies, waits for them, and re-layouts: 3.02 us -> 0.68 us  [placed_at(): return lax.dynamic_update_index_in_dim(buffer, piece, place, 0)]
  transfers between devices with their start and end apart: 23 -> 23, of which waited for: 16 -> 14; matrix products, arithmetic and copies ran while one was open for 7% -> 2% of each run, Pallas kernels for 3% -> 4%
where the time goes in v2:
time: 88.3 us; the launch traced here: 88 us
  starting transfers between devices  47.8 us (54%)
  waiting for transfers between devices  23.7 us (27%)
  Pallas kernels  6.85 us (8%)
  local copies, waits for them, and re-layouts  6.08 us (7%)
  other arithmetic  2 us (2%)
  between operations  1.63 us (2%)
    ppermute x21, starting transfers between devices, swapped(): lax.ppermute(value, BOTH, [pair for pair in pairs if pair[1] is not None])  42.5 us
    ppermute x21, waiting for transfers between devices, swapped(): lax.ppermute(value, BOTH, [pair for pair in pairs if pair[1] is not None])  23.7 us
    ppermute x2, starting transfers between devices, shifted(): return lax.ppermute(value, BOTH, pairs)  5.24 us
    unnamed x12, local copies, waits for them, and re-layouts  4.8 us
    pallas_call x1, Pallas kernels, shards(): pl.pallas_call(input_kernel, out_shape=jax.ShapeDtypeStruct((512, 256), B...  3.52 us
    pallas_call x1, Pallas kernels, shards(): pl.pallas_call(weight_kernel, out_shape=(jax.ShapeDtypeStruct((3464, 128)...  3.22 us
  transfers between devices with their start and end apart: 23, of which 14 were waited for; matrix products, arithmetic and copies ran while one was open for 2% of the time, Pallas kernels for 4%

profile of v2, /device:TPU:1, one launch (start us, length us, event | category | flops | bytes accessed | tf_op | source)
XLA Modules:
  0.0 88.0 jit_solution(13272445245225427023)
XLA Ops:
  1.3 1.0 %copy-done = bf16[8,8,32,128]{3,2,1,0:T(8,128)(2,1)S(1)} copy-done((bf16[8,8,32,128]{3,2,1,0:T(8,128)(2,1)S(1)}, bf16[8,8,32,128]{3,2,1,0:T(8,128)(2,1)}, u32[]{:S(2)}) %copy-start) | copy-done | bytes 524312
  2.3 0.9 %copy-done.1 = bf16[8,4,16,256]{3,2,1,0:T(8,128)(2,1)S(1)} copy-done((bf16[8,4,16,256]{3,2,1,0:T(8,128)(2,1)S(1)}, bf16[8,4,16,256]{3,2,1,0:T(8,128)(2,1)}, u32[]{:S(2)}) %copy-start.1) | copy-done | bytes 262168
  3.4 3.9 %collective-permute-start = (bf16[2,64,256]{2,1,0:T(8,128)(2,1)S(1)}, bf16[2,64,256]{2,1,0:T(8,128)(2,1)S(1)}, u32[]{:S(2)}, u32[]{:S(2)}) collective-permute-start(bf16[2,64,256]{2,1,0:T(8,128)(2,1)S(1)} %get-tuple-element.14), channel_id=1, source_target_pairs={{0,16},{1,17},{2,18},{3,19},{4,20},{5,21},{6,22},{7,23},{8,24},{9,... | collective-permute-start | bytes 196616 | tf_op jit(solution)/shard_map/edges/ppermute | solution.py:49
  7.3 1.0 %collective-permute-start.1 = (bf16[8,32,128]{2,1,0:T(8,128)(2,1)S(1)}, bf16[8,32,128]{2,1,0:T(8,128)(2,1)S(1)}, u32[]{:S(2)}, u32[]{:S(2)}) collective-permute-start(bf16[8,32,128]{2,1,0:T(8,128)(2,1)S(1)} %get-tuple-element.15), channel_id=1, source_target_pairs={{0,1},{1,0},{2,3},{3,2},{4,5},{5,4},{6,7},{7,6},{8,9},{9,8},{10,11... | collective-permute-start | bytes 196616 | tf_op jit(solution)/shard_map/edges/ppermute | solution.py:39
  8.4 3.4 %collective-permute-start.2 = (bf16[8,32,128]{2,1,0:T(8,128)(2,1)S(1)}, bf16[8,32,128]{2,1,0:T(8,128)(2,1)S(1)}, u32[]{:S(2)}, u32[]{:S(2)}) collective-permute-start(bf16[8,32,128]{2,1,0:T(8,128)(2,1)S(1)} %get-tuple-element.16), channel_id=1, source_target_pairs={{1,2},{2,1},{3,4},{4,3},{5,6},{6,5},{7,8},{8,7},{9,10},{10,9},{11,... | collective-permute-start | bytes 196616 | tf_op jit(solution)/shard_map/edges/ppermute | solution.py:39
  11.9 2.1 %collective-permute-done.2.outer_ref = bf16[8,32,128]{2,1,0:T(8,128)(2,1)S(1)} collective-permute-done((bf16[8,32,128]{2,1,0:T(8,128)(2,1)S(1)}, bf16[8,32,128]{2,1,0:T(8,128)(2,1)S(1)}, u32[]{:S(2)}, u32[]{:S(2)}) %collective-permute-start.2) | collective-permute-done | bytes 65568 | tf_op jit(solution)/shard_map/edges/ppermute | solution.py:39
  14.0 1.0 %copy-done.3 = bf16[576,320]{1,0:T(8,128)(2,1)S(1)} copy-done((bf16[576,320]{1,0:T(8,128)(2,1)S(1)}, bf16[576,320]{1,0:T(8,128)(2,1)}, u32[]{:S(2)}) %copy-start.3) | copy-done | bytes 368664
  15.0 3.2 %weight_terms.1 = (f32[3464,128]{1,0:T(8,128)S(1)}, f32[3464,128]{1,0:T(8,128)S(1)}, bf16[512,1152]{1,0:T(8,128)(2,1)S(1)}, bf16[512,1152]{1,0:T(8,128)(2,1)S(1)}, bf16[2,320,128]{2,1,0:T(8,128)(2,1)S(1)}) custom-call(s32[1]{0:T(128)S(6)} %copy.21.count, bf16[512,256]{1,0:T(8,128)(2,1)S(1)} %bitcast.58, bf16[8,256,128]{2,1,0:T(8,128)(2,1)S(1)} %bitcast.56, ...), custom_call_target="tpu_custom_call" | custom-call | flops 3000000000 | bytes 10000000 | tf_op jit(solution)/shard_map/weight_terms/pallas_call | solution.py:296
  18.3 1.3 %collective-permute-start.7 = (bf16[2,320,128]{2,1,0:T(8,128)(2,1)S(1)}, bf16[2,320,128]{2,1,0:T(8,128)(2,1)S(1)}, u32[]{:S(2)}, u32[]{:S(2)}) collective-permute-start(bf16[2,320,128]{2,1,0:T(8,128)(2,1)S(1)} %get-tuple-element.19), channel_id=1, source_target_pairs={{16,0},{17,1},{18,2},{19,3},{20,4},{21,5},{22,6},{23,7},{24,8},{25... | collective-permute-start | bytes 491528 | tf_op jit(solution)/shard_map/halves/ppermute | solution.py:49
  19.6 2.4 %collective-permute-done.3 = f32[3464,128]{1,0:T(8,128)S(1)} collective-permute-done((f32[3464,128]{1,0:T(8,128)S(1)}, f32[3464,128]{1,0:T(8,128)S(1)}, u32[]{:S(2)}, u32[]{:S(2)}) %collective-permute-start.3) | collective-permute-done | bytes 1773600 | tf_op jit(solution)/shard_map/halves/ppermute | solution.py:39
  22.1 0.2 fusion.3
  22.3 0.2 pad_maximum_fusion.2
  22.5 2.0 %collective-permute-start.4 = (f16[872,128]{1,0:T(8,128)(2,1)S(1)}, f16[872,128]{1,0:T(8,128)(2,1)S(1)}, u32[]{:S(2)}, u32[]{:S(2)}) collective-permute-start(f16[872,128]{1,0:T(8,128)(2,1)S(1)} %get-tuple-element.57), channel_id=1, source_target_pairs={{0,16},{1,65},{2,18},{3,67},{4,20},{5,69},{6,22},{7,71},{8,24},{9,... | collective-permute-start | bytes 669704 | tf_op jit(solution)/shard_map/weight_sum/ppermute | solution.py:39
  24.5 1.9 %collective-permute-start.5 = (f16[872,128]{1,0:T(8,128)(2,1)S(1)}, f16[872,128]{1,0:T(8,128)(2,1)S(1)}, u32[]{:S(2)}, u32[]{:S(2)}) collective-permute-start(f16[872,128]{1,0:T(8,128)(2,1)S(1)} %get-tuple-element.56), channel_id=1, source_target_pairs={{0,48},{1,193},{2,50},{3,195},{4,52},{5,197},{6,54},{7,199},{8,56}... | collective-permute-start | bytes 669704 | tf_op jit(solution)/shard_map/weight_sum/ppermute | solution.py:39
  26.4 0.7 collective-permute-start.6
  27.1 3.5 %input_terms.1 = bf16[512,256]{1,0:T(8,128)(2,1)} custom-call(s32[1]{0:T(128)S(6)} %copy.21.count, bf16[27,256,128]{2,1,0:T(8,128)(2,1)S(1)} %copy-done.2, bf16[576,320]{1,0:T(8,128)(2,1)S(1)} %copy-done.4, bf16[2,320,128]{2,1,0:T(8,128)(2,1)S(1)} %collective-permute-done.7.later_ref, bf16[512,1152]{1,0:T(8,128)(2,1)S(1)} %get-tuple-element.20.high_ref, ...), custom_call_target="tpu_custom_call" | custom-call | flops 2000000000 | bytes 5000000 | tf_op jit(solution)/shard_map/input_terms/pallas_call | solution.py:320
  30.7 1.1 %collective-permute-done.5 = f16[872,128]{1,0:T(8,128)(2,1)S(1)} collective-permute-done((f16[872,128]{1,0:T(8,128)(2,1)S(1)}, f16[872,128]{1,0:T(8,128)(2,1)S(1)}, u32[]{:S(2)}, u32[]{:S(2)}) %collective-permute-start.5) | collective-permute-done | bytes 223264 | tf_op jit(solution)/shard_map/weight_sum/ppermute | solution.py:39
  31.7 1.4 %collective-permute-done.6 = f16[872,128]{1,0:T(8,128)(2,1)S(1)} collective-permute-done((f16[872,128]{1,0:T(8,128)(2,1)S(1)}, f16[872,128]{1,0:T(8,128)(2,1)S(1)}, u32[]{:S(2)}, u32[]{:S(2)}) %collective-permute-start.6) | collective-permute-done | bytes 223264 | tf_op jit(solution)/shard_map/weight_sum/ppermute | solution.py:39
  33.2 0.2 fusion.1
  33.5 1.7 %collective-permute-start.10 = (f16[224,128]{1,0:T(8,128)(2,1)S(1)}, f16[224,128]{1,0:T(8,128)(2,1)S(1)}, u32[]{:S(2)}, u32[]{:S(2)}) collective-permute-start(f16[224,128]{1,0:T(8,128)(2,1)S(1)} %get-tuple-element.54), channel_id=1, source_target_pairs={{0,128},{1,33},{2,130},{3,35},{4,132},{5,37},{6,134},{7,39},{8,136... | collective-permute-start | bytes 172040 | tf_op jit(solution)/shard_map/weight_sum/ppermute | solution.py:39
  35.2 0.7 collective-permute-start.8
  35.9 0.9 %collective-permute-start.9 = (f16[224,128]{1,0:T(8,128)(2,1)S(1)}, f16[224,128]{1,0:T(8,128)(2,1)S(1)}, u32[]{:S(2)}, u32[]{:S(2)}) collective-permute-start(f16[224,128]{1,0:T(8,128)(2,1)S(1)} %get-tuple-element.53), channel_id=1, source_target_pairs={{0,192},{1,49},{2,194},{3,51},{4,196},{5,53},{6,198},{7,55},{8,200... | collective-permute-start | bytes 172040 | tf_op jit(solution)/shard_map/weight_sum/ppermute | solution.py:39
  36.8 1.3 %collective-permute-done.10 = f16[224,128]{1,0:T(8,128)(2,1)S(1)} collective-permute-done((f16[224,128]{1,0:T(8,128)(2,1)S(1)}, f16[224,128]{1,0:T(8,128)(2,1)S(1)}, u32[]{:S(2)}, u32[]{:S(2)}) %collective-permute-start.10) | collective-permute-done | bytes 57376 | tf_op jit(solution)/shard_map/weight_sum/ppermute | solution.py:39
  38.1 0.4 collective-permute-done.8
  38.5 1.7 %collective-permute-done.9 = f16[224,128]{1,0:T(8,128)(2,1)S(1)} collective-permute-done((f16[224,128]{1,0:T(8,128)(2,1)S(1)}, f16[224,128]{1,0:T(8,128)(2,1)S(1)}, u32[]{:S(2)}, u32[]{:S(2)}) %collective-permute-start.9) | collective-permute-done | bytes 57376 | tf_op jit(solution)/shard_map/weight_sum/ppermute | solution.py:39
  40.3 1.7 %collective-permute-start.11 = (f16[224,128]{1,0:T(8,128)(2,1)S(1)}, f16[224,128]{1,0:T(8,128)(2,1)S(1)}, u32[]{:S(2)}, u32[]{:S(2)}) collective-permute-start(f16[224,128]{1,0:T(8,128)(2,1)S(1)} %pad_maximum_fusion.8), channel_id=1, source_target_pairs={{0,2},{1,3},{2,0},{3,1},{4,6},{5,7},{6,4},{7,5},{8,10},{9,11},{10,... | collective-permute-start | bytes 172040 | tf_op jit(solution)/shard_map/weight_sum/ppermute | solution.py:39
  42.0 1.6 %collective-permute-done.11 = f16[224,128]{1,0:T(8,128)(2,1)S(1)} collective-permute-done((f16[224,128]{1,0:T(8,128)(2,1)S(1)}, f16[224,128]{1,0:T(8,128)(2,1)S(1)}, u32[]{:S(2)}, u32[]{:S(2)}) %collective-permute-start.11) | collective-permute-done | bytes 57376 | tf_op jit(solution)/shard_map/weight_sum/ppermute | solution.py:39
  43.7 6.7 %collective-permute-start.12 = (f16[224,128]{1,0:T(8,128)(2,1)S(1)}, f16[224,128]{1,0:T(8,128)(2,1)S(1)}, u32[]{:S(2)}, u32[]{:S(2)}) collective-permute-start(f16[224,128]{1,0:T(8,128)(2,1)S(1)} %pad_maximum_fusion.9), channel_id=1, source_target_pairs={{0,10},{1,11},{2,8},{3,9},{4,14},{5,15},{6,12},{7,13},{8,2},{9,3},... | collective-permute-start | bytes 172040 | tf_op jit(solution)/shard_map/weight_sum/ppermute | solution.py:39
  50.4 1.1 %collective-permute-start.13 = (f16[224,128]{1,0:T(8,128)(2,1)S(1)}, f16[224,128]{1,0:T(8,128)(2,1)S(1)}, u32[]{:S(2)}, u32[]{:S(2)}) collective-permute-start(f16[224,128]{1,0:T(8,128)(2,1)S(1)} %pad_maximum_fusion.9), channel_id=1, source_target_pairs={{0,12},{1,13},{2,6},{3,7},{4,0},{5,1},{6,10},{7,11},{8,4},{9,5},{1... | collective-permute-start | bytes 172040 | tf_op jit(solution)/shard_map/weight_sum/ppermute | solution.py:39
  51.6 2.7 %collective-permute-start.14 = (f16[224,128]{1,0:T(8,128)(2,1)S(1)}, f16[224,128]{1,0:T(8,128)(2,1)S(1)}, u32[]{:S(2)}, u32[]{:S(2)}) collective-permute-start(f16[224,128]{1,0:T(8,128)(2,1)S(1)} %pad_maximum_fusion.9), channel_id=1, source_target_pairs={{0,14},{1,15},{2,4},{3,5},{4,2},{5,3},{6,8},{7,9},{8,6},{9,7},{10,... | collective-permute-start | bytes 172040 | tf_op jit(solution)/shard_map/weight_sum/ppermute | solution.py:39
  54.4 3.2 %collective-permute-done.14 = f16[224,128]{1,0:T(8,128)(2,1)S(1)} collective-permute-done((f16[224,128]{1,0:T(8,128)(2,1)S(1)}, f16[224,128]{1,0:T(8,128)(2,1)S(1)}, u32[]{:S(2)}, u32[]{:S(2)}) %collective-permute-start.14) | collective-permute-done | bytes 57376 | tf_op jit(solution)/shard_map/weight_sum/ppermute | solution.py:39
  57.8 0.7 collective-permute-start.16
  58.5 2.6 %collective-permute-start.17 = (f16[224,128]{1,0:T(8,128)(2,1)S(1)}, f16[224,128]{1,0:T(8,128)(2,1)S(1)}, u32[]{:S(2)}, u32[]{:S(2)}) collective-permute-start(f16[224,128]{1,0:T(8,128)(2,1)S(1)} %pad_maximum_fusion.10), channel_id=1, source_target_pairs={{0,128},{1,33},{2,130},{3,35},{4,132},{5,37},{6,134},{7,39},{8,136... | collective-permute-start | bytes 172040 | tf_op jit(solution)/shard_map/weight_sum/ppermute | solution.py:39
  61.2 1.0 %collective-permute-done.16 = f16[224,128]{1,0:T(8,128)(2,1)S(1)} collective-permute-done((f16[224,128]{1,0:T(8,128)(2,1)S(1)}, f16[224,128]{1,0:T(8,128)(2,1)S(1)}, u32[]{:S(2)}, u32[]{:S(2)}) %collective-permute-start.16) | collective-permute-done | bytes 57376 | tf_op jit(solution)/shard_map/weight_sum/ppermute | solution.py:39
  62.2 0.9 collective-permute-done.17
  63.1 2.1 %collective-permute-start.19 = (f16[4,224,128]{2,1,0:T(8,128)(2,1)S(1)}, f16[4,224,128]{2,1,0:T(8,128)(2,1)S(1)}, u32[]{:S(2)}, u32[]{:S(2)}) collective-permute-start(f16[4,224,128]{2,1,0:T(8,128)(2,1)S(1)} %bitcast_dynamic-update-slice_fusion.2), channel_id=1, source_target_pairs={{0,48},{1,193},{2,50},{3,195},{4,52},{5,197},{6,54},{7,199},{8,56}... | collective-permute-start | bytes 688136 | tf_op jit(solution)/shard_map/weight_sum/ppermute | solution.py:39
  65.2 1.5 %collective-permute-start.20 = (f16[4,224,128]{2,1,0:T(8,128)(2,1)S(1)}, f16[4,224,128]{2,1,0:T(8,128)(2,1)S(1)}, u32[]{:S(2)}, u32[]{:S(2)}) collective-permute-start(f16[4,224,128]{2,1,0:T(8,128)(2,1)S(1)} %bitcast_dynamic-update-slice_fusion.2), channel_id=1, source_target_pairs={{0,32},{1,129},{2,34},{3,131},{4,36},{5,133},{6,38},{7,135},{8,40}... | collective-permute-start | bytes 688136 | tf_op jit(solution)/shard_map/weight_sum/ppermute | solution.py:39
  66.6 0.1 broadcast_in_dim.576.clone
  66.8 6.1 %collective-permute-done.19 = f16[4,224,128]{2,1,0:T(8,128)(2,1)S(1)} collective-permute-done((f16[4,224,128]{2,1,0:T(8,128)(2,1)S(1)}, f16[4,224,128]{2,1,0:T(8,128)(2,1)S(1)}, u32[]{:S(2)}, u32[]{:S(2)}) %collective-permute-start.19) | collective-permute-done | bytes 229408 | tf_op jit(solution)/shard_map/weight_sum/ppermute | solution.py:39
  73.1 10.1 %collective-permute-start.22 = (f16[2,4,224,128]{3,2,1,0:T(8,128)(2,1)S(1)}, f16[2,4,224,128]{3,2,1,0:T(8,128)(2,1)S(1)}, u32[]{:S(2)}, u32[]{:S(2)}) collective-permute-start(f16[2,4,224,128]{3,2,1,0:T(8,128)(2,1)S(1)} %pad_maximum_fusion.1), channel_id=1, source_target_pairs={{0,1},{1,0},{2,3},{3,2},{4,5},{5,4},{6,7},{7,6},{8,9},{9,8},{10,11... | collective-permute-start | bytes 1376264 | tf_op jit(solution)/shard_map/weight_sum/ppermute | solution.py:39
  83.2 0.1 pad_maximum_fusion
  83.3 0.7 collective-permute-start.21
  84.4 0.3 broadcast_in_dim.575
  84.6 0.2 bitcast_dynamic-update-slice_fusion.1
  84.8 0.6 collective-permute-done.21
  85.4 0.1 broadcast_in_dim.576.clone.1
  86.0 0.2 bitcast_dynamic-update-slice_fusion
  86.2 1.8 %copy-done.5 = f32[2,4,4,216,128]{4,3,2,1,0:T(8,128)} copy-done((f32[2,4,4,216,128]{4,3,2,1,0:T(8,128)}, f32[2,4,4,216,128]{4,3,2,1,0:T(8,128)S(1)}, u32[]{:S(2)}) %copy-start.5) | copy-done | bytes 3538968
  (63 shorter events, 2.1 us)
Async XLA Ops:
  1.3 1.0 %copy-start = (bf16[8,8,32,128]{3,2,1,0:T(8,128)(2,1)S(1)}, bf16[8,8,32,128]{3,2,1,0:T(8,128)(2,1)}, u32[]{:S(2)}) copy-start(bf16[8,8,32,128]{3,2,1,0:T(8,128)(2,1)} %param.6) | copy-start | bytes 1572868
  2.3 0.9 %copy-start.1 = (bf16[8,4,16,256]{3,2,1,0:T(8,128)(2,1)S(1)}, bf16[8,4,16,256]{3,2,1,0:T(8,128)(2,1)}, u32[]{:S(2)}) copy-start(bf16[8,4,16,256]{3,2,1,0:T(8,128)(2,1)} %param.5) | copy-start | bytes 786436
  3.4 8.5 %collective-permute-start = (bf16[2,64,256]{2,1,0:T(8,128)(2,1)S(1)}, bf16[2,64,256]{2,1,0:T(8,128)(2,1)S(1)}, u32[]{:S(2)}, u32[]{:S(2)}) collective-permute-start(bf16[2,64,256]{2,1,0:T(8,128)(2,1)S(1)} %get-tuple-element.14), channel_id=1, source_target_pairs={{0,16},{1,17},{2,18},{3,19},{4,20},{5,21},{6,22},{7,23},{8,24},{9,... | collective-permute-start | bytes 196616 | tf_op jit(solution)/shard_map/edges/ppermute | solution.py:49
  7.3 4.5 %collective-permute-start.1 = (bf16[8,32,128]{2,1,0:T(8,128)(2,1)S(1)}, bf16[8,32,128]{2,1,0:T(8,128)(2,1)S(1)}, u32[]{:S(2)}, u32[]{:S(2)}) collective-permute-start(bf16[8,32,128]{2,1,0:T(8,128)(2,1)S(1)} %get-tuple-element.15), channel_id=1, source_target_pairs={{0,1},{1,0},{2,3},{3,2},{4,5},{5,4},{6,7},{7,6},{8,9},{9,8},{10,11... | collective-permute-start | bytes 196616 | tf_op jit(solution)/shard_map/edges/ppermute | solution.py:39
  8.4 5.6 %collective-permute-start.2 = (bf16[8,32,128]{2,1,0:T(8,128)(2,1)S(1)}, bf16[8,32,128]{2,1,0:T(8,128)(2,1)S(1)}, u32[]{:S(2)}, u32[]{:S(2)}) collective-permute-start(bf16[8,32,128]{2,1,0:T(8,128)(2,1)S(1)} %get-tuple-element.16), channel_id=1, source_target_pairs={{1,2},{2,1},{3,4},{4,3},{5,6},{6,5},{7,8},{8,7},{9,10},{10,9},{11,... | collective-permute-start | bytes 196616 | tf_op jit(solution)/shard_map/edges/ppermute | solution.py:39
  14.0 1.0 %copy-start.3 = (bf16[576,320]{1,0:T(8,128)(2,1)S(1)}, bf16[576,320]{1,0:T(8,128)(2,1)}, u32[]{:S(2)}) copy-start(bf16[576,320]{1,0:T(8,128)(2,1)} %constant.149.clone.box_ref) | copy-start | bytes 1105924
  18.2 3.8 %collective-permute-start.3 = (f32[3464,128]{1,0:T(8,128)S(1)}, f32[3464,128]{1,0:T(8,128)S(1)}, u32[]{:S(2)}, u32[]{:S(2)}) collective-permute-start(f32[3464,128]{1,0:T(8,128)S(1)} %get-tuple-element.18), channel_id=1, source_target_pairs={{0,1},{1,0},{2,3},{3,2},{4,5},{5,4},{6,7},{7,6},{8,9},{9,8},{10,11... | collective-permute-start | bytes 5320712 | tf_op jit(solution)/shard_map/halves/ppermute | solution.py:39
  18.3 8.8 %collective-permute-start.7 = (bf16[2,320,128]{2,1,0:T(8,128)(2,1)S(1)}, bf16[2,320,128]{2,1,0:T(8,128)(2,1)S(1)}, u32[]{:S(2)}, u32[]{:S(2)}) collective-permute-start(bf16[2,320,128]{2,1,0:T(8,128)(2,1)S(1)} %get-tuple-element.19), channel_id=1, source_target_pairs={{16,0},{17,1},{18,2},{19,3},{20,4},{21,5},{22,6},{23,7},{24,8},{25... | collective-permute-start | bytes 491528 | tf_op jit(solution)/shard_map/halves/ppermute | solution.py:49
  22.0 5.1 %copy-start.2 = (bf16[27,256,128]{2,1,0:T(8,128)(2,1)S(1)}, bf16[27,256,128]{2,1,0:T(8,128)(2,1)}, u32[]{:S(2)}) copy-start(bf16[27,256,128]{2,1,0:T(8,128)(2,1)} %weight_ref.1) | copy-start | bytes 5308420
  22.0 5.1 %copy-start.4 = (bf16[576,320]{1,0:T(8,128)(2,1)S(1)}, bf16[576,320]{1,0:T(8,128)(2,1)}, u32[]{:S(2)}) copy-start(bf16[576,320]{1,0:T(8,128)(2,1)} %constant.149.clone.box_ref) | copy-start | bytes 1105924
  22.5 8.2 %collective-permute-start.4 = (f16[872,128]{1,0:T(8,128)(2,1)S(1)}, f16[872,128]{1,0:T(8,128)(2,1)S(1)}, u32[]{:S(2)}, u32[]{:S(2)}) collective-permute-start(f16[872,128]{1,0:T(8,128)(2,1)S(1)} %get-tuple-element.57), channel_id=1, source_target_pairs={{0,16},{1,65},{2,18},{3,67},{4,20},{5,69},{6,22},{7,71},{8,24},{9,... | collective-permute-start | bytes 669704 | tf_op jit(solution)/shard_map/weight_sum/ppermute | solution.py:39
  24.5 7.2 %collective-permute-start.5 = (f16[872,128]{1,0:T(8,128)(2,1)S(1)}, f16[872,128]{1,0:T(8,128)(2,1)S(1)}, u32[]{:S(2)}, u32[]{:S(2)}) collective-permute-start(f16[872,128]{1,0:T(8,128)(2,1)S(1)} %get-tuple-element.56), channel_id=1, source_target_pairs={{0,48},{1,193},{2,50},{3,195},{4,52},{5,197},{6,54},{7,199},{8,56}... | collective-permute-start | bytes 669704 | tf_op jit(solution)/shard_map/weight_sum/ppermute | solution.py:39
  26.4 6.7 %collective-permute-start.6 = (f16[872,128]{1,0:T(8,128)(2,1)S(1)}, f16[872,128]{1,0:T(8,128)(2,1)S(1)}, u32[]{:S(2)}, u32[]{:S(2)}) collective-permute-start(f16[872,128]{1,0:T(8,128)(2,1)S(1)} %get-tuple-element.55), channel_id=1, source_target_pairs={{0,32},{1,129},{2,34},{3,131},{4,36},{5,133},{6,38},{7,135},{8,40}... | collective-permute-start | bytes 669704 | tf_op jit(solution)/shard_map/weight_sum/ppermute | solution.py:39
  33.5 4.6 %collective-permute-start.10 = (f16[224,128]{1,0:T(8,128)(2,1)S(1)}, f16[224,128]{1,0:T(8,128)(2,1)S(1)}, u32[]{:S(2)}, u32[]{:S(2)}) collective-permute-start(f16[224,128]{1,0:T(8,128)(2,1)S(1)} %get-tuple-element.54), channel_id=1, source_target_pairs={{0,128},{1,33},{2,130},{3,35},{4,132},{5,37},{6,134},{7,39},{8,136... | collective-permute-start | bytes 172040 | tf_op jit(solution)/shard_map/weight_sum/ppermute | solution.py:39
  35.2 3.3 %collective-permute-start.8 = (f16[224,128]{1,0:T(8,128)(2,1)S(1)}, f16[224,128]{1,0:T(8,128)(2,1)S(1)}, u32[]{:S(2)}, u32[]{:S(2)}) collective-permute-start(f16[224,128]{1,0:T(8,128)(2,1)S(1)} %get-tuple-element.52), channel_id=1, source_target_pairs={{0,64},{1,17},{2,66},{3,19},{4,68},{5,21},{6,70},{7,23},{8,72},{9,... | collective-permute-start | bytes 172040 | tf_op jit(solution)/shard_map/weight_sum/ppermute | solution.py:39
  35.9 4.2 %collective-permute-start.9 = (f16[224,128]{1,0:T(8,128)(2,1)S(1)}, f16[224,128]{1,0:T(8,128)(2,1)S(1)}, u32[]{:S(2)}, u32[]{:S(2)}) collective-permute-start(f16[224,128]{1,0:T(8,128)(2,1)S(1)} %get-tuple-element.53), channel_id=1, source_target_pairs={{0,192},{1,49},{2,194},{3,51},{4,196},{5,53},{6,198},{7,55},{8,200... | collective-permute-start | bytes 172040 | tf_op jit(solution)/shard_map/weight_sum/ppermute | solution.py:39
  40.3 3.3 %collective-permute-start.11 = (f16[224,128]{1,0:T(8,128)(2,1)S(1)}, f16[224,128]{1,0:T(8,128)(2,1)S(1)}, u32[]{:S(2)}, u32[]{:S(2)}) collective-permute-start(f16[224,128]{1,0:T(8,128)(2,1)S(1)} %pad_maximum_fusion.8), channel_id=1, source_target_pairs={{0,2},{1,3},{2,0},{3,1},{4,6},{5,7},{6,4},{7,5},{8,10},{9,11},{10,... | collective-permute-start | bytes 172040 | tf_op jit(solution)/shard_map/weight_sum/ppermute | solution.py:39
  43.7 10.6 %collective-permute-start.12 = (f16[224,128]{1,0:T(8,128)(2,1)S(1)}, f16[224,128]{1,0:T(8,128)(2,1)S(1)}, u32[]{:S(2)}, u32[]{:S(2)}) collective-permute-start(f16[224,128]{1,0:T(8,128)(2,1)S(1)} %pad_maximum_fusion.9), channel_id=1, source_target_pairs={{0,10},{1,11},{2,8},{3,9},{4,14},{5,15},{6,12},{7,13},{8,2},{9,3},... | collective-permute-start | bytes 172040 | tf_op jit(solution)/shard_map/weight_sum/ppermute | solution.py:39
  50.4 3.9 %collective-permute-start.13 = (f16[224,128]{1,0:T(8,128)(2,1)S(1)}, f16[224,128]{1,0:T(8,128)(2,1)S(1)}, u32[]{:S(2)}, u32[]{:S(2)}) collective-permute-start(f16[224,128]{1,0:T(8,128)(2,1)S(1)} %pad_maximum_fusion.9), channel_id=1, source_target_pairs={{0,12},{1,13},{2,6},{3,7},{4,0},{5,1},{6,10},{7,11},{8,4},{9,5},{1... | collective-permute-start | bytes 172040 | tf_op jit(solution)/shard_map/weight_sum/ppermute | solution.py:39
  51.6 6.0 %collective-permute-start.14 = (f16[224,128]{1,0:T(8,128)(2,1)S(1)}, f16[224,128]{1,0:T(8,128)(2,1)S(1)}, u32[]{:S(2)}, u32[]{:S(2)}) collective-permute-start(f16[224,128]{1,0:T(8,128)(2,1)S(1)} %pad_maximum_fusion.9), channel_id=1, source_target_pairs={{0,14},{1,15},{2,4},{3,5},{4,2},{5,3},{6,8},{7,9},{8,6},{9,7},{10,... | collective-permute-start | bytes 172040 | tf_op jit(solution)/shard_map/weight_sum/ppermute | solution.py:39
  57.7 3.4 %collective-permute-start.15 = (f16[224,128]{1,0:T(8,128)(2,1)S(1)}, f16[224,128]{1,0:T(8,128)(2,1)S(1)}, u32[]{:S(2)}, u32[]{:S(2)}) collective-permute-start(f16[224,128]{1,0:T(8,128)(2,1)S(1)} %pad_maximum_fusion.10), channel_id=1, source_target_pairs={{0,64},{1,17},{2,66},{3,19},{4,68},{5,21},{6,70},{7,23},{8,72},{9,... | collective-permute-start | bytes 172040 | tf_op jit(solution)/shard_map/weight_sum/ppermute | solution.py:39
  57.8 4.3 %collective-permute-start.16 = (f16[224,128]{1,0:T(8,128)(2,1)S(1)}, f16[224,128]{1,0:T(8,128)(2,1)S(1)}, u32[]{:S(2)}, u32[]{:S(2)}) collective-permute-start(f16[224,128]{1,0:T(8,128)(2,1)S(1)} %pad_maximum_fusion.10), channel_id=1, source_target_pairs={{0,192},{1,49},{2,194},{3,51},{4,196},{5,53},{6,198},{7,55},{8,200... | collective-permute-start | bytes 172040 | tf_op jit(solution)/shard_map/weight_sum/ppermute | solution.py:39
  58.5 4.5 %collective-permute-start.17 = (f16[224,128]{1,0:T(8,128)(2,1)S(1)}, f16[224,128]{1,0:T(8,128)(2,1)S(1)}, u32[]{:S(2)}, u32[]{:S(2)}) collective-permute-start(f16[224,128]{1,0:T(8,128)(2,1)S(1)} %pad_maximum_fusion.10), channel_id=1, source_target_pairs={{0,128},{1,33},{2,130},{3,35},{4,132},{5,37},{6,134},{7,39},{8,136... | collective-permute-start | bytes 172040 | tf_op jit(solution)/shard_map/weight_sum/ppermute | solution.py:39
  63.1 9.9 %collective-permute-start.19 = (f16[4,224,128]{2,1,0:T(8,128)(2,1)S(1)}, f16[4,224,128]{2,1,0:T(8,128)(2,1)S(1)}, u32[]{:S(2)}, u32[]{:S(2)}) collective-permute-start(f16[4,224,128]{2,1,0:T(8,128)(2,1)S(1)} %bitcast_dynamic-update-slice_fusion.2), channel_id=1, source_target_pairs={{0,48},{1,193},{2,50},{3,195},{4,52},{5,197},{6,54},{7,199},{8,56}... | collective-permute-start | bytes 688136 | tf_op jit(solution)/shard_map/weight_sum/ppermute | solution.py:39
  65.2 7.8 %collective-permute-start.20 = (f16[4,224,128]{2,1,0:T(8,128)(2,1)S(1)}, f16[4,224,128]{2,1,0:T(8,128)(2,1)S(1)}, u32[]{:S(2)}, u32[]{:S(2)}) collective-permute-start(f16[4,224,128]{2,1,0:T(8,128)(2,1)S(1)} %bitcast_dynamic-update-slice_fusion.2), channel_id=1, source_target_pairs={{0,32},{1,129},{2,34},{3,131},{4,36},{5,133},{6,38},{7,135},{8,40}... | collective-permute-start | bytes 688136 | tf_op jit(solution)/shard_map/weight_sum/ppermute | solution.py:39
  66.6 16.5 %collective-permute-start.18 = (f16[4,224,128]{2,1,0:T(8,128)(2,1)S(1)}, f16[4,224,128]{2,1,0:T(8,128)(2,1)S(1)}, u32[]{:S(2)}, u32[]{:S(2)}) collective-permute-start(f16[4,224,128]{2,1,0:T(8,128)(2,1)S(1)} %bitcast_dynamic-update-slice_fusion.2), channel_id=1, source_target_pairs={{0,16},{1,65},{2,18},{3,67},{4,20},{5,69},{6,22},{7,71},{8,24},{9,... | collective-permute-start | bytes 688136 | tf_op jit(solution)/shard_map/weight_sum/ppermute | solution.py:39
  73.1 12.7 %collective-permute-start.22 = (f16[2,4,224,128]{3,2,1,0:T(8,128)(2,1)S(1)}, f16[2,4,224,128]{3,2,1,0:T(8,128)(2,1)S(1)}, u32[]{:S(2)}, u32[]{:S(2)}) collective-permute-start(f16[2,4,224,128]{3,2,1,0:T(8,128)(2,1)S(1)} %pad_maximum_fusion.1), channel_id=1, source_target_pairs={{0,1},{1,0},{2,3},{3,2},{4,5},{5,4},{6,7},{7,6},{8,9},{9,8},{10,11... | collective-permute-start | bytes 1376264 | tf_op jit(solution)/shard_map/weight_sum/ppermute | solution.py:39
  83.3 2.2 %collective-permute-start.21 = (f16[2,4,224,128]{3,2,1,0:T(8,128)(2,1)S(1)}, f16[2,4,224,128]{3,2,1,0:T(8,128)(2,1)S(1)}, u32[]{:S(2)}, u32[]{:S(2)}) collective-permute-start(f16[2,4,224,128]{3,2,1,0:T(8,128)(2,1)S(1)} %pad_maximum_fusion), channel_id=1, source_target_pairs={{0,1},{1,0},{2,3},{3,2},{4,5},{5,4},{6,7},{7,6},{8,9},{9,8},{10,11... | collective-permute-start | bytes 1376264 | tf_op jit(solution)/shard_map/weight_sum/ppermute | solution.py:39
  86.2 1.8 %copy-start.5 = (f32[2,4,4,216,128]{4,3,2,1,0:T(8,128)}, f32[2,4,4,216,128]{4,3,2,1,0:T(8,128)S(1)}, u32[]{:S(2)}) copy-start(f32[2,4,4,216,128]{4,3,2,1,0:T(8,128)S(1)} %bitcast_dynamic-update-slice_fusion) | copy-start | bytes 10616836

commit v3 on v2

--- a/solution.py
+++ b/solution.py
@@ -2,7 +2,6 @@
 
 import jax
 import jax.numpy as jnp
-import numpy as np
 from jax import lax
 from jax.experimental import pallas as pl
 from jax.experimental.pallas import tpu as pltpu
@@ -18,20 +17,21 @@
     tm, tile = divmod(rank, 16)
     y, x = divmod(tm, 4)
     z, core = divmod(tile, 2)
-    if kind == "core":
-        core ^= 1
-    elif kind == "strip":
+    half = core ^ ((x + y + z) & 1)
+    if kind == "strip":
         tile += 1 if core else -1
         return tm * 16 + tile if 0 <= tile < 16 else None
+    if kind == "core":
+        half ^= 1
     elif kind == "pair":
         z ^= 1
     elif kind == "z":
         z = (z + step if z % 2 else z - step) % 8
-    elif (kind == "first") == (core == 0):
+    elif (kind == "first") == (half == 0):
         x ^= step
     else:
         y ^= step
-    return (y * 4 + x) * 16 + z * 2 + core
+    return (y * 4 + x) * 16 + z * 2 + (half ^ ((x + y + z) & 1))
 
 
 def swapped(value, kind, step=1):
@@ -51,8 +51,9 @@
 
 def position():
     tm, tile = lax.axis_index("tm"), lax.axis_index("tile")
-    y, x, core = tm // 4, tm % 4, tile % 2
-    return core, jnp.where(core == 0, x, y), jnp.where(core == 0, y, x)
+    y, x, z, core = tm // 4, tm % 4, tile // 2, tile % 2
+    half = core ^ ((x + y + z) & 1)
+    return half, jnp.where(half == 0, x, y), jnp.where(half == 0, y, x)
 
 
 def power(exponent):
@@ -94,7 +95,7 @@
 
 
 def summed_everywhere(own, received, grad_input, factor):
-    core, first, second = position()
+    half, first, second = position()
     bound = own[3456:3457] + received[3456:3457]
     exponent = jnp.floor(13 - jnp.log2(jnp.maximum(bound, F32(1e-30))))
     pieces = [own[r : r + 864] + received[r : r + 864] for r in range(0, 3456, 864)]
@@ -121,24 +122,26 @@
             mine = placed_at(mine, pair[k], first ^ step)
             theirs = placed_at(theirs, other[k], second ^ step)
     result = jnp.zeros((2, 4, 4, 216, 128), F32)
-    for half, pieces in ((core, mine), (1 - core, theirs)):
+    for at, pieces in ((half, mine), (1 - half, theirs)):
         scale = power(-pieces[:, :, -8:-7].astype(F32)) * F32(factor)
-        result = placed_at(result, pieces[:, :, :-8].astype(F32) * scale, half)
+        result = placed_at(result, pieces[:, :, :-8].astype(F32) * scale, at)
     return result, grad_input
 
 
-def box_matrix():
-    box = np.zeros((9, 4, 16, 320), np.float32)
-    for dh in range(3):
-        for dw in range(3):
+def box_matrix(box_ref):
+    j = lax.broadcasted_iota(jnp.int32, (16, 320), 0)
+    column = lax.broadcasted_iota(jnp.int32, (16, 320), 1)
+    w = column % 32
+    h = jnp.where(column < 256, column // 32, jnp.where(column < 288, -1, 8))
+    for dw in range(3):
+        from_first = w - (2 * j + 1 - dw)
+        inside = (from_first == 0) | (from_first == 1)
+        for dh in range(3):
             for i in range(4):
-                for j in range(16):
-                    for h in (2 * i + 1 - dh, 2 * i + 2 - dh):
-                        for w in (2 * j + 1 - dw, 2 * j + 2 - dw):
-                            if 0 <= w < 32:
-                                row = 256 if h < 0 else 288 if h > 7 else 32 * h
-                                box[3 * dh + dw, i, j, row + w] = 1
-    return box.reshape(576, 320)
+                from_top = h - (2 * i + 1 - dh)
+                ones = inside & ((from_top == 0) | (from_top == 1))
+                row = 64 * (3 * dh + dw) + 16 * i
+                box_ref[row : row + 16] = jnp.where(ones, F32(1), F32(0)).astype(BF16)
 
 
 def box_sums(box, frame, next_frame, high_ref, low_ref, row):
@@ -181,12 +184,14 @@
 
 
 def weight_kernel(
-    count, x_ref, g_ref, box_ref, previous_ref, inner_ref, outer_ref,
-    own_ref, sent_ref, high_ref, low_ref, later_ref,
+    count, x_ref, g_ref, previous_ref, inner_ref, outer_ref,
+    own_ref, sent_ref, high_ref, low_ref, later_ref, box_ref,
     frames, terms,
 ):
     used = count[0]
-    core, first, second = position()
+    core = lax.axis_index("tile") % 2
+    half, first, second = position()
+    box_matrix(box_ref)
     frames[:, 0:256] = g_ref[...]
     frames[:, pl.ds(pl.multiple_of(288 - 32 * core, 32), 32)] = inner_ref[...]
     frames[:, pl.ds(pl.multiple_of(256 + 32 * core, 32), 32)] = outer_ref[...]
@@ -218,18 +223,18 @@
                     peak[0] = jnp.maximum(peak[0], most(block[: 128 if tap == 13 else 256]))
                 if tap >= 13:
                     peak[1] = jnp.maximum(peak[1], most(block[128 if tap == 13 else 0 :]))
-    for target, half, outer, inner in (
-        (own_ref, core, first, second),
-        (sent_ref, 1 - core, second, first),
+    for target, which, outer, inner in (
+        (own_ref, half, first, second),
+        (sent_ref, 1 - half, second, first),
     ):
         for j in range(16):
-            start = 3456 * half + 864 * ((j // 4) ^ outer) + 216 * ((j % 4) ^ inner)
+            start = 3456 * which + 864 * ((j // 4) ^ outer) + 216 * ((j % 4) ^ inner)
             rows = terms[pl.ds(pl.multiple_of(start, 8), 216)]
             target[216 * j : 216 * j + 216] = rows
     low_half = jnp.broadcast_to(jnp.max(peak[0]), (8, 128))
     high_half = jnp.broadcast_to(jnp.max(peak[1]), (8, 128))
-    own_ref[3456:3464] = jnp.where(core == 0, low_half, high_half)
-    sent_ref[3456:3464] = jnp.where(core == 0, high_half, low_half)
+    own_ref[3456:3464] = jnp.where(half == 0, low_half, high_half)
+    sent_ref[3456:3464] = jnp.where(half == 0, high_half, low_half)
 
 
 def times_taps(high, low, weight_ref, dt):
@@ -270,7 +275,6 @@
 def shards(activations, grad_output, conv_weight, frame_counts):
     latent = activations.reshape(8, 64, 256)
     cotangent = grad_output.reshape(8, 256, 128)
-    box = jnp.asarray(box_matrix(), BF16)
     far = pl.BlockSpec(memory_space=pltpu.HBM)
     near = pl.BlockSpec(memory_space=pltpu.VMEM)
     scalars = pl.BlockSpec(memory_space=pltpu.SMEM)
@@ -293,7 +297,7 @@
         inner = swapped(inner, "core")
         outer = swapped(outer, "strip")
     with jax.named_scope("weight_terms"):
-        own, sent, high, low, later = pl.pallas_call(
+        own, sent, high, low, later, box = pl.pallas_call(
             weight_kernel,
             out_shape=(
                 jax.ShapeDtypeStruct((3464, 128), F32),
@@ -301,9 +305,10 @@
                 jax.ShapeDtypeStruct((512, 1152), BF16),
                 jax.ShapeDtypeStruct((512, 1152), BF16),
                 jax.ShapeDtypeStruct((2, 320, 128), BF16),
+                jax.ShapeDtypeStruct((576, 320), BF16),
             ),
-            in_specs=[scalars] + [near] * 6,
-            out_specs=(near,) * 5,
+            in_specs=[scalars] + [near] * 5,
+            out_specs=(near,) * 6,
             scratch_shapes=[
                 pltpu.VMEM((8, 320, 128), BF16),
                 pltpu.VMEM((6912, 128), F32),
@@ -312,7 +317,7 @@
             cost_estimate=pl.CostEstimate(
                 flops=3 * 10**9, bytes_accessed=10**7, transcendentals=0
             ),
-        )(frame_counts, latent.reshape(512, 256), cotangent, box, previous, inner, outer)
+        )(frame_counts, latent.reshape(512, 256), cotangent, previous, inner, outer)
     with jax.named_scope("halves"):
         later = shifted(later, -1, 0)
         received = swapped(sent, "core")

time: 88.3 us -> 80.9 us (0.916)
  starting transfers between devices: 47.8 us -> 39.3 us
  waiting for transfers between devices: 23.7 us -> 25.6 us
  local copies, waits for them, and re-layouts: 6.08 us -> 5.06 us
    ppermute x21, starting transfers between devices: 42.5 us -> 34.1 us  [swapped(): lax.ppermute(value, BOTH, [pair for pair in pairs if pair[1] is not None])]
    ppermute x21, waiting for transfers between devices: 23.7 us -> 25.6 us  [swapped(): lax.ppermute(value, BOTH, [pair for pair in pairs if pair[1] is not None])]
    unnamed x12 -> x8, local copies, waits for them, and re-layouts: 4.8 us -> 3.78 us
  transfers between devices with their start and end apart: 23 -> 23, of which waited for: 14 -> 13; matrix products, arithmetic and copies ran while one was open for 2% -> 3% of each run, Pallas kernels for 4% -> 4%
where the time goes in v3:
time: 80.9 us; the launch traced here: 80.6 us
  starting transfers between devices  39.3 us (49%)
  waiting for transfers between devices  25.6 us (32%)
  Pallas kernels  6.97 us (9%)
  local copies, waits for them, and re-layouts  5.06 us (6%)
  other arithmetic  2 us (2%)
  between operations  1.62 us (2%)
    ppermute x21, starting transfers between devices, swapped(): lax.ppermute(value, BOTH, [pair for pair in pairs if pair[1] is not None])  34.1 us
    ppermute x21, waiting for transfers between devices, swapped(): lax.ppermute(value, BOTH, [pair for pair in pairs if pair[1] is not None])  25.6 us
    ppermute x2, starting transfers between devices, shifted(): return lax.ppermute(value, BOTH, pairs)  5.24 us
    unnamed x8, local copies, waits for them, and re-layouts  3.78 us
    pallas_call x1, Pallas kernels, shards(): pl.pallas_call(input_kernel, out_shape=jax.ShapeDtypeStruct((512, 256), B...  3.53 us
    pallas_call x1, Pallas kernels, shards(): pl.pallas_call(weight_kernel, out_shape=(jax.ShapeDtypeStruct((3464, 128)...  3.34 us
  transfers between devices with their start and end apart: 23, of which 13 were waited for; matrix products, arithmetic and copies ran while one was open for 3% of the time, Pallas kernels for 4%

profile of v3, /device:TPU:1, one launch (start us, length us, event | category | flops | bytes accessed | tf_op | source)
XLA Modules:
  0.0 80.6 jit_solution(17462023223064391393)
XLA Ops:
  1.3 1.0 %copy-done = bf16[8,8,32,128]{3,2,1,0:T(8,128)(2,1)S(1)} copy-done((bf16[8,8,32,128]{3,2,1,0:T(8,128)(2,1)S(1)}, bf16[8,8,32,128]{3,2,1,0:T(8,128)(2,1)}, u32[]{:S(2)}) %copy-start) | copy-done | bytes 524312
  2.3 0.9 %copy-done.1 = bf16[8,4,16,256]{3,2,1,0:T(8,128)(2,1)S(1)} copy-done((bf16[8,4,16,256]{3,2,1,0:T(8,128)(2,1)S(1)}, bf16[8,4,16,256]{3,2,1,0:T(8,128)(2,1)}, u32[]{:S(2)}) %copy-start.1) | copy-done | bytes 262168
  3.4 3.9 %collective-permute-start = (bf16[2,64,256]{2,1,0:T(8,128)(2,1)S(1)}, bf16[2,64,256]{2,1,0:T(8,128)(2,1)S(1)}, u32[]{:S(2)}, u32[]{:S(2)}) collective-permute-start(bf16[2,64,256]{2,1,0:T(8,128)(2,1)S(1)} %get-tuple-element.15), channel_id=1, source_target_pairs={{0,16},{1,17},{2,18},{3,19},{4,20},{5,21},{6,22},{7,23},{8,24},{9,... | collective-permute-start | bytes 196616 | tf_op jit(solution)/shard_map/edges/ppermute | solution.py:49
  7.3 1.0 %collective-permute-start.1 = (bf16[8,32,128]{2,1,0:T(8,128)(2,1)S(1)}, bf16[8,32,128]{2,1,0:T(8,128)(2,1)S(1)}, u32[]{:S(2)}, u32[]{:S(2)}) collective-permute-start(bf16[8,32,128]{2,1,0:T(8,128)(2,1)S(1)} %get-tuple-element.16), channel_id=1, source_target_pairs={{0,1},{1,0},{2,3},{3,2},{4,5},{5,4},{6,7},{7,6},{8,9},{9,8},{10,11... | collective-permute-start | bytes 196616 | tf_op jit(solution)/shard_map/edges/ppermute | solution.py:39
  8.4 3.4 %collective-permute-start.2 = (bf16[8,32,128]{2,1,0:T(8,128)(2,1)S(1)}, bf16[8,32,128]{2,1,0:T(8,128)(2,1)S(1)}, u32[]{:S(2)}, u32[]{:S(2)}) collective-permute-start(bf16[8,32,128]{2,1,0:T(8,128)(2,1)S(1)} %get-tuple-element.17), channel_id=1, source_target_pairs={{1,2},{2,1},{3,4},{4,3},{5,6},{6,5},{7,8},{8,7},{9,10},{10,9},{11,... | collective-permute-start | bytes 196616 | tf_op jit(solution)/shard_map/edges/ppermute | solution.py:39
  11.9 2.1 %collective-permute-done.2.outer_ref = bf16[8,32,128]{2,1,0:T(8,128)(2,1)S(1)} collective-permute-done((bf16[8,32,128]{2,1,0:T(8,128)(2,1)S(1)}, bf16[8,32,128]{2,1,0:T(8,128)(2,1)S(1)}, u32[]{:S(2)}, u32[]{:S(2)}) %collective-permute-start.2) | collective-permute-done | bytes 65568 | tf_op jit(solution)/shard_map/edges/ppermute | solution.py:39
  14.0 3.3 %weight_terms.1 = (f32[3464,128]{1,0:T(8,128)S(1)}, f32[3464,128]{1,0:T(8,128)S(1)}, bf16[512,1152]{1,0:T(8,128)(2,1)S(1)}, bf16[512,1152]{1,0:T(8,128)(2,1)S(1)...) custom-call(s32[1]{0:T(128)S(6)} %copy.20.count, bf16[512,256]{1,0:T(8,128)(2,1)S(1)} %bitcast.58, ...), custom_call_target="tpu_custom_call" | custom-call | flops 3000000000 | bytes 10000000 | tf_op jit(solution)/shard_map/weight_terms/pallas_call | solution.py:300
  17.4 1.3 %collective-permute-start.7 = (bf16[2,320,128]{2,1,0:T(8,128)(2,1)S(1)}, bf16[2,320,128]{2,1,0:T(8,128)(2,1)S(1)}, u32[]{:S(2)}, u32[]{:S(2)}) collective-permute-start(bf16[2,320,128]{2,1,0:T(8,128)(2,1)S(1)} %get-tuple-element.21), channel_id=1, source_target_pairs={{16,0},{17,1},{18,2},{19,3},{20,4},{21,5},{22,6},{23,7},{24,8},{25... | collective-permute-start | bytes 491528 | tf_op jit(solution)/shard_map/halves/ppermute | solution.py:49
  18.7 2.4 %collective-permute-done.3 = f32[3464,128]{1,0:T(8,128)S(1)} collective-permute-done((f32[3464,128]{1,0:T(8,128)S(1)}, f32[3464,128]{1,0:T(8,128)S(1)}, u32[]{:S(2)}, u32[]{:S(2)}) %collective-permute-start.3) | collective-permute-done | bytes 1773600 | tf_op jit(solution)/shard_map/halves/ppermute | solution.py:39
  21.1 0.2 fusion.3
  21.4 0.2 pad_maximum_fusion.2
  21.6 2.6 %collective-permute-start.4 = (f16[872,128]{1,0:T(8,128)(2,1)S(1)}, f16[872,128]{1,0:T(8,128)(2,1)S(1)}, u32[]{:S(2)}, u32[]{:S(2)}) collective-permute-start(f16[872,128]{1,0:T(8,128)(2,1)S(1)} %get-tuple-element.59), channel_id=1, source_target_pairs={{0,17},{1,64},{2,67},{3,18},{4,21},{5,68},{6,71},{7,22},{8,25},{9,... | collective-permute-start | bytes 669704 | tf_op jit(solution)/shard_map/weight_sum/ppermute | solution.py:39
  24.2 1.5 %collective-permute-start.5 = (f16[872,128]{1,0:T(8,128)(2,1)S(1)}, f16[872,128]{1,0:T(8,128)(2,1)S(1)}, u32[]{:S(2)}, u32[]{:S(2)}) collective-permute-start(f16[872,128]{1,0:T(8,128)(2,1)S(1)} %get-tuple-element.58), channel_id=1, source_target_pairs={{0,49},{1,192},{2,195},{3,50},{4,53},{5,196},{6,199},{7,54},{8,57}... | collective-permute-start | bytes 669704 | tf_op jit(solution)/shard_map/weight_sum/ppermute | solution.py:39
  25.7 1.1 %collective-permute-start.6 = (f16[872,128]{1,0:T(8,128)(2,1)S(1)}, f16[872,128]{1,0:T(8,128)(2,1)S(1)}, u32[]{:S(2)}, u32[]{:S(2)}) collective-permute-start(f16[872,128]{1,0:T(8,128)(2,1)S(1)} %get-tuple-element.57), channel_id=1, source_target_pairs={{0,32},{1,129},{2,130},{3,35},{4,36},{5,133},{6,134},{7,39},{8,40}... | collective-permute-start | bytes 669704 | tf_op jit(solution)/shard_map/weight_sum/ppermute | solution.py:39
  26.8 3.5 %input_terms.1 = bf16[512,256]{1,0:T(8,128)(2,1)} custom-call(s32[1]{0:T(128)S(6)} %copy.20.count, bf16[27,256,128]{2,1,0:T(8,128)(2,1)S(1)} %copy-done.2, bf16[576,320]{1,0:T(8,128)(2,1)S(1)} %get-tuple-element.20.box_ref, bf16[2,320,128]{2,1,0:T(8,128)(2,1)S(1)} %collective-permute-done.7.later_ref, bf16[512,1152]{1,0:T(8,128)(2,1)S(1)} %get-tuple-element.22.high_ref, ...), custom_call_target="tpu_custom_call" | custom-call | flops 2000000000 | bytes 5000000 | tf_op jit(solution)/shard_map/input_terms/pallas_call | solution.py:325
  30.4 2.8 %collective-permute-done.5 = f16[872,128]{1,0:T(8,128)(2,1)S(1)} collective-permute-done((f16[872,128]{1,0:T(8,128)(2,1)S(1)}, f16[872,128]{1,0:T(8,128)(2,1)S(1)}, u32[]{:S(2)}, u32[]{:S(2)}) %collective-permute-start.5) | collective-permute-done | bytes 223264 | tf_op jit(solution)/shard_map/weight_sum/ppermute | solution.py:39
  33.2 0.2 fusion.1
  33.5 1.3 %collective-permute-start.10 = (f16[224,128]{1,0:T(8,128)(2,1)S(1)}, f16[224,128]{1,0:T(8,128)(2,1)S(1)}, u32[]{:S(2)}, u32[]{:S(2)}) collective-permute-start(f16[224,128]{1,0:T(8,128)(2,1)S(1)} %get-tuple-element.56), channel_id=1, source_target_pairs={{0,128},{1,33},{2,34},{3,131},{4,132},{5,37},{6,38},{7,135},{8,136... | collective-permute-start | bytes 172040 | tf_op jit(solution)/shard_map/weight_sum/ppermute | solution.py:39
  34.9 1.2 %collective-permute-start.8 = (f16[224,128]{1,0:T(8,128)(2,1)S(1)}, f16[224,128]{1,0:T(8,128)(2,1)S(1)}, u32[]{:S(2)}, u32[]{:S(2)}) collective-permute-start(f16[224,128]{1,0:T(8,128)(2,1)S(1)} %get-tuple-element.54), channel_id=1, source_target_pairs={{0,65},{1,16},{2,19},{3,66},{4,69},{5,20},{6,23},{7,70},{8,73},{9,... | collective-permute-start | bytes 172040 | tf_op jit(solution)/shard_map/weight_sum/ppermute | solution.py:39
  36.1 1.1 %collective-permute-start.9 = (f16[224,128]{1,0:T(8,128)(2,1)S(1)}, f16[224,128]{1,0:T(8,128)(2,1)S(1)}, u32[]{:S(2)}, u32[]{:S(2)}) collective-permute-start(f16[224,128]{1,0:T(8,128)(2,1)S(1)} %get-tuple-element.55), channel_id=1, source_target_pairs={{0,193},{1,48},{2,51},{3,194},{4,197},{5,52},{6,55},{7,198},{8,201... | collective-permute-start | bytes 172040 | tf_op jit(solution)/shard_map/weight_sum/ppermute | solution.py:39
  37.2 1.0 %collective-permute-done.10 = f16[224,128]{1,0:T(8,128)(2,1)S(1)} collective-permute-done((f16[224,128]{1,0:T(8,128)(2,1)S(1)}, f16[224,128]{1,0:T(8,128)(2,1)S(1)}, u32[]{:S(2)}, u32[]{:S(2)}) %collective-permute-start.10) | collective-permute-done | bytes 57376 | tf_op jit(solution)/shard_map/weight_sum/ppermute | solution.py:39
  38.2 0.7 collective-permute-done.8
  38.8 2.0 %collective-permute-done.9 = f16[224,128]{1,0:T(8,128)(2,1)S(1)} collective-permute-done((f16[224,128]{1,0:T(8,128)(2,1)S(1)}, f16[224,128]{1,0:T(8,128)(2,1)S(1)}, u32[]{:S(2)}, u32[]{:S(2)}) %collective-permute-start.9) | collective-permute-done | bytes 57376 | tf_op jit(solution)/shard_map/weight_sum/ppermute | solution.py:39
  41.1 1.4 %collective-permute-start.11 = (f16[224,128]{1,0:T(8,128)(2,1)S(1)}, f16[224,128]{1,0:T(8,128)(2,1)S(1)}, u32[]{:S(2)}, u32[]{:S(2)}) collective-permute-start(f16[224,128]{1,0:T(8,128)(2,1)S(1)} %pad_maximum_fusion.8), channel_id=1, source_target_pairs={{0,3},{1,2},{2,1},{3,0},{4,7},{5,6},{6,5},{7,4},{8,11},{9,10},{10,... | collective-permute-start | bytes 172040 | tf_op jit(solution)/shard_map/weight_sum/ppermute | solution.py:39
  42.5 2.6 %collective-permute-done.11 = f16[224,128]{1,0:T(8,128)(2,1)S(1)} collective-permute-done((f16[224,128]{1,0:T(8,128)(2,1)S(1)}, f16[224,128]{1,0:T(8,128)(2,1)S(1)}, u32[]{:S(2)}, u32[]{:S(2)}) %collective-permute-start.11) | collective-permute-done | bytes 57376 | tf_op jit(solution)/shard_map/weight_sum/ppermute | solution.py:39
  45.2 6.9 %collective-permute-start.12 = (f16[224,128]{1,0:T(8,128)(2,1)S(1)}, f16[224,128]{1,0:T(8,128)(2,1)S(1)}, u32[]{:S(2)}, u32[]{:S(2)}) collective-permute-start(f16[224,128]{1,0:T(8,128)(2,1)S(1)} %pad_maximum_fusion.9), channel_id=1, source_target_pairs={{0,11},{1,10},{2,9},{3,8},{4,15},{5,14},{6,13},{7,12},{8,3},{9,2},... | collective-permute-start | bytes 172040 | tf_op jit(solution)/shard_map/weight_sum/ppermute | solution.py:39
  52.1 0.5 collective-permute-start.13
  52.6 3.6 %collective-permute-start.14 = (f16[224,128]{1,0:T(8,128)(2,1)S(1)}, f16[224,128]{1,0:T(8,128)(2,1)S(1)}, u32[]{:S(2)}, u32[]{:S(2)}) collective-permute-start(f16[224,128]{1,0:T(8,128)(2,1)S(1)} %pad_maximum_fusion.9), channel_id=1, source_target_pairs={{0,15},{1,14},{2,5},{3,4},{4,3},{5,2},{6,9},{7,8},{8,7},{9,6},{10,... | collective-permute-start | bytes 172040 | tf_op jit(solution)/shard_map/weight_sum/ppermute | solution.py:39
  56.2 0.8 collective-permute-done.13
  57.0 2.0 %collective-permute-done.14 = f16[224,128]{1,0:T(8,128)(2,1)S(1)} collective-permute-done((f16[224,128]{1,0:T(8,128)(2,1)S(1)}, f16[224,128]{1,0:T(8,128)(2,1)S(1)}, u32[]{:S(2)}, u32[]{:S(2)}) %collective-permute-start.14) | collective-permute-done | bytes 57376 | tf_op jit(solution)/shard_map/weight_sum/ppermute | solution.py:39
  59.3 2.0 %collective-permute-start.16 = (f16[224,128]{1,0:T(8,128)(2,1)S(1)}, f16[224,128]{1,0:T(8,128)(2,1)S(1)}, u32[]{:S(2)}, u32[]{:S(2)}) collective-permute-start(f16[224,128]{1,0:T(8,128)(2,1)S(1)} %pad_maximum_fusion.10), channel_id=1, source_target_pairs={{0,193},{1,48},{2,51},{3,194},{4,197},{5,52},{6,55},{7,198},{8,201... | collective-permute-start | bytes 172040 | tf_op jit(solution)/shard_map/weight_sum/ppermute | solution.py:39
  61.3 1.5 %collective-permute-start.17 = (f16[224,128]{1,0:T(8,128)(2,1)S(1)}, f16[224,128]{1,0:T(8,128)(2,1)S(1)}, u32[]{:S(2)}, u32[]{:S(2)}) collective-permute-start(f16[224,128]{1,0:T(8,128)(2,1)S(1)} %pad_maximum_fusion.10), channel_id=1, source_target_pairs={{0,128},{1,33},{2,34},{3,131},{4,132},{5,37},{6,38},{7,135},{8,136... | collective-permute-start | bytes 172040 | tf_op jit(solution)/shard_map/weight_sum/ppermute | solution.py:39
  62.9 1.3 %collective-permute-done.16 = f16[224,128]{1,0:T(8,128)(2,1)S(1)} collective-permute-done((f16[224,128]{1,0:T(8,128)(2,1)S(1)}, f16[224,128]{1,0:T(8,128)(2,1)S(1)}, u32[]{:S(2)}, u32[]{:S(2)}) %collective-permute-start.16) | collective-permute-done | bytes 57376 | tf_op jit(solution)/shard_map/weight_sum/ppermute | solution.py:39
  64.2 1.6 %collective-permute-done.17 = f16[224,128]{1,0:T(8,128)(2,1)S(1)} collective-permute-done((f16[224,128]{1,0:T(8,128)(2,1)S(1)}, f16[224,128]{1,0:T(8,128)(2,1)S(1)}, u32[]{:S(2)}, u32[]{:S(2)}) %collective-permute-start.17) | collective-permute-done | bytes 57376 | tf_op jit(solution)/shard_map/weight_sum/ppermute | solution.py:39
  65.8 2.7 %collective-permute-start.19 = (f16[4,224,128]{2,1,0:T(8,128)(2,1)S(1)}, f16[4,224,128]{2,1,0:T(8,128)(2,1)S(1)}, u32[]{:S(2)}, u32[]{:S(2)}) collective-permute-start(f16[4,224,128]{2,1,0:T(8,128)(2,1)S(1)} %bitcast_dynamic-update-slice_fusion.2), channel_id=1, source_target_pairs={{0,49},{1,192},{2,195},{3,50},{4,53},{5,196},{6,199},{7,54},{8,57}... | collective-permute-start | bytes 688136 | tf_op jit(solution)/shard_map/weight_sum/ppermute | solution.py:39
  68.5 1.0 %collective-permute-start.20 = (f16[4,224,128]{2,1,0:T(8,128)(2,1)S(1)}, f16[4,224,128]{2,1,0:T(8,128)(2,1)S(1)}, u32[]{:S(2)}, u32[]{:S(2)}) collective-permute-start(f16[4,224,128]{2,1,0:T(8,128)(2,1)S(1)} %bitcast_dynamic-update-slice_fusion.2), channel_id=1, source_target_pairs={{0,32},{1,129},{2,130},{3,35},{4,36},{5,133},{6,134},{7,39},{8,40}... | collective-permute-start | bytes 688136 | tf_op jit(solution)/shard_map/weight_sum/ppermute | solution.py:39
  69.5 0.3 collective-permute-start.18
  69.8 0.1 broadcast_in_dim.576.clone
  70.0 5.4 %collective-permute-done.19 = f16[4,224,128]{2,1,0:T(8,128)(2,1)S(1)} collective-permute-done((f16[4,224,128]{2,1,0:T(8,128)(2,1)S(1)}, f16[4,224,128]{2,1,0:T(8,128)(2,1)S(1)}, u32[]{:S(2)}, u32[]{:S(2)}) %collective-permute-start.19) | collective-permute-done | bytes 229408 | tf_op jit(solution)/shard_map/weight_sum/ppermute | solution.py:39
  75.3 0.1 pad_maximum_fusion.1
  75.5 0.5 collective-permute-start.22
  76.1 0.2 collective-permute-start.21
  76.6 0.3 broadcast_in_dim.575
  76.9 0.2 bitcast_dynamic-update-slice_fusion.1
  77.1 0.9 %collective-permute-done.21 = f16[2,4,224,128]{3,2,1,0:T(8,128)(2,1)S(1)} collective-permute-done((f16[2,4,224,128]{3,2,1,0:T(8,128)(2,1)S(1)}, f16[2,4,224,128]{3,2,1,0:T(8,128)(2,1)S(1)}, u32[]{:S(2)}, u32[]{:S(2)}) %collective-permute-start.21) | collective-permute-done | bytes 458784 | tf_op jit(solution)/shard_map/weight_sum/ppermute | solution.py:39
  78.1 0.1 broadcast_in_dim.576.clone.1
  78.6 0.2 bitcast_dynamic-update-slice_fusion
  78.9 1.8 %copy-done.3 = f32[2,4,4,216,128]{4,3,2,1,0:T(8,128)} copy-done((f32[2,4,4,216,128]{4,3,2,1,0:T(8,128)}, f32[2,4,4,216,128]{4,3,2,1,0:T(8,128)S(1)}, u32[]{:S(2)}) %copy-start.3) | copy-done | bytes 3538968
  (59 shorter events, 2.0 us)
Async XLA Ops:
  1.3 1.0 %copy-start = (bf16[8,8,32,128]{3,2,1,0:T(8,128)(2,1)S(1)}, bf16[8,8,32,128]{3,2,1,0:T(8,128)(2,1)}, u32[]{:S(2)}) copy-start(bf16[8,8,32,128]{3,2,1,0:T(8,128)(2,1)} %param.5) | copy-start | bytes 1572868
  2.3 0.9 %copy-start.1 = (bf16[8,4,16,256]{3,2,1,0:T(8,128)(2,1)S(1)}, bf16[8,4,16,256]{3,2,1,0:T(8,128)(2,1)}, u32[]{:S(2)}) copy-start(bf16[8,4,16,256]{3,2,1,0:T(8,128)(2,1)} %param.4) | copy-start | bytes 786436
  3.4 8.5 %collective-permute-start = (bf16[2,64,256]{2,1,0:T(8,128)(2,1)S(1)}, bf16[2,64,256]{2,1,0:T(8,128)(2,1)S(1)}, u32[]{:S(2)}, u32[]{:S(2)}) collective-permute-start(bf16[2,64,256]{2,1,0:T(8,128)(2,1)S(1)} %get-tuple-element.15), channel_id=1, source_target_pairs={{0,16},{1,17},{2,18},{3,19},{4,20},{5,21},{6,22},{7,23},{8,24},{9,... | collective-permute-start | bytes 196616 | tf_op jit(solution)/shard_map/edges/ppermute | solution.py:49
  7.3 4.5 %collective-permute-start.1 = (bf16[8,32,128]{2,1,0:T(8,128)(2,1)S(1)}, bf16[8,32,128]{2,1,0:T(8,128)(2,1)S(1)}, u32[]{:S(2)}, u32[]{:S(2)}) collective-permute-start(bf16[8,32,128]{2,1,0:T(8,128)(2,1)S(1)} %get-tuple-element.16), channel_id=1, source_target_pairs={{0,1},{1,0},{2,3},{3,2},{4,5},{5,4},{6,7},{7,6},{8,9},{9,8},{10,11... | collective-permute-start | bytes 196616 | tf_op jit(solution)/shard_map/edges/ppermute | solution.py:39
  8.4 5.6 %collective-permute-start.2 = (bf16[8,32,128]{2,1,0:T(8,128)(2,1)S(1)}, bf16[8,32,128]{2,1,0:T(8,128)(2,1)S(1)}, u32[]{:S(2)}, u32[]{:S(2)}) collective-permute-start(bf16[8,32,128]{2,1,0:T(8,128)(2,1)S(1)} %get-tuple-element.17), channel_id=1, source_target_pairs={{1,2},{2,1},{3,4},{4,3},{5,6},{6,5},{7,8},{8,7},{9,10},{10,9},{11,... | collective-permute-start | bytes 196616 | tf_op jit(solution)/shard_map/edges/ppermute | solution.py:39
  17.3 3.8 %collective-permute-start.3 = (f32[3464,128]{1,0:T(8,128)S(1)}, f32[3464,128]{1,0:T(8,128)S(1)}, u32[]{:S(2)}, u32[]{:S(2)}) collective-permute-start(f32[3464,128]{1,0:T(8,128)S(1)} %get-tuple-element.19), channel_id=1, source_target_pairs={{0,1},{1,0},{2,3},{3,2},{4,5},{5,4},{6,7},{7,6},{8,9},{9,8},{10,11... | collective-permute-start | bytes 5320712 | tf_op jit(solution)/shard_map/halves/ppermute | solution.py:39
  17.4 9.4 %collective-permute-start.7 = (bf16[2,320,128]{2,1,0:T(8,128)(2,1)S(1)}, bf16[2,320,128]{2,1,0:T(8,128)(2,1)S(1)}, u32[]{:S(2)}, u32[]{:S(2)}) collective-permute-start(bf16[2,320,128]{2,1,0:T(8,128)(2,1)S(1)} %get-tuple-element.21), channel_id=1, source_target_pairs={{16,0},{17,1},{18,2},{19,3},{20,4},{21,5},{22,6},{23,7},{24,8},{25... | collective-permute-start | bytes 491528 | tf_op jit(solution)/shard_map/halves/ppermute | solution.py:49
  21.1 5.7 %copy-start.2 = (bf16[27,256,128]{2,1,0:T(8,128)(2,1)S(1)}, bf16[27,256,128]{2,1,0:T(8,128)(2,1)}, u32[]{:S(2)}) copy-start(bf16[27,256,128]{2,1,0:T(8,128)(2,1)} %weight_ref.1) | copy-start | bytes 5308420
  21.6 8.8 %collective-permute-start.4 = (f16[872,128]{1,0:T(8,128)(2,1)S(1)}, f16[872,128]{1,0:T(8,128)(2,1)S(1)}, u32[]{:S(2)}, u32[]{:S(2)}) collective-permute-start(f16[872,128]{1,0:T(8,128)(2,1)S(1)} %get-tuple-element.59), channel_id=1, source_target_pairs={{0,17},{1,64},{2,67},{3,18},{4,21},{5,68},{6,71},{7,22},{8,25},{9,... | collective-permute-start | bytes 669704 | tf_op jit(solution)/shard_map/weight_sum/ppermute | solution.py:39
  24.2 9.0 %collective-permute-start.5 = (f16[872,128]{1,0:T(8,128)(2,1)S(1)}, f16[872,128]{1,0:T(8,128)(2,1)S(1)}, u32[]{:S(2)}, u32[]{:S(2)}) collective-permute-start(f16[872,128]{1,0:T(8,128)(2,1)S(1)} %get-tuple-element.58), channel_id=1, source_target_pairs={{0,49},{1,192},{2,195},{3,50},{4,53},{5,196},{6,199},{7,54},{8,57}... | collective-permute-start | bytes 669704 | tf_op jit(solution)/shard_map/weight_sum/ppermute | solution.py:39
  25.7 7.5 %collective-permute-start.6 = (f16[872,128]{1,0:T(8,128)(2,1)S(1)}, f16[872,128]{1,0:T(8,128)(2,1)S(1)}, u32[]{:S(2)}, u32[]{:S(2)}) collective-permute-start(f16[872,128]{1,0:T(8,128)(2,1)S(1)} %get-tuple-element.57), channel_id=1, source_target_pairs={{0,32},{1,129},{2,130},{3,35},{4,36},{5,133},{6,134},{7,39},{8,40}... | collective-permute-start | bytes 669704 | tf_op jit(solution)/shard_map/weight_sum/ppermute | solution.py:39
  33.5 4.6 %collective-permute-start.10 = (f16[224,128]{1,0:T(8,128)(2,1)S(1)}, f16[224,128]{1,0:T(8,128)(2,1)S(1)}, u32[]{:S(2)}, u32[]{:S(2)}) collective-permute-start(f16[224,128]{1,0:T(8,128)(2,1)S(1)} %get-tuple-element.56), channel_id=1, source_target_pairs={{0,128},{1,33},{2,34},{3,131},{4,132},{5,37},{6,38},{7,135},{8,136... | collective-permute-start | bytes 172040 | tf_op jit(solution)/shard_map/weight_sum/ppermute | solution.py:39
  34.9 4.0 %collective-permute-start.8 = (f16[224,128]{1,0:T(8,128)(2,1)S(1)}, f16[224,128]{1,0:T(8,128)(2,1)S(1)}, u32[]{:S(2)}, u32[]{:S(2)}) collective-permute-start(f16[224,128]{1,0:T(8,128)(2,1)S(1)} %get-tuple-element.54), channel_id=1, source_target_pairs={{0,65},{1,16},{2,19},{3,66},{4,69},{5,20},{6,23},{7,70},{8,73},{9,... | collective-permute-start | bytes 172040 | tf_op jit(solution)/shard_map/weight_sum/ppermute | solution.py:39
  36.1 4.8 %collective-permute-start.9 = (f16[224,128]{1,0:T(8,128)(2,1)S(1)}, f16[224,128]{1,0:T(8,128)(2,1)S(1)}, u32[]{:S(2)}, u32[]{:S(2)}) collective-permute-start(f16[224,128]{1,0:T(8,128)(2,1)S(1)} %get-tuple-element.55), channel_id=1, source_target_pairs={{0,193},{1,48},{2,51},{3,194},{4,197},{5,52},{6,55},{7,198},{8,201... | collective-permute-start | bytes 172040 | tf_op jit(solution)/shard_map/weight_sum/ppermute | solution.py:39
  41.1 4.0 %collective-permute-start.11 = (f16[224,128]{1,0:T(8,128)(2,1)S(1)}, f16[224,128]{1,0:T(8,128)(2,1)S(1)}, u32[]{:S(2)}, u32[]{:S(2)}) collective-permute-start(f16[224,128]{1,0:T(8,128)(2,1)S(1)} %pad_maximum_fusion.8), channel_id=1, source_target_pairs={{0,3},{1,2},{2,1},{3,0},{4,7},{5,6},{6,5},{7,4},{8,11},{9,10},{10,... | collective-permute-start | bytes 172040 | tf_op jit(solution)/shard_map/weight_sum/ppermute | solution.py:39
  45.2 11.0 %collective-permute-start.12 = (f16[224,128]{1,0:T(8,128)(2,1)S(1)}, f16[224,128]{1,0:T(8,128)(2,1)S(1)}, u32[]{:S(2)}, u32[]{:S(2)}) collective-permute-start(f16[224,128]{1,0:T(8,128)(2,1)S(1)} %pad_maximum_fusion.9), channel_id=1, source_target_pairs={{0,11},{1,10},{2,9},{3,8},{4,15},{5,14},{6,13},{7,12},{8,3},{9,2},... | collective-permute-start | bytes 172040 | tf_op jit(solution)/shard_map/weight_sum/ppermute | solution.py:39
  52.1 4.9 %collective-permute-start.13 = (f16[224,128]{1,0:T(8,128)(2,1)S(1)}, f16[224,128]{1,0:T(8,128)(2,1)S(1)}, u32[]{:S(2)}, u32[]{:S(2)}) collective-permute-start(f16[224,128]{1,0:T(8,128)(2,1)S(1)} %pad_maximum_fusion.9), channel_id=1, source_target_pairs={{0,12},{1,13},{2,6},{3,7},{4,0},{5,1},{6,10},{7,11},{8,4},{9,5},{1... | collective-permute-start | bytes 172040 | tf_op jit(solution)/shard_map/weight_sum/ppermute | solution.py:39
  52.6 6.4 %collective-permute-start.14 = (f16[224,128]{1,0:T(8,128)(2,1)S(1)}, f16[224,128]{1,0:T(8,128)(2,1)S(1)}, u32[]{:S(2)}, u32[]{:S(2)}) collective-permute-start(f16[224,128]{1,0:T(8,128)(2,1)S(1)} %pad_maximum_fusion.9), channel_id=1, source_target_pairs={{0,15},{1,14},{2,5},{3,4},{4,3},{5,2},{6,9},{7,8},{8,7},{9,6},{10,... | collective-permute-start | bytes 172040 | tf_op jit(solution)/shard_map/weight_sum/ppermute | solution.py:39
  59.2 3.7 %collective-permute-start.15 = (f16[224,128]{1,0:T(8,128)(2,1)S(1)}, f16[224,128]{1,0:T(8,128)(2,1)S(1)}, u32[]{:S(2)}, u32[]{:S(2)}) collective-permute-start(f16[224,128]{1,0:T(8,128)(2,1)S(1)} %pad_maximum_fusion.10), channel_id=1, source_target_pairs={{0,65},{1,16},{2,19},{3,66},{4,69},{5,20},{6,23},{7,70},{8,73},{9,... | collective-permute-start | bytes 172040 | tf_op jit(solution)/shard_map/weight_sum/ppermute | solution.py:39
  59.3 4.9 %collective-permute-start.16 = (f16[224,128]{1,0:T(8,128)(2,1)S(1)}, f16[224,128]{1,0:T(8,128)(2,1)S(1)}, u32[]{:S(2)}, u32[]{:S(2)}) collective-permute-start(f16[224,128]{1,0:T(8,128)(2,1)S(1)} %pad_maximum_fusion.10), channel_id=1, source_target_pairs={{0,193},{1,48},{2,51},{3,194},{4,197},{5,52},{6,55},{7,198},{8,201... | collective-permute-start | bytes 172040 | tf_op jit(solution)/shard_map/weight_sum/ppermute | solution.py:39
  61.3 4.5 %collective-permute-start.17 = (f16[224,128]{1,0:T(8,128)(2,1)S(1)}, f16[224,128]{1,0:T(8,128)(2,1)S(1)}, u32[]{:S(2)}, u32[]{:S(2)}) collective-permute-start(f16[224,128]{1,0:T(8,128)(2,1)S(1)} %pad_maximum_fusion.10), channel_id=1, source_target_pairs={{0,128},{1,33},{2,34},{3,131},{4,132},{5,37},{6,38},{7,135},{8,136... | collective-permute-start | bytes 172040 | tf_op jit(solution)/shard_map/weight_sum/ppermute | solution.py:39
  65.8 9.5 %collective-permute-start.19 = (f16[4,224,128]{2,1,0:T(8,128)(2,1)S(1)}, f16[4,224,128]{2,1,0:T(8,128)(2,1)S(1)}, u32[]{:S(2)}, u32[]{:S(2)}) collective-permute-start(f16[4,224,128]{2,1,0:T(8,128)(2,1)S(1)} %bitcast_dynamic-update-slice_fusion.2), channel_id=1, source_target_pairs={{0,49},{1,192},{2,195},{3,50},{4,53},{5,196},{6,199},{7,54},{8,57}... | collective-permute-start | bytes 688136 | tf_op jit(solution)/shard_map/weight_sum/ppermute | solution.py:39
  68.5 6.8 %collective-permute-start.20 = (f16[4,224,128]{2,1,0:T(8,128)(2,1)S(1)}, f16[4,224,128]{2,1,0:T(8,128)(2,1)S(1)}, u32[]{:S(2)}, u32[]{:S(2)}) collective-permute-start(f16[4,224,128]{2,1,0:T(8,128)(2,1)S(1)} %bitcast_dynamic-update-slice_fusion.2), channel_id=1, source_target_pairs={{0,32},{1,129},{2,130},{3,35},{4,36},{5,133},{6,134},{7,39},{8,40}... | collective-permute-start | bytes 688136 | tf_op jit(solution)/shard_map/weight_sum/ppermute | solution.py:39
  69.5 6.5 %collective-permute-start.18 = (f16[4,224,128]{2,1,0:T(8,128)(2,1)S(1)}, f16[4,224,128]{2,1,0:T(8,128)(2,1)S(1)}, u32[]{:S(2)}, u32[]{:S(2)}) collective-permute-start(f16[4,224,128]{2,1,0:T(8,128)(2,1)S(1)} %bitcast_dynamic-update-slice_fusion.2), channel_id=1, source_target_pairs={{0,17},{1,64},{2,67},{3,18},{4,21},{5,68},{6,71},{7,22},{8,25},{9,... | collective-permute-start | bytes 688136 | tf_op jit(solution)/shard_map/weight_sum/ppermute | solution.py:39
  75.5 2.9 %collective-permute-start.22 = (f16[2,4,224,128]{3,2,1,0:T(8,128)(2,1)S(1)}, f16[2,4,224,128]{3,2,1,0:T(8,128)(2,1)S(1)}, u32[]{:S(2)}, u32[]{:S(2)}) collective-permute-start(f16[2,4,224,128]{3,2,1,0:T(8,128)(2,1)S(1)} %pad_maximum_fusion.1), channel_id=1, source_target_pairs={{0,1},{1,0},{2,3},{3,2},{4,5},{5,4},{6,7},{7,6},{8,9},{9,8},{10,11... | collective-permute-start | bytes 1376264 | tf_op jit(solution)/shard_map/weight_sum/ppermute | solution.py:39
  76.1 2.0 %collective-permute-start.21 = (f16[2,4,224,128]{3,2,1,0:T(8,128)(2,1)S(1)}, f16[2,4,224,128]{3,2,1,0:T(8,128)(2,1)S(1)}, u32[]{:S(2)}, u32[]{:S(2)}) collective-permute-start(f16[2,4,224,128]{3,2,1,0:T(8,128)(2,1)S(1)} %pad_maximum_fusion), channel_id=1, source_target_pairs={{0,1},{1,0},{2,3},{3,2},{4,5},{5,4},{6,7},{7,6},{8,9},{9,8},{10,11... | collective-permute-start | bytes 1376264 | tf_op jit(solution)/shard_map/weight_sum/ppermute | solution.py:39
  78.8 1.8 %copy-start.3 = (f32[2,4,4,216,128]{4,3,2,1,0:T(8,128)}, f32[2,4,4,216,128]{4,3,2,1,0:T(8,128)S(1)}, u32[]{:S(2)}) copy-start(f32[2,4,4,216,128]{4,3,2,1,0:T(8,128)S(1)} %bitcast_dynamic-update-slice_fusion) | copy-start | bytes 10616836

commit v4 on v3

--- a/solution.py
+++ b/solution.py
@@ -1,3 +1,4 @@
+import functools
 import math
 
 import jax
@@ -8,6 +9,7 @@
 from jax.sharding import PartitionSpec as P
 
 BOTH = ("tm", "tile")
+ORDER = (0, 1, 3, 2)
 F32 = jnp.float32
 BF16 = jnp.bfloat16
 F16 = jnp.float16
@@ -71,6 +73,10 @@
     return jnp.concatenate([(value * scale).astype(F16), tail], axis=0)
 
 
+def fitting(bound):
+    return jnp.floor(13 - jnp.log2(jnp.maximum(bound, F32(1e-30))))
+
+
 def opened(message):
     exponent = message[-8:-7].astype(F32)
     return message[:-8].astype(F32) * power(-exponent), exponent
@@ -80,7 +86,7 @@
     scale = power(exponent)
     lowest = exponent
     parts = [pieces[0]]
-    arrived = [swapped(packed(pieces[step], exponent, scale), kind, step) for step in (1, 3, 2)]
+    arrived = [swapped(packed(pieces[step], exponent, scale), kind, step) for step in ORDER[1:]]
     if after is not None:
         *arrived, after = lax.optimization_barrier((*arrived, after))
     for message in arrived:
@@ -94,37 +100,37 @@
     return lax.dynamic_update_index_in_dim(buffer, piece, place, 0)
 
 
-def summed_everywhere(own, received, grad_input, factor):
+def summed_everywhere(own, received, partial, finished, factor):
     half, first, second = position()
-    bound = own[3456:3457] + received[3456:3457]
-    exponent = jnp.floor(13 - jnp.log2(jnp.maximum(bound, F32(1e-30))))
+    received, theirs = opened(received)
+    exponent = fitting(own[3456:3457] + 2.0**14 * power(-theirs))
     pieces = [own[r : r + 864] + received[r : r + 864] for r in range(0, 3456, 864)]
-    total, exponent, grad_input = scattered(pieces, exponent, "first", grad_input)
+    total, exponent, partial = scattered(pieces, exponent, "first", partial)
     pieces = [total[r : r + 216] for r in range(0, 864, 216)]
-    total, exponent, _ = scattered(pieces, exponent, "second")
+    total, exponent, grad_input = scattered(pieces, exponent, "second", finished(partial))
     message = packed(total, exponent, power(exponent))
     (a, e), (b, f) = opened(message), opened(swapped(message, "pair"))
     total, exponent = a + b, jnp.minimum(e, f) - 1
     message = packed(total, exponent, power(exponent))
-    parts = [opened(message)] + [opened(swapped(message, "z", step)) for step in (3, 2, 1)]
-    total = (parts[0][0] + parts[1][0]) + (parts[2][0] + parts[3][0])
+    parts = [opened(message)] + [opened(swapped(message, "z", step)) for step in (1, 2, 3)]
+    total = (parts[0][0] + parts[3][0]) + (parts[1][0] + parts[2][0])
     exponent = jnp.stack([part[1] for part in parts]).min(axis=0) - 2
     message = packed(total, exponent, power(exponent))
     row = jnp.zeros((4, 224, 128), F16)
-    for step in (0, 1, 3, 2):
+    for step in ORDER:
         theirs = swapped(message, "second", step) if step else message
         row = placed_at(row, theirs, second ^ step)
-    pieces = [row] + [swapped(row, "first", step) for step in (1, 3, 2)]
-    mine = theirs = jnp.zeros((4, 4, 224, 128), F16)
-    for pair, steps in ((pieces[:2], (0, 1)), (pieces[2:], (3, 2))):
-        other = swapped(jnp.stack(pair), "core")
-        for k, step in enumerate(steps):
-            mine = placed_at(mine, pair[k], first ^ step)
-            theirs = placed_at(theirs, other[k], second ^ step)
-    result = jnp.zeros((2, 4, 4, 216, 128), F32)
-    for at, pieces in ((half, mine), (1 - half, theirs)):
-        scale = power(-pieces[:, :, -8:-7].astype(F32)) * F32(factor)
-        result = placed_at(result, pieces[:, :, :-8].astype(F32) * scale, at)
+    mine = [row] + [swapped(row, "first", step) for step in ORDER[1:]]
+    theirs = [
+        piece for pair in (mine[:2], mine[2:]) for piece in swapped(jnp.stack(pair), "core")
+    ]
+
+    def restored(piece):
+        scale = power(-piece[:, -8:-7].astype(F32)) * F32(factor)
+        return piece[:, :-8].astype(F32) * scale
+
+    result = stored([restored(piece) for piece in mine])
+    result = stored([restored(piece) for piece in theirs], result)
     return result, grad_input
 
 
@@ -251,11 +257,7 @@
     return total
 
 
-def input_kernel(
-    count, weight_ref, box_ref, later_ref, high_ref, low_ref,
-    grad_ref, later_high, later_low, total,
-):
-    used = count[0]
+def input_kernel(weight_ref, high_ref, low_ref, total):
     for dt in (2, 1, 0):
         start = 64 * (2 - dt)
         term = times_taps(high_ref[start:512], low_ref[start:512], weight_ref, dt)
@@ -263,6 +265,13 @@
             total[0 : 512 - start] += term
         else:
             total[...] = term
+
+
+def later_kernel(
+    count, weight_ref, box_ref, later_ref, before_ref, grad_ref, later_high, later_low, total
+):
+    used = count[0]
+    total[...] = before_ref[...]
     box_sums(box_ref[...], later_ref[0], later_ref[1], later_high, later_low, 0)
     two = pl.ds(pl.multiple_of(64 * used - 128, 64), 128)
     total[two] += times_taps(later_high[...], later_low[...], weight_ref, 0)
@@ -270,6 +279,36 @@
     total[one] += times_taps(later_high[0:64], later_low[0:64], weight_ref, 1)
     slot = lax.broadcasted_iota(jnp.int32, (512, 256), 0) // 64
     grad_ref[...] = jnp.where(slot < used, total[...], F32(0)).astype(BF16)
+
+
+def store_kernel(other, *refs):
+    pieces, (out, sems) = refs[:4], refs[-2:]
+    half, first, second = position()
+    half, place = (1 - half, second) if other else (half, first)
+    copies = [
+        pltpu.make_async_copy(piece, out.at[half, place ^ step], sems.at[step])
+        for step, piece in zip(ORDER, pieces)
+    ]
+    for copy in copies:
+        copy.start()
+    for copy in copies:
+        copy.wait()
+
+
+def stored(pieces, before=None):
+    far = pl.BlockSpec(memory_space=pltpu.HBM)
+    near = pl.BlockSpec(memory_space=pltpu.VMEM)
+    other = before is not None
+    return pl.pallas_call(
+        functools.partial(store_kernel, other),
+        out_shape=jax.ShapeDtypeStruct((2, 4, 4, 216, 128), F32),
+        in_specs=[near] * 4 + [far] * other,
+        out_specs=far,
+        scratch_shapes=[pltpu.SemaphoreType.DMA((4,))],
+        input_output_aliases={4: 0} if other else {},
+        compiler_params=pltpu.CompilerParams(vmem_limit_bytes=24 * 2**20),
+        cost_estimate=pl.CostEstimate(flops=0, bytes_accessed=4 * 10**6, transcendentals=0),
+    )(*pieces, *([before] if other else []))
 
 
 def shards(activations, grad_output, conv_weight, frame_counts):
@@ -319,27 +358,42 @@
             ),
         )(frame_counts, latent.reshape(512, 256), cotangent, previous, inner, outer)
     with jax.named_scope("halves"):
+        exponent = fitting(sent[3456:3457])
+        received = swapped(packed(sent[:3456], exponent, power(exponent)), "core")
         later = shifted(later, -1, 0)
-        received = swapped(sent, "core")
     with jax.named_scope("input_terms"):
-        grad_input = pl.pallas_call(
+        partial = pl.pallas_call(
             input_kernel,
-            out_shape=jax.ShapeDtypeStruct((512, 256), BF16),
-            in_specs=[scalars] + [near] * 5,
+            out_shape=jax.ShapeDtypeStruct((512, 256), F32),
+            in_specs=[near] * 3,
             out_specs=near,
-            scratch_shapes=[
-                pltpu.VMEM((128, 1152), BF16),
-                pltpu.VMEM((128, 1152), BF16),
-                pltpu.VMEM((512, 256), F32),
-            ],
             compiler_params=params,
             cost_estimate=pl.CostEstimate(
                 flops=2 * 10**9, bytes_accessed=5 * 10**6, transcendentals=0
             ),
-        )(frame_counts, conv_weight, box, later, high, low)
+        )(conv_weight, high, low)
+    with jax.named_scope("later"):
+
+        def finished(partial):
+            return pl.pallas_call(
+                later_kernel,
+                out_shape=jax.ShapeDtypeStruct((512, 256), BF16),
+                in_specs=[scalars] + [near] * 4,
+                out_specs=near,
+                scratch_shapes=[
+                    pltpu.VMEM((128, 1152), BF16),
+                    pltpu.VMEM((128, 1152), BF16),
+                    pltpu.VMEM((512, 256), F32),
+                ],
+                compiler_params=params,
+                cost_estimate=pl.CostEstimate(
+                    flops=5 * 10**8, bytes_accessed=10**6, transcendentals=0
+                ),
+            )(frame_counts, conv_weight, box, later, partial)
+
     with jax.named_scope("weight_sum"):
         factor = 1.0 / math.sqrt(16 * 16 * 2048)
-        grad_weight, grad_input = summed_everywhere(own, received, grad_input, factor)
+        grad_weight, grad_input = summed_everywhere(own, received, partial, finished, factor)
     return grad_input.reshape(8, 4, 16, 256), grad_weight.reshape(27, 256, 128)
 
 

time: 80.9 us -> 80.7 us (level)
  local copies, waits for them, and re-layouts: 5.06 us -> 2.33 us
  Pallas kernels: 6.97 us -> 9.62 us
  waiting for transfers between devices: 25.6 us -> 24.7 us
    pallas_call x1 -> x4, Pallas kernels: 3.53 us -> 6.19 us  [the longest x2 2.52 us: stored(): pl.pallas_call(functools.partial(store_kernel, other), out_shape=jax.Shap...]
    unnamed x8 -> x6, local copies, waits for them, and re-layouts: 3.78 us -> 1.99 us
    ppermute x21, waiting for transfers between devices: 25.6 us -> 24.7 us  [swapped(): lax.ppermute(value, BOTH, [pair for pair in pairs if pair[1] is not None])]
  transfers between devices with their start and end apart: 23 -> 23, of which waited for: 13 -> 15; matrix products, arithmetic and copies ran while one was open for 3% -> 1% of each run, Pallas kernels for 4% -> 6%
where the time goes in v4:
time: 80.7 us; the launch traced here: 80.5 us
  starting transfers between devices  39.4 us (49%)
  waiting for transfers between devices  24.7 us (31%)
  Pallas kernels  9.62 us (12%)
  other arithmetic  2.47 us (3%)
  local copies, waits for them, and re-layouts  2.33 us (3%)
  between operations  1.92 us (2%)
    ppermute x21, starting transfers between devices, swapped(): lax.ppermute(value, BOTH, [pair for pair in pairs if pair[1] is not None])  34.2 us
    ppermute x21, waiting for transfers between devices, swapped(): lax.ppermute(value, BOTH, [pair for pair in pairs if pair[1] is not None])  24.7 us
    ppermute x2, starting transfers between devices, shifted(): return lax.ppermute(value, BOTH, pairs)  5.23 us
    pallas_call x1, Pallas kernels, shards(): pl.pallas_call(weight_kernel, out_shape=(jax.ShapeDtypeStruct((3464, 128)...  3.33 us
    pallas_call x2, Pallas kernels, stored(): pl.pallas_call(functools.partial(store_kernel, other), out_shape=jax.Shap...  2.52 us
    unnamed x6, local copies, waits for them, and re-layouts  1.99 us
    pallas_call x1, Pallas kernels, shards(): pl.pallas_call(input_kernel, out_shape=jax.ShapeDtypeStruct((512, 256), F...  1.96 us
    pallas_call x1, Pallas kernels, finished(): pl.pallas_call(later_kernel, out_shape=jax.ShapeDtypeStruct((512, 256), B...  1.71 us
  transfers between devices with their start and end apart: 23, of which 15 were waited for; matrix products, arithmetic and copies ran while one was open for 1% of the time, Pallas kernels for 6%

profile of v4, /device:TPU:1, one launch (start us, length us, event | category | flops | bytes accessed | tf_op | source)
XLA Modules:
  0.0 80.5 jit_solution(9618627251394497082)
XLA Ops:
  1.3 1.0 %copy-done.1 = bf16[8,8,32,128]{3,2,1,0:T(8,128)(2,1)S(1)} copy-done((bf16[8,8,32,128]{3,2,1,0:T(8,128)(2,1)S(1)}, bf16[8,8,32,128]{3,2,1,0:T(8,128)(2,1)}, u32[]{:S(2)}) %copy-start.1) | copy-done | bytes 524312
  2.3 0.9 %copy-done.2 = bf16[8,4,16,256]{3,2,1,0:T(8,128)(2,1)S(1)} copy-done((bf16[8,4,16,256]{3,2,1,0:T(8,128)(2,1)S(1)}, bf16[8,4,16,256]{3,2,1,0:T(8,128)(2,1)}, u32[]{:S(2)}) %copy-start.2) | copy-done | bytes 262168
  3.3 0.1 edges.1
  3.4 3.9 %collective-permute-start = (bf16[2,64,256]{2,1,0:T(8,128)(2,1)S(1)}, bf16[2,64,256]{2,1,0:T(8,128)(2,1)S(1)}, u32[]{:S(2)}, u32[]{:S(2)}) collective-permute-start(bf16[2,64,256]{2,1,0:T(8,128)(2,1)S(1)} %get-tuple-element.19), channel_id=1, source_target_pairs={{0,16},{1,17},{2,18},{3,19},{4,20},{5,21},{6,22},{7,23},{8,24},{9,... | collective-permute-start | bytes 196616 | tf_op jit(solution)/shard_map/edges/ppermute | solution.py:51
  7.3 1.0 %collective-permute-start.1 = (bf16[8,32,128]{2,1,0:T(8,128)(2,1)S(1)}, bf16[8,32,128]{2,1,0:T(8,128)(2,1)S(1)}, u32[]{:S(2)}, u32[]{:S(2)}) collective-permute-start(bf16[8,32,128]{2,1,0:T(8,128)(2,1)S(1)} %get-tuple-element.20), channel_id=1, source_target_pairs={{0,1},{1,0},{2,3},{3,2},{4,5},{5,4},{6,7},{7,6},{8,9},{9,8},{10,11... | collective-permute-start | bytes 196616 | tf_op jit(solution)/shard_map/edges/ppermute | solution.py:41
  8.4 3.4 %collective-permute-start.2 = (bf16[8,32,128]{2,1,0:T(8,128)(2,1)S(1)}, bf16[8,32,128]{2,1,0:T(8,128)(2,1)S(1)}, u32[]{:S(2)}, u32[]{:S(2)}) collective-permute-start(bf16[8,32,128]{2,1,0:T(8,128)(2,1)S(1)} %get-tuple-element.21), channel_id=1, source_target_pairs={{1,2},{2,1},{3,4},{4,3},{5,6},{6,5},{7,8},{8,7},{9,10},{10,9},{11,... | collective-permute-start | bytes 196616 | tf_op jit(solution)/shard_map/edges/ppermute | solution.py:41
  11.9 2.1 %collective-permute-done.2.outer_ref = bf16[8,32,128]{2,1,0:T(8,128)(2,1)S(1)} collective-permute-done((bf16[8,32,128]{2,1,0:T(8,128)(2,1)S(1)}, bf16[8,32,128]{2,1,0:T(8,128)(2,1)S(1)}, u32[]{:S(2)}, u32[]{:S(2)}) %collective-permute-start.2) | collective-permute-done | bytes 65568 | tf_op jit(solution)/shard_map/edges/ppermute | solution.py:41
  14.0 3.3 %weight_terms.1 = (f32[3464,128]{1,0:T(8,128)S(1)}, f32[3464,128]{1,0:T(8,128)S(1)}, bf16[512,1152]{1,0:T(8,128)(2,1)S(1)}, bf16[512,1152]{1,0:T(8,128)(2,1)S(1)...) custom-call(s32[1]{0:T(128)S(6)} %copy.12.count, bf16[512,256]{1,0:T(8,128)(2,1)S(1)} %bitcast.68, ...), custom_call_target="tpu_custom_call" | custom-call | flops 3000000000 | bytes 10000000 | tf_op jit(solution)/shard_map/weight_terms/pallas_call | solution.py:339
  17.3 0.2 multiply_convert_fusion
  17.5 0.2 pad_maximum_fusion
  17.9 2.4 %collective-permute-done.3 = f16[3464,128]{1,0:T(8,128)(2,1)S(1)} collective-permute-done((f16[3464,128]{1,0:T(8,128)(2,1)S(1)}, f16[3464,128]{1,0:T(8,128)(2,1)S(1)}, u32[]{:S(2)}, u32[]{:S(2)}) %collective-permute-start.3) | collective-permute-done | bytes 886816 | tf_op jit(solution)/shard_map/halves/ppermute | solution.py:41
  20.3 0.1 convert_multiply_fusion
  20.5 0.2 fusion.1
  20.7 0.2 pad_maximum_fusion.3
  20.9 3.0 %collective-permute-start.6 = (f16[872,128]{1,0:T(8,128)(2,1)S(1)}, f16[872,128]{1,0:T(8,128)(2,1)S(1)}, u32[]{:S(2)}, u32[]{:S(2)}) collective-permute-start(f16[872,128]{1,0:T(8,128)(2,1)S(1)} %get-tuple-element.71), channel_id=1, source_target_pairs={{0,32},{1,129},{2,130},{3,35},{4,36},{5,133},{6,134},{7,39},{8,40}... | collective-permute-start | bytes 669704 | tf_op jit(solution)/shard_map/weight_sum/ppermute | solution.py:41
  23.9 1.1 %collective-permute-start.5 = (f16[872,128]{1,0:T(8,128)(2,1)S(1)}, f16[872,128]{1,0:T(8,128)(2,1)S(1)}, u32[]{:S(2)}, u32[]{:S(2)}) collective-permute-start(f16[872,128]{1,0:T(8,128)(2,1)S(1)} %get-tuple-element.72), channel_id=1, source_target_pairs={{0,49},{1,192},{2,195},{3,50},{4,53},{5,196},{6,199},{7,54},{8,57}... | collective-permute-start | bytes 669704 | tf_op jit(solution)/shard_map/weight_sum/ppermute | solution.py:41
  25.0 1.3 %collective-permute-start.10 = (bf16[2,320,128]{2,1,0:T(8,128)(2,1)S(1)}, bf16[2,320,128]{2,1,0:T(8,128)(2,1)S(1)}, u32[]{:S(2)}, u32[]{:S(2)}) collective-permute-start(bf16[2,320,128]{2,1,0:T(8,128)(2,1)S(1)} %get-tuple-element.30), channel_id=1, source_target_pairs={{16,0},{17,1},{18,2},{19,3},{20,4},{21,5},{22,6},{23,7},{24,8},{25... | collective-permute-start | bytes 491528 | tf_op jit(solution)/shard_map/halves/ppermute | solution.py:51
  26.3 2.0 %input_terms.1.before_ref = f32[512,256]{1,0:T(8,128)S(1)} custom-call(bf16[27,256,128]{2,1,0:T(8,128)(2,1)S(1)} %copy-done, bf16[512,1152]{1,0:T(8,128)(2,1)S(1)} %get-tuple-element.24.high_ref, bf16[512,1152]{1,0:T(8,128)(2,1)S(1)} %get-tuple-element.25.low_ref), custom_call_target="tpu_custom_call" | custom-call | flops 2000000000 | bytes 5000000 | tf_op jit(solution)/shard_map/input_terms/pallas_call | solution.py:365
  28.2 2.3 %collective-permute-done.5 = f16[872,128]{1,0:T(8,128)(2,1)S(1)} collective-permute-done((f16[872,128]{1,0:T(8,128)(2,1)S(1)}, f16[872,128]{1,0:T(8,128)(2,1)S(1)}, u32[]{:S(2)}, u32[]{:S(2)}) %collective-permute-start.5) | collective-permute-done | bytes 223264 | tf_op jit(solution)/shard_map/weight_sum/ppermute | solution.py:41
  30.6 0.4 collective-permute-done.4
  31.0 0.2 fusion.7
  31.3 2.5 %collective-permute-start.9 = (f16[224,128]{1,0:T(8,128)(2,1)S(1)}, f16[224,128]{1,0:T(8,128)(2,1)S(1)}, u32[]{:S(2)}, u32[]{:S(2)}) collective-permute-start(f16[224,128]{1,0:T(8,128)(2,1)S(1)} %get-tuple-element.68), channel_id=1, source_target_pairs={{0,128},{1,33},{2,34},{3,131},{4,132},{5,37},{6,38},{7,135},{8,136... | collective-permute-start | bytes 172040 | tf_op jit(solution)/shard_map/weight_sum/ppermute | solution.py:41
  33.8 1.3 %collective-permute-start.8 = (f16[224,128]{1,0:T(8,128)(2,1)S(1)}, f16[224,128]{1,0:T(8,128)(2,1)S(1)}, u32[]{:S(2)}, u32[]{:S(2)}) collective-permute-start(f16[224,128]{1,0:T(8,128)(2,1)S(1)} %get-tuple-element.69), channel_id=1, source_target_pairs={{0,193},{1,48},{2,51},{3,194},{4,197},{5,52},{6,55},{7,198},{8,201... | collective-permute-start | bytes 172040 | tf_op jit(solution)/shard_map/weight_sum/ppermute | solution.py:41
  35.1 1.7 %weight_sum.3 = bf16[512,256]{1,0:T(8,128)(2,1)} custom-call(s32[1]{0:T(128)S(6)} %copy.12.count, bf16[27,256,128]{2,1,0:T(8,128)(2,1)S(1)} %copy-done, bf16[576,320]{1,0:T(8,128)(2,1)S(1)} %get-tuple-element.29.box_ref, bf16[2,320,128]{2,1,0:T(8,128)(2,1)S(1)} %collective-permute-done.10.later_ref, f32[512,256]{1,0:T(8,128)S(1)} %input_terms.1.before_ref), custom_call_target="tpu_custom_call" | custom-call | flops 500000000 | bytes 1000000 | tf_op jit(solution)/shard_map/weight_sum/pallas_call | solution.py:378
  36.8 2.1 %collective-permute-done.8 = f16[224,128]{1,0:T(8,128)(2,1)S(1)} collective-permute-done((f16[224,128]{1,0:T(8,128)(2,1)S(1)}, f16[224,128]{1,0:T(8,128)(2,1)S(1)}, u32[]{:S(2)}, u32[]{:S(2)}) %collective-permute-start.8) | collective-permute-done | bytes 57376 | tf_op jit(solution)/shard_map/weight_sum/ppermute | solution.py:41
  39.2 1.5 %collective-permute-start.11 = (f16[224,128]{1,0:T(8,128)(2,1)S(1)}, f16[224,128]{1,0:T(8,128)(2,1)S(1)}, u32[]{:S(2)}, u32[]{:S(2)}) collective-permute-start(f16[224,128]{1,0:T(8,128)(2,1)S(1)} %pad_maximum_fusion.9), channel_id=1, source_target_pairs={{0,3},{1,2},{2,1},{3,0},{4,7},{5,6},{6,5},{7,4},{8,11},{9,10},{10,... | collective-permute-start | bytes 172040 | tf_op jit(solution)/shard_map/weight_sum/ppermute | solution.py:41
  40.7 3.0 %collective-permute-done.11 = f16[224,128]{1,0:T(8,128)(2,1)S(1)} collective-permute-done((f16[224,128]{1,0:T(8,128)(2,1)S(1)}, f16[224,128]{1,0:T(8,128)(2,1)S(1)}, u32[]{:S(2)}, u32[]{:S(2)}) %collective-permute-start.11) | collective-permute-done | bytes 57376 | tf_op jit(solution)/shard_map/weight_sum/ppermute | solution.py:41
  43.9 6.1 %collective-permute-start.14 = (f16[224,128]{1,0:T(8,128)(2,1)S(1)}, f16[224,128]{1,0:T(8,128)(2,1)S(1)}, u32[]{:S(2)}, u32[]{:S(2)}) collective-permute-start(f16[224,128]{1,0:T(8,128)(2,1)S(1)} %pad_maximum_fusion.10), channel_id=1, source_target_pairs={{0,12},{1,13},{2,6},{3,7},{4,0},{5,1},{6,10},{7,11},{8,4},{9,5},{1... | collective-permute-start | bytes 172040 | tf_op jit(solution)/shard_map/weight_sum/ppermute | solution.py:41
  50.0 3.7 %collective-permute-start.12 = (f16[224,128]{1,0:T(8,128)(2,1)S(1)}, f16[224,128]{1,0:T(8,128)(2,1)S(1)}, u32[]{:S(2)}, u32[]{:S(2)}) collective-permute-start(f16[224,128]{1,0:T(8,128)(2,1)S(1)} %pad_maximum_fusion.10), channel_id=1, source_target_pairs={{0,11},{1,10},{2,9},{3,8},{4,15},{5,14},{6,13},{7,12},{8,3},{9,2},... | collective-permute-start | bytes 172040 | tf_op jit(solution)/shard_map/weight_sum/ppermute | solution.py:41
  53.7 1.9 %collective-permute-done.13 = f16[224,128]{1,0:T(8,128)(2,1)S(1)} collective-permute-done((f16[224,128]{1,0:T(8,128)(2,1)S(1)}, f16[224,128]{1,0:T(8,128)(2,1)S(1)}, u32[]{:S(2)}, u32[]{:S(2)}) %collective-permute-start.13) | collective-permute-done | bytes 57376 | tf_op jit(solution)/shard_map/weight_sum/ppermute | solution.py:41
  55.7 2.0 %collective-permute-done.12 = f16[224,128]{1,0:T(8,128)(2,1)S(1)} collective-permute-done((f16[224,128]{1,0:T(8,128)(2,1)S(1)}, f16[224,128]{1,0:T(8,128)(2,1)S(1)}, u32[]{:S(2)}, u32[]{:S(2)}) %collective-permute-start.12) | collective-permute-done | bytes 57376 | tf_op jit(solution)/shard_map/weight_sum/ppermute | solution.py:41
  57.8 0.4 collective-permute-start.16
  58.2 0.8 %collective-permute-start.15 = (f16[224,128]{1,0:T(8,128)(2,1)S(1)}, f16[224,128]{1,0:T(8,128)(2,1)S(1)}, u32[]{:S(2)}, u32[]{:S(2)}) collective-permute-start(f16[224,128]{1,0:T(8,128)(2,1)S(1)} %pad_maximum_fusion.11), channel_id=1, source_target_pairs={{0,65},{1,16},{2,19},{3,66},{4,69},{5,20},{6,23},{7,70},{8,73},{9,... | collective-permute-start | bytes 172040 | tf_op jit(solution)/shard_map/weight_sum/ppermute | solution.py:41
  59.0 3.0 %collective-permute-start.17 = (f16[224,128]{1,0:T(8,128)(2,1)S(1)}, f16[224,128]{1,0:T(8,128)(2,1)S(1)}, u32[]{:S(2)}, u32[]{:S(2)}) collective-permute-start(f16[224,128]{1,0:T(8,128)(2,1)S(1)} %pad_maximum_fusion.11), channel_id=1, source_target_pairs={{0,128},{1,33},{2,34},{3,131},{4,132},{5,37},{6,38},{7,135},{8,136... | collective-permute-start | bytes 172040 | tf_op jit(solution)/shard_map/weight_sum/ppermute | solution.py:41
  62.2 0.7 collective-permute-done.16
  62.9 1.4 %collective-permute-done.17 = f16[224,128]{1,0:T(8,128)(2,1)S(1)} collective-permute-done((f16[224,128]{1,0:T(8,128)(2,1)S(1)}, f16[224,128]{1,0:T(8,128)(2,1)S(1)}, u32[]{:S(2)}, u32[]{:S(2)}) %collective-permute-start.17) | collective-permute-done | bytes 57376 | tf_op jit(solution)/shard_map/weight_sum/ppermute | solution.py:41
  64.3 1.0 %collective-permute-start.21 = (f16[4,224,128]{2,1,0:T(8,128)(2,1)S(1)}, f16[4,224,128]{2,1,0:T(8,128)(2,1)S(1)}, u32[]{:S(2)}, u32[]{:S(2)}) collective-permute-start(f16[4,224,128]{2,1,0:T(8,128)(2,1)S(1)} %bitcast_dynamic-update-slice_fusion), channel_id=1, source_target_pairs={{0,32},{1,129},{2,130},{3,35},{4,36},{5,133},{6,134},{7,39},{8,40}... | collective-permute-start | bytes 688136 | tf_op jit(solution)/shard_map/weight_sum/ppermute | solution.py:41
  65.3 3.7 %collective-permute-start.20 = (f16[4,224,128]{2,1,0:T(8,128)(2,1)S(1)}, f16[4,224,128]{2,1,0:T(8,128)(2,1)S(1)}, u32[]{:S(2)}, u32[]{:S(2)}) collective-permute-start(f16[4,224,128]{2,1,0:T(8,128)(2,1)S(1)} %bitcast_dynamic-update-slice_fusion), channel_id=1, source_target_pairs={{0,49},{1,192},{2,195},{3,50},{4,53},{5,196},{6,199},{7,54},{8,57}... | collective-permute-start | bytes 688136 | tf_op jit(solution)/shard_map/weight_sum/ppermute | solution.py:41
  69.1 2.0 %collective-permute-done.21 = f16[4,224,128]{2,1,0:T(8,128)(2,1)S(1)} collective-permute-done((f16[4,224,128]{2,1,0:T(8,128)(2,1)S(1)}, f16[4,224,128]{2,1,0:T(8,128)(2,1)S(1)}, u32[]{:S(2)}, u32[]{:S(2)}) %collective-permute-start.21) | collective-permute-done | bytes 229408 | tf_op jit(solution)/shard_map/weight_sum/ppermute | solution.py:41
  71.1 3.0 %collective-permute-done.20 = f16[4,224,128]{2,1,0:T(8,128)(2,1)S(1)} collective-permute-done((f16[4,224,128]{2,1,0:T(8,128)(2,1)S(1)}, f16[4,224,128]{2,1,0:T(8,128)(2,1)S(1)}, u32[]{:S(2)}, u32[]{:S(2)}) %collective-permute-start.20) | collective-permute-done | bytes 229408 | tf_op jit(solution)/shard_map/weight_sum/ppermute | solution.py:41
  74.1 1.0 %collective-permute-done.18 = f16[4,224,128]{2,1,0:T(8,128)(2,1)S(1)} collective-permute-done((f16[4,224,128]{2,1,0:T(8,128)(2,1)S(1)}, f16[4,224,128]{2,1,0:T(8,128)(2,1)S(1)}, u32[]{:S(2)}, u32[]{:S(2)}) %collective-permute-start.18) | collective-permute-done | bytes 229408 | tf_op jit(solution)/shard_map/weight_sum/ppermute | solution.py:41
  75.2 0.1 pad_maximum_fusion.2
  75.3 1.3 %collective-permute-start.22 = (f16[2,4,224,128]{3,2,1,0:T(8,128)(2,1)S(1)}, f16[2,4,224,128]{3,2,1,0:T(8,128)(2,1)S(1)}, u32[]{:S(2)}, u32[]{:S(2)}) collective-permute-start(f16[2,4,224,128]{3,2,1,0:T(8,128)(2,1)S(1)} %pad_maximum_fusion.2), channel_id=1, source_target_pairs={{0,1},{1,0},{2,3},{3,2},{4,5},{5,4},{6,7},{7,6},{8,9},{9,8},{10,11... | collective-permute-start | bytes 1376264 | tf_op jit(solution)/shard_map/weight_sum/ppermute | solution.py:41
  76.6 0.1 pad_maximum_fusion.1
  76.7 0.1 collective-permute-start.19
  77.0 1.3 %weight_sum.4.refs_4_ = f32[2,4,4,216,128]{4,3,2,1,0:T(8,128)} custom-call(f32[4,216,128]{2,1,0:T(8,128)S(1)} %convert_multiply_fusion.4.refs_0_, f32[4,216,128]{2,1,0:T(8,128)S(1)} %convert_multiply_fusion.3.refs_1_, f32[4,216,128]{2,1,0:T(8,128)S(1)} %convert_multiply_fusion.2.refs_2_, f32[4,216,128]{2,1,0:T(8,128)S(1)} %convert_multiply_fusion.1.refs_3_), custom_call_target="tpu_custom_call" | custom-call | bytes 4000000 | tf_op jit(solution)/shard_map/weight_sum/pallas_call | solution.py:302
  78.5 0.3 collective-permute-done.19
  79.1 1.3 %weight_sum.5 = f32[2,4,4,216,128]{4,3,2,1,0:T(8,128)} custom-call(f32[4,216,128]{2,1,0:T(8,128)S(1)} %get-tuple-element.79.refs_0_, f32[4,216,128]{2,1,0:T(8,128)S(1)} %get-tuple-element.78.refs_1_, f32[4,216,128]{2,1,0:T(8,128)S(1)} %get-tuple-element.81.refs_2_, f32[4,216,128]{2,1,0:T(8,128)S(1)} %get-tuple-element.80.refs_3_, ...), custom_call_target="tpu_custom_call", output_to_operand_aliasing={{}: (4, {})} | custom-call | bytes 4000000 | tf_op jit(solution)/shard_map/weight_sum/pallas_call | solution.py:302
  (74 shorter events, 1.7 us)
Async XLA Ops:
  1.3 1.0 %copy-start.1 = (bf16[8,8,32,128]{3,2,1,0:T(8,128)(2,1)S(1)}, bf16[8,8,32,128]{3,2,1,0:T(8,128)(2,1)}, u32[]{:S(2)}) copy-start(bf16[8,8,32,128]{3,2,1,0:T(8,128)(2,1)} %param.5) | copy-start | bytes 1572868
  2.3 0.9 %copy-start.2 = (bf16[8,4,16,256]{3,2,1,0:T(8,128)(2,1)S(1)}, bf16[8,4,16,256]{3,2,1,0:T(8,128)(2,1)}, u32[]{:S(2)}) copy-start(bf16[8,4,16,256]{3,2,1,0:T(8,128)(2,1)} %param.4) | copy-start | bytes 786436
  3.4 8.5 %collective-permute-start = (bf16[2,64,256]{2,1,0:T(8,128)(2,1)S(1)}, bf16[2,64,256]{2,1,0:T(8,128)(2,1)S(1)}, u32[]{:S(2)}, u32[]{:S(2)}) collective-permute-start(bf16[2,64,256]{2,1,0:T(8,128)(2,1)S(1)} %get-tuple-element.19), channel_id=1, source_target_pairs={{0,16},{1,17},{2,18},{3,19},{4,20},{5,21},{6,22},{7,23},{8,24},{9,... | collective-permute-start | bytes 196616 | tf_op jit(solution)/shard_map/edges/ppermute | solution.py:51
  7.3 4.5 %collective-permute-start.1 = (bf16[8,32,128]{2,1,0:T(8,128)(2,1)S(1)}, bf16[8,32,128]{2,1,0:T(8,128)(2,1)S(1)}, u32[]{:S(2)}, u32[]{:S(2)}) collective-permute-start(bf16[8,32,128]{2,1,0:T(8,128)(2,1)S(1)} %get-tuple-element.20), channel_id=1, source_target_pairs={{0,1},{1,0},{2,3},{3,2},{4,5},{5,4},{6,7},{7,6},{8,9},{9,8},{10,11... | collective-permute-start | bytes 196616 | tf_op jit(solution)/shard_map/edges/ppermute | solution.py:41
  8.4 5.6 %collective-permute-start.2 = (bf16[8,32,128]{2,1,0:T(8,128)(2,1)S(1)}, bf16[8,32,128]{2,1,0:T(8,128)(2,1)S(1)}, u32[]{:S(2)}, u32[]{:S(2)}) collective-permute-start(bf16[8,32,128]{2,1,0:T(8,128)(2,1)S(1)} %get-tuple-element.21), channel_id=1, source_target_pairs={{1,2},{2,1},{3,4},{4,3},{5,6},{6,5},{7,8},{8,7},{9,10},{10,9},{11,... | collective-permute-start | bytes 196616 | tf_op jit(solution)/shard_map/edges/ppermute | solution.py:41
  17.8 2.5 %collective-permute-start.3 = (f16[3464,128]{1,0:T(8,128)(2,1)S(1)}, f16[3464,128]{1,0:T(8,128)(2,1)S(1)}, u32[]{:S(2)}, u32[]{:S(2)}) collective-permute-start(f16[3464,128]{1,0:T(8,128)(2,1)S(1)} %pad_maximum_fusion), channel_id=1, source_target_pairs={{0,1},{1,0},{2,3},{3,2},{4,5},{5,4},{6,7},{7,6},{8,9},{9,8},{10,11... | collective-permute-start | bytes 2660360 | tf_op jit(solution)/shard_map/halves/ppermute | solution.py:41
  20.5 5.8 %copy-start = (bf16[27,256,128]{2,1,0:T(8,128)(2,1)S(1)}, bf16[27,256,128]{2,1,0:T(8,128)(2,1)}, u32[]{:S(2)}) copy-start(bf16[27,256,128]{2,1,0:T(8,128)(2,1)} %weight_ref.3) | copy-start | bytes 5308420
  20.9 7.4 %collective-permute-start.6 = (f16[872,128]{1,0:T(8,128)(2,1)S(1)}, f16[872,128]{1,0:T(8,128)(2,1)S(1)}, u32[]{:S(2)}, u32[]{:S(2)}) collective-permute-start(f16[872,128]{1,0:T(8,128)(2,1)S(1)} %get-tuple-element.71), channel_id=1, source_target_pairs={{0,32},{1,129},{2,130},{3,35},{4,36},{5,133},{6,134},{7,39},{8,40}... | collective-permute-start | bytes 669704 | tf_op jit(solution)/shard_map/weight_sum/ppermute | solution.py:41
  23.9 6.7 %collective-permute-start.5 = (f16[872,128]{1,0:T(8,128)(2,1)S(1)}, f16[872,128]{1,0:T(8,128)(2,1)S(1)}, u32[]{:S(2)}, u32[]{:S(2)}) collective-permute-start(f16[872,128]{1,0:T(8,128)(2,1)S(1)} %get-tuple-element.72), channel_id=1, source_target_pairs={{0,49},{1,192},{2,195},{3,50},{4,53},{5,196},{6,199},{7,54},{8,57}... | collective-permute-start | bytes 669704 | tf_op jit(solution)/shard_map/weight_sum/ppermute | solution.py:41
  25.0 6.0 %collective-permute-start.4 = (f16[872,128]{1,0:T(8,128)(2,1)S(1)}, f16[872,128]{1,0:T(8,128)(2,1)S(1)}, u32[]{:S(2)}, u32[]{:S(2)}) collective-permute-start(f16[872,128]{1,0:T(8,128)(2,1)S(1)} %get-tuple-element.73), channel_id=1, source_target_pairs={{0,17},{1,64},{2,67},{3,18},{4,21},{5,68},{6,71},{7,22},{8,25},{9,... | collective-permute-start | bytes 669704 | tf_op jit(solution)/shard_map/weight_sum/ppermute | solution.py:41
  25.0 10.2 %collective-permute-start.10 = (bf16[2,320,128]{2,1,0:T(8,128)(2,1)S(1)}, bf16[2,320,128]{2,1,0:T(8,128)(2,1)S(1)}, u32[]{:S(2)}, u32[]{:S(2)}) collective-permute-start(bf16[2,320,128]{2,1,0:T(8,128)(2,1)S(1)} %get-tuple-element.30), channel_id=1, source_target_pairs={{16,0},{17,1},{18,2},{19,3},{20,4},{21,5},{22,6},{23,7},{24,8},{25... | collective-permute-start | bytes 491528 | tf_op jit(solution)/shard_map/halves/ppermute | solution.py:51
  31.3 5.6 %collective-permute-start.9 = (f16[224,128]{1,0:T(8,128)(2,1)S(1)}, f16[224,128]{1,0:T(8,128)(2,1)S(1)}, u32[]{:S(2)}, u32[]{:S(2)}) collective-permute-start(f16[224,128]{1,0:T(8,128)(2,1)S(1)} %get-tuple-element.68), channel_id=1, source_target_pairs={{0,128},{1,33},{2,34},{3,131},{4,132},{5,37},{6,38},{7,135},{8,136... | collective-permute-start | bytes 172040 | tf_op jit(solution)/shard_map/weight_sum/ppermute | solution.py:41
  33.8 5.1 %collective-permute-start.8 = (f16[224,128]{1,0:T(8,128)(2,1)S(1)}, f16[224,128]{1,0:T(8,128)(2,1)S(1)}, u32[]{:S(2)}, u32[]{:S(2)}) collective-permute-start(f16[224,128]{1,0:T(8,128)(2,1)S(1)} %get-tuple-element.69), channel_id=1, source_target_pairs={{0,193},{1,48},{2,51},{3,194},{4,197},{5,52},{6,55},{7,198},{8,201... | collective-permute-start | bytes 172040 | tf_op jit(solution)/shard_map/weight_sum/ppermute | solution.py:41
  35.1 3.9 %collective-permute-start.7 = (f16[224,128]{1,0:T(8,128)(2,1)S(1)}, f16[224,128]{1,0:T(8,128)(2,1)S(1)}, u32[]{:S(2)}, u32[]{:S(2)}) collective-permute-start(f16[224,128]{1,0:T(8,128)(2,1)S(1)} %get-tuple-element.70), channel_id=1, source_target_pairs={{0,65},{1,16},{2,19},{3,66},{4,69},{5,20},{6,23},{7,70},{8,73},{9,... | collective-permute-start | bytes 172040 | tf_op jit(solution)/shard_map/weight_sum/ppermute | solution.py:41
  39.2 4.6 %collective-permute-start.11 = (f16[224,128]{1,0:T(8,128)(2,1)S(1)}, f16[224,128]{1,0:T(8,128)(2,1)S(1)}, u32[]{:S(2)}, u32[]{:S(2)}) collective-permute-start(f16[224,128]{1,0:T(8,128)(2,1)S(1)} %pad_maximum_fusion.9), channel_id=1, source_target_pairs={{0,3},{1,2},{2,1},{3,0},{4,7},{5,6},{6,5},{7,4},{8,11},{9,10},{10,... | collective-permute-start | bytes 172040 | tf_op jit(solution)/shard_map/weight_sum/ppermute | solution.py:41
  43.9 9.8 %collective-permute-start.14 = (f16[224,128]{1,0:T(8,128)(2,1)S(1)}, f16[224,128]{1,0:T(8,128)(2,1)S(1)}, u32[]{:S(2)}, u32[]{:S(2)}) collective-permute-start(f16[224,128]{1,0:T(8,128)(2,1)S(1)} %pad_maximum_fusion.10), channel_id=1, source_target_pairs={{0,12},{1,13},{2,6},{3,7},{4,0},{5,1},{6,10},{7,11},{8,4},{9,5},{1... | collective-permute-start | bytes 172040 | tf_op jit(solution)/shard_map/weight_sum/ppermute | solution.py:41
  50.0 5.7 %collective-permute-start.13 = (f16[224,128]{1,0:T(8,128)(2,1)S(1)}, f16[224,128]{1,0:T(8,128)(2,1)S(1)}, u32[]{:S(2)}, u32[]{:S(2)}) collective-permute-start(f16[224,128]{1,0:T(8,128)(2,1)S(1)} %pad_maximum_fusion.10), channel_id=1, source_target_pairs={{0,15},{1,14},{2,5},{3,4},{4,3},{5,2},{6,9},{7,8},{8,7},{9,6},{10,... | collective-permute-start | bytes 172040 | tf_op jit(solution)/shard_map/weight_sum/ppermute | solution.py:41
  50.0 7.7 %collective-permute-start.12 = (f16[224,128]{1,0:T(8,128)(2,1)S(1)}, f16[224,128]{1,0:T(8,128)(2,1)S(1)}, u32[]{:S(2)}, u32[]{:S(2)}) collective-permute-start(f16[224,128]{1,0:T(8,128)(2,1)S(1)} %pad_maximum_fusion.10), channel_id=1, source_target_pairs={{0,11},{1,10},{2,9},{3,8},{4,15},{5,14},{6,13},{7,12},{8,3},{9,2},... | collective-permute-start | bytes 172040 | tf_op jit(solution)/shard_map/weight_sum/ppermute | solution.py:41
  57.8 5.0 %collective-permute-start.16 = (f16[224,128]{1,0:T(8,128)(2,1)S(1)}, f16[224,128]{1,0:T(8,128)(2,1)S(1)}, u32[]{:S(2)}, u32[]{:S(2)}) collective-permute-start(f16[224,128]{1,0:T(8,128)(2,1)S(1)} %pad_maximum_fusion.11), channel_id=1, source_target_pairs={{0,193},{1,48},{2,51},{3,194},{4,197},{5,52},{6,55},{7,198},{8,201... | collective-permute-start | bytes 172040 | tf_op jit(solution)/shard_map/weight_sum/ppermute | solution.py:41
  58.2 3.9 %collective-permute-start.15 = (f16[224,128]{1,0:T(8,128)(2,1)S(1)}, f16[224,128]{1,0:T(8,128)(2,1)S(1)}, u32[]{:S(2)}, u32[]{:S(2)}) collective-permute-start(f16[224,128]{1,0:T(8,128)(2,1)S(1)} %pad_maximum_fusion.11), channel_id=1, source_target_pairs={{0,65},{1,16},{2,19},{3,66},{4,69},{5,20},{6,23},{7,70},{8,73},{9,... | collective-permute-start | bytes 172040 | tf_op jit(solution)/shard_map/weight_sum/ppermute | solution.py:41
  59.0 5.2 %collective-permute-start.17 = (f16[224,128]{1,0:T(8,128)(2,1)S(1)}, f16[224,128]{1,0:T(8,128)(2,1)S(1)}, u32[]{:S(2)}, u32[]{:S(2)}) collective-permute-start(f16[224,128]{1,0:T(8,128)(2,1)S(1)} %pad_maximum_fusion.11), channel_id=1, source_target_pairs={{0,128},{1,33},{2,34},{3,131},{4,132},{5,37},{6,38},{7,135},{8,136... | collective-permute-start | bytes 172040 | tf_op jit(solution)/shard_map/weight_sum/ppermute | solution.py:41
  64.3 6.8 %collective-permute-start.21 = (f16[4,224,128]{2,1,0:T(8,128)(2,1)S(1)}, f16[4,224,128]{2,1,0:T(8,128)(2,1)S(1)}, u32[]{:S(2)}, u32[]{:S(2)}) collective-permute-start(f16[4,224,128]{2,1,0:T(8,128)(2,1)S(1)} %bitcast_dynamic-update-slice_fusion), channel_id=1, source_target_pairs={{0,32},{1,129},{2,130},{3,35},{4,36},{5,133},{6,134},{7,39},{8,40}... | collective-permute-start | bytes 688136 | tf_op jit(solution)/shard_map/weight_sum/ppermute | solution.py:41
  65.3 8.8 %collective-permute-start.20 = (f16[4,224,128]{2,1,0:T(8,128)(2,1)S(1)}, f16[4,224,128]{2,1,0:T(8,128)(2,1)S(1)}, u32[]{:S(2)}, u32[]{:S(2)}) collective-permute-start(f16[4,224,128]{2,1,0:T(8,128)(2,1)S(1)} %bitcast_dynamic-update-slice_fusion), channel_id=1, source_target_pairs={{0,49},{1,192},{2,195},{3,50},{4,53},{5,196},{6,199},{7,54},{8,57}... | collective-permute-start | bytes 688136 | tf_op jit(solution)/shard_map/weight_sum/ppermute | solution.py:41
  69.0 6.1 %collective-permute-start.18 = (f16[4,224,128]{2,1,0:T(8,128)(2,1)S(1)}, f16[4,224,128]{2,1,0:T(8,128)(2,1)S(1)}, u32[]{:S(2)}, u32[]{:S(2)}) collective-permute-start(f16[4,224,128]{2,1,0:T(8,128)(2,1)S(1)} %bitcast_dynamic-update-slice_fusion), channel_id=1, source_target_pairs={{0,17},{1,64},{2,67},{3,18},{4,21},{5,68},{6,71},{7,22},{8,25},{9,... | collective-permute-start | bytes 688136 | tf_op jit(solution)/shard_map/weight_sum/ppermute | solution.py:41
  75.3 2.9 %collective-permute-start.22 = (f16[2,4,224,128]{3,2,1,0:T(8,128)(2,1)S(1)}, f16[2,4,224,128]{3,2,1,0:T(8,128)(2,1)S(1)}, u32[]{:S(2)}, u32[]{:S(2)}) collective-permute-start(f16[2,4,224,128]{3,2,1,0:T(8,128)(2,1)S(1)} %pad_maximum_fusion.2), channel_id=1, source_target_pairs={{0,1},{1,0},{2,3},{3,2},{4,5},{5,4},{6,7},{7,6},{8,9},{9,8},{10,11... | collective-permute-start | bytes 1376264 | tf_op jit(solution)/shard_map/weight_sum/ppermute | solution.py:41
  76.7 2.0 %collective-permute-start.19 = (f16[2,4,224,128]{3,2,1,0:T(8,128)(2,1)S(1)}, f16[2,4,224,128]{3,2,1,0:T(8,128)(2,1)S(1)}, u32[]{:S(2)}, u32[]{:S(2)}) collective-permute-start(f16[2,4,224,128]{3,2,1,0:T(8,128)(2,1)S(1)} %pad_maximum_fusion.1), channel_id=1, source_target_pairs={{0,1},{1,0},{2,3},{3,2},{4,5},{5,4},{6,7},{7,6},{8,9},{9,8},{10,11... | collective-permute-start | bytes 1376264 | tf_op jit(solution)/shard_map/weight_sum/ppermute | solution.py:41

commit v5 on v4

--- a/solution.py
+++ b/solution.py
@@ -190,14 +190,13 @@
 
 
 def weight_kernel(
-    count, x_ref, g_ref, previous_ref, inner_ref, outer_ref,
-    own_ref, sent_ref, high_ref, low_ref, later_ref, box_ref,
+    count, x_ref, g_ref, previous_ref, inner_ref, outer_ref, box_ref,
+    own_ref, sent_ref, high_ref, low_ref, later_ref,
     frames, terms,
 ):
     used = count[0]
     core = lax.axis_index("tile") % 2
     half, first, second = position()
-    box_matrix(box_ref)
     frames[:, 0:256] = g_ref[...]
     frames[:, pl.ds(pl.multiple_of(288 - 32 * core, 32), 32)] = inner_ref[...]
     frames[:, pl.ds(pl.multiple_of(256 + 32 * core, 32), 32)] = outer_ref[...]
@@ -335,8 +334,18 @@
         previous = shifted(previous, 1, 0).reshape(128, 256)
         inner = swapped(inner, "core")
         outer = swapped(outer, "strip")
+    with jax.named_scope("box"):
+        box = pl.pallas_call(
+            box_matrix,
+            out_shape=jax.ShapeDtypeStruct((576, 320), BF16),
+            out_specs=near,
+            compiler_params=params,
+            cost_estimate=pl.CostEstimate(
+                flops=10**8, bytes_accessed=4 * 10**5, transcendentals=0
+            ),
+        )()
     with jax.named_scope("weight_terms"):
-        own, sent, high, low, later, box = pl.pallas_call(
+        own, sent, high, low, later = pl.pallas_call(
             weight_kernel,
             out_shape=(
                 jax.ShapeDtypeStruct((3464, 128), F32),
@@ -344,10 +353,9 @@
                 jax.ShapeDtypeStruct((512, 1152), BF16),
                 jax.ShapeDtypeStruct((512, 1152), BF16),
                 jax.ShapeDtypeStruct((2, 320, 128), BF16),
-                jax.ShapeDtypeStruct((576, 320), BF16),
             ),
-            in_specs=[scalars] + [near] * 5,
-            out_specs=(near,) * 6,
+            in_specs=[scalars] + [near] * 6,
+            out_specs=(near,) * 5,
             scratch_shapes=[
                 pltpu.VMEM((8, 320, 128), BF16),
                 pltpu.VMEM((6912, 128), F32),
@@ -356,7 +364,7 @@
             cost_estimate=pl.CostEstimate(
                 flops=3 * 10**9, bytes_accessed=10**7, transcendentals=0
             ),
-        )(frame_counts, latent.reshape(512, 256), cotangent, previous, inner, outer)
+        )(frame_counts, latent.reshape(512, 256), cotangent, previous, inner, outer, box)
     with jax.named_scope("halves"):
         exponent = fitting(sent[3456:3457])
         received = swapped(packed(sent[:3456], exponent, power(exponent)), "core")

time: 80.7 us -> 81.7 us (1.012)
  local copies, waits for them, and re-layouts: 2.33 us -> 3.37 us
    unnamed x6 -> x8, local copies, waits for them, and re-layouts: 1.99 us -> 3.03 us
where the time goes in v5:
time: 81.7 us; the launch traced here: 81.4 us
  starting transfers between devices  39.4 us (48%)
  waiting for transfers between devices  24.6 us (30%)
  Pallas kernels  9.61 us (12%)
  local copies, waits for them, and re-layouts  3.37 us (4%)
  other arithmetic  2.47 us (3%)
  between operations  1.93 us (2%)
    ppermute x21, starting transfers between devices, swapped(): lax.ppermute(value, BOTH, [pair for pair in pairs if pair[1] is not None])  34.2 us
    ppermute x21, waiting for transfers between devices, swapped(): lax.ppermute(value, BOTH, [pair for pair in pairs if pair[1] is not None])  24.6 us
    ppermute x2, starting transfers between devices, shifted(): return lax.ppermute(value, BOTH, pairs)  5.23 us
    pallas_call x1, Pallas kernels, shards(): pl.pallas_call(weight_kernel, out_shape=(jax.ShapeDtypeStruct((3464, 128)...  3.26 us
    unnamed x8, local copies, waits for them, and re-layouts  3.03 us
    pallas_call x2, Pallas kernels, stored(): pl.pallas_call(functools.partial(store_kernel, other), out_shape=jax.Shap...  2.52 us
    pallas_call x1, Pallas kernels, shards(): pl.pallas_call(input_kernel, out_shape=jax.ShapeDtypeStruct((512, 256), F...  1.95 us
    pallas_call x1, Pallas kernels, finished(): pl.pallas_call(later_kernel, out_shape=jax.ShapeDtypeStruct((512, 256), B...  1.71 us
  transfers between devices with their start and end apart: 23, of which 15 were waited for; matrix products, arithmetic and copies ran while one was open for 1% of the time, Pallas kernels for 6%

profile of v5, /device:TPU:1, one launch (start us, length us, event | category | flops | bytes accessed | tf_op | source)
XLA Modules:
  0.0 81.4 jit_solution(14210210058932688371)
XLA Ops:
  1.3 1.0 %copy-done.1 = bf16[8,8,32,128]{3,2,1,0:T(8,128)(2,1)S(1)} copy-done((bf16[8,8,32,128]{3,2,1,0:T(8,128)(2,1)S(1)}, bf16[8,8,32,128]{3,2,1,0:T(8,128)(2,1)}, u32[]{:S(2)}) %copy-start.1) | copy-done | bytes 524312
  2.3 0.9 %copy-done.3 = bf16[8,4,16,256]{3,2,1,0:T(8,128)(2,1)S(1)} copy-done((bf16[8,4,16,256]{3,2,1,0:T(8,128)(2,1)S(1)}, bf16[8,4,16,256]{3,2,1,0:T(8,128)(2,1)}, u32[]{:S(2)}) %copy-start.3) | copy-done | bytes 262168
  3.4 3.9 %collective-permute-start = (bf16[2,64,256]{2,1,0:T(8,128)(2,1)S(1)}, bf16[2,64,256]{2,1,0:T(8,128)(2,1)S(1)}, u32[]{:S(2)}, u32[]{:S(2)}) collective-permute-start(bf16[2,64,256]{2,1,0:T(8,128)(2,1)S(1)} %get-tuple-element.18), channel_id=1, source_target_pairs={{0,16},{1,17},{2,18},{3,19},{4,20},{5,21},{6,22},{7,23},{8,24},{9,... | collective-permute-start | bytes 196616 | tf_op jit(solution)/shard_map/edges/ppermute | solution.py:51
  7.3 1.0 %collective-permute-start.1 = (bf16[8,32,128]{2,1,0:T(8,128)(2,1)S(1)}, bf16[8,32,128]{2,1,0:T(8,128)(2,1)S(1)}, u32[]{:S(2)}, u32[]{:S(2)}) collective-permute-start(bf16[8,32,128]{2,1,0:T(8,128)(2,1)S(1)} %get-tuple-element.19), channel_id=1, source_target_pairs={{0,1},{1,0},{2,3},{3,2},{4,5},{5,4},{6,7},{7,6},{8,9},{9,8},{10,11... | collective-permute-start | bytes 196616 | tf_op jit(solution)/shard_map/edges/ppermute | solution.py:41
  8.4 3.4 %collective-permute-start.2 = (bf16[8,32,128]{2,1,0:T(8,128)(2,1)S(1)}, bf16[8,32,128]{2,1,0:T(8,128)(2,1)S(1)}, u32[]{:S(2)}, u32[]{:S(2)}) collective-permute-start(bf16[8,32,128]{2,1,0:T(8,128)(2,1)S(1)} %get-tuple-element.20), channel_id=1, source_target_pairs={{1,2},{2,1},{3,4},{4,3},{5,6},{6,5},{7,8},{8,7},{9,10},{10,9},{11,... | collective-permute-start | bytes 196616 | tf_op jit(solution)/shard_map/edges/ppermute | solution.py:41
  11.9 2.0 %collective-permute-done.2.outer_ref = bf16[8,32,128]{2,1,0:T(8,128)(2,1)S(1)} collective-permute-done((bf16[8,32,128]{2,1,0:T(8,128)(2,1)S(1)}, bf16[8,32,128]{2,1,0:T(8,128)(2,1)S(1)}, u32[]{:S(2)}, u32[]{:S(2)}) %collective-permute-start.2) | collective-permute-done | bytes 65568 | tf_op jit(solution)/shard_map/edges/ppermute | solution.py:41
  14.0 1.0 %copy-done.2 = bf16[8,8,32,128]{3,2,1,0:T(8,128)(2,1)S(1)} copy-done((bf16[8,8,32,128]{3,2,1,0:T(8,128)(2,1)S(1)}, bf16[8,8,32,128]{3,2,1,0:T(8,128)(2,1)}, u32[]{:S(2)}) %copy-start.2) | copy-done | bytes 524312
  15.0 3.3 %weight_terms.1 = (f32[3464,128]{1,0:T(8,128)S(1)}, f32[3464,128]{1,0:T(8,128)S(1)}, bf16[512,1152]{1,0:T(8,128)(2,1)S(1)}, bf16[512,1152]{1,0:T(8,128)(2,1)S(1)}, bf16[2,320,128]{2,1,0:T(8,128)(2,1)S(1)}) custom-call(s32[1]{0:T(128)S(6)} %copy.12.count, bf16[512,256]{1,0:T(8,128)(2,1)S(1)} %bitcast.68, bf16[8,256,128]{2,1,0:T(8,128)(2,1)S(1)} %bitcast.66, ...), custom_call_target="tpu_custom_call" | custom-call | flops 3000000000 | bytes 10000000 | tf_op jit(solution)/shard_map/weight_terms/pallas_call | solution.py:348
  18.3 0.2 multiply_convert_fusion
  18.5 0.2 pad_maximum_fusion
  18.8 2.4 %collective-permute-done.3 = f16[3464,128]{1,0:T(8,128)(2,1)S(1)} collective-permute-done((f16[3464,128]{1,0:T(8,128)(2,1)S(1)}, f16[3464,128]{1,0:T(8,128)(2,1)S(1)}, u32[]{:S(2)}, u32[]{:S(2)}) %collective-permute-start.3) | collective-permute-done | bytes 886816 | tf_op jit(solution)/shard_map/halves/ppermute | solution.py:41
  21.3 0.1 convert_multiply_fusion
  21.5 0.2 fusion.1
  21.7 0.2 pad_maximum_fusion.3
  21.9 3.0 %collective-permute-start.6 = (f16[872,128]{1,0:T(8,128)(2,1)S(1)}, f16[872,128]{1,0:T(8,128)(2,1)S(1)}, u32[]{:S(2)}, u32[]{:S(2)}) collective-permute-start(f16[872,128]{1,0:T(8,128)(2,1)S(1)} %get-tuple-element.69), channel_id=1, source_target_pairs={{0,32},{1,129},{2,130},{3,35},{4,36},{5,133},{6,134},{7,39},{8,40}... | collective-permute-start | bytes 669704 | tf_op jit(solution)/shard_map/weight_sum/ppermute | solution.py:41
  24.9 1.1 %collective-permute-start.5 = (f16[872,128]{1,0:T(8,128)(2,1)S(1)}, f16[872,128]{1,0:T(8,128)(2,1)S(1)}, u32[]{:S(2)}, u32[]{:S(2)}) collective-permute-start(f16[872,128]{1,0:T(8,128)(2,1)S(1)} %get-tuple-element.70), channel_id=1, source_target_pairs={{0,49},{1,192},{2,195},{3,50},{4,53},{5,196},{6,199},{7,54},{8,57}... | collective-permute-start | bytes 669704 | tf_op jit(solution)/shard_map/weight_sum/ppermute | solution.py:41
  26.0 1.3 %collective-permute-start.10 = (bf16[2,320,128]{2,1,0:T(8,128)(2,1)S(1)}, bf16[2,320,128]{2,1,0:T(8,128)(2,1)S(1)}, u32[]{:S(2)}, u32[]{:S(2)}) collective-permute-start(bf16[2,320,128]{2,1,0:T(8,128)(2,1)S(1)} %get-tuple-element.28), channel_id=1, source_target_pairs={{16,0},{17,1},{18,2},{19,3},{20,4},{21,5},{22,6},{23,7},{24,8},{25... | collective-permute-start | bytes 491528 | tf_op jit(solution)/shard_map/halves/ppermute | solution.py:51
  27.3 1.9 %input_terms.1.before_ref = f32[512,256]{1,0:T(8,128)S(1)} custom-call(bf16[27,256,128]{2,1,0:T(8,128)(2,1)S(1)} %copy-done, bf16[512,1152]{1,0:T(8,128)(2,1)S(1)} %get-tuple-element.23.high_ref, bf16[512,1152]{1,0:T(8,128)(2,1)S(1)} %get-tuple-element.24.low_ref), custom_call_target="tpu_custom_call" | custom-call | flops 2000000000 | bytes 5000000 | tf_op jit(solution)/shard_map/input_terms/pallas_call | solution.py:373
  29.2 2.3 %collective-permute-done.5 = f16[872,128]{1,0:T(8,128)(2,1)S(1)} collective-permute-done((f16[872,128]{1,0:T(8,128)(2,1)S(1)}, f16[872,128]{1,0:T(8,128)(2,1)S(1)}, u32[]{:S(2)}, u32[]{:S(2)}) %collective-permute-start.5) | collective-permute-done | bytes 223264 | tf_op jit(solution)/shard_map/weight_sum/ppermute | solution.py:41
  31.5 0.4 collective-permute-done.4
  31.9 0.2 fusion.7
  32.2 2.6 %collective-permute-start.9 = (f16[224,128]{1,0:T(8,128)(2,1)S(1)}, f16[224,128]{1,0:T(8,128)(2,1)S(1)}, u32[]{:S(2)}, u32[]{:S(2)}) collective-permute-start(f16[224,128]{1,0:T(8,128)(2,1)S(1)} %get-tuple-element.66), channel_id=1, source_target_pairs={{0,128},{1,33},{2,34},{3,131},{4,132},{5,37},{6,38},{7,135},{8,136... | collective-permute-start | bytes 172040 | tf_op jit(solution)/shard_map/weight_sum/ppermute | solution.py:41
  34.8 1.3 %collective-permute-start.8 = (f16[224,128]{1,0:T(8,128)(2,1)S(1)}, f16[224,128]{1,0:T(8,128)(2,1)S(1)}, u32[]{:S(2)}, u32[]{:S(2)}) collective-permute-start(f16[224,128]{1,0:T(8,128)(2,1)S(1)} %get-tuple-element.67), channel_id=1, source_target_pairs={{0,193},{1,48},{2,51},{3,194},{4,197},{5,52},{6,55},{7,198},{8,201... | collective-permute-start | bytes 172040 | tf_op jit(solution)/shard_map/weight_sum/ppermute | solution.py:41
  36.2 1.7 %weight_sum.3 = bf16[512,256]{1,0:T(8,128)(2,1)} custom-call(s32[1]{0:T(128)S(6)} %copy.12.count, bf16[27,256,128]{2,1,0:T(8,128)(2,1)S(1)} %copy-done, bf16[576,320]{1,0:T(8,128)(2,1)S(1)} %box.1.box_ref, bf16[2,320,128]{2,1,0:T(8,128)(2,1)S(1)} %collective-permute-done.10.later_ref, f32[512,256]{1,0:T(8,128)S(1)} %input_terms.1.before_ref), custom_call_target="tpu_custom_call" | custom-call | flops 500000000 | bytes 1000000 | tf_op jit(solution)/shard_map/weight_sum/pallas_call | solution.py:386
  37.9 2.1 %collective-permute-done.8 = f16[224,128]{1,0:T(8,128)(2,1)S(1)} collective-permute-done((f16[224,128]{1,0:T(8,128)(2,1)S(1)}, f16[224,128]{1,0:T(8,128)(2,1)S(1)}, u32[]{:S(2)}, u32[]{:S(2)}) %collective-permute-start.8) | collective-permute-done | bytes 57376 | tf_op jit(solution)/shard_map/weight_sum/ppermute | solution.py:41
  39.9 0.1 collective-permute-done.7
  40.2 1.5 %collective-permute-start.11 = (f16[224,128]{1,0:T(8,128)(2,1)S(1)}, f16[224,128]{1,0:T(8,128)(2,1)S(1)}, u32[]{:S(2)}, u32[]{:S(2)}) collective-permute-start(f16[224,128]{1,0:T(8,128)(2,1)S(1)} %pad_maximum_fusion.9), channel_id=1, source_target_pairs={{0,3},{1,2},{2,1},{3,0},{4,7},{5,6},{6,5},{7,4},{8,11},{9,10},{10,... | collective-permute-start | bytes 172040 | tf_op jit(solution)/shard_map/weight_sum/ppermute | solution.py:41
  41.7 3.0 %collective-permute-done.11 = f16[224,128]{1,0:T(8,128)(2,1)S(1)} collective-permute-done((f16[224,128]{1,0:T(8,128)(2,1)S(1)}, f16[224,128]{1,0:T(8,128)(2,1)S(1)}, u32[]{:S(2)}, u32[]{:S(2)}) %collective-permute-start.11) | collective-permute-done | bytes 57376 | tf_op jit(solution)/shard_map/weight_sum/ppermute | solution.py:41
  44.9 6.0 %collective-permute-start.14 = (f16[224,128]{1,0:T(8,128)(2,1)S(1)}, f16[224,128]{1,0:T(8,128)(2,1)S(1)}, u32[]{:S(2)}, u32[]{:S(2)}) collective-permute-start(f16[224,128]{1,0:T(8,128)(2,1)S(1)} %pad_maximum_fusion.10), channel_id=1, source_target_pairs={{0,12},{1,13},{2,6},{3,7},{4,0},{5,1},{6,10},{7,11},{8,4},{9,5},{1... | collective-permute-start | bytes 172040 | tf_op jit(solution)/shard_map/weight_sum/ppermute | solution.py:41
  50.9 3.7 %collective-permute-start.12 = (f16[224,128]{1,0:T(8,128)(2,1)S(1)}, f16[224,128]{1,0:T(8,128)(2,1)S(1)}, u32[]{:S(2)}, u32[]{:S(2)}) collective-permute-start(f16[224,128]{1,0:T(8,128)(2,1)S(1)} %pad_maximum_fusion.10), channel_id=1, source_target_pairs={{0,11},{1,10},{2,9},{3,8},{4,15},{5,14},{6,13},{7,12},{8,3},{9,2},... | collective-permute-start | bytes 172040 | tf_op jit(solution)/shard_map/weight_sum/ppermute | solution.py:41
  54.6 2.0 %collective-permute-done.13 = f16[224,128]{1,0:T(8,128)(2,1)S(1)} collective-permute-done((f16[224,128]{1,0:T(8,128)(2,1)S(1)}, f16[224,128]{1,0:T(8,128)(2,1)S(1)}, u32[]{:S(2)}, u32[]{:S(2)}) %collective-permute-start.13) | collective-permute-done | bytes 57376 | tf_op jit(solution)/shard_map/weight_sum/ppermute | solution.py:41
  56.6 2.0 %collective-permute-done.12 = f16[224,128]{1,0:T(8,128)(2,1)S(1)} collective-permute-done((f16[224,128]{1,0:T(8,128)(2,1)S(1)}, f16[224,128]{1,0:T(8,128)(2,1)S(1)}, u32[]{:S(2)}, u32[]{:S(2)}) %collective-permute-start.12) | collective-permute-done | bytes 57376 | tf_op jit(solution)/shard_map/weight_sum/ppermute | solution.py:41
  58.7 1.1 %collective-permute-start.16 = (f16[224,128]{1,0:T(8,128)(2,1)S(1)}, f16[224,128]{1,0:T(8,128)(2,1)S(1)}, u32[]{:S(2)}, u32[]{:S(2)}) collective-permute-start(f16[224,128]{1,0:T(8,128)(2,1)S(1)} %pad_maximum_fusion.11), channel_id=1, source_target_pairs={{0,193},{1,48},{2,51},{3,194},{4,197},{5,52},{6,55},{7,198},{8,201... | collective-permute-start | bytes 172040 | tf_op jit(solution)/shard_map/weight_sum/ppermute | solution.py:41
  59.8 0.2 collective-permute-start.15
  60.0 2.9 %collective-permute-start.17 = (f16[224,128]{1,0:T(8,128)(2,1)S(1)}, f16[224,128]{1,0:T(8,128)(2,1)S(1)}, u32[]{:S(2)}, u32[]{:S(2)}) collective-permute-start(f16[224,128]{1,0:T(8,128)(2,1)S(1)} %pad_maximum_fusion.11), channel_id=1, source_target_pairs={{0,128},{1,33},{2,34},{3,131},{4,132},{5,37},{6,38},{7,135},{8,136... | collective-permute-start | bytes 172040 | tf_op jit(solution)/shard_map/weight_sum/ppermute | solution.py:41
  63.0 0.7 collective-permute-done.15
  63.8 1.4 %collective-permute-done.17 = f16[224,128]{1,0:T(8,128)(2,1)S(1)} collective-permute-done((f16[224,128]{1,0:T(8,128)(2,1)S(1)}, f16[224,128]{1,0:T(8,128)(2,1)S(1)}, u32[]{:S(2)}, u32[]{:S(2)}) %collective-permute-start.17) | collective-permute-done | bytes 57376 | tf_op jit(solution)/shard_map/weight_sum/ppermute | solution.py:41
  65.2 1.1 %collective-permute-start.21 = (f16[4,224,128]{2,1,0:T(8,128)(2,1)S(1)}, f16[4,224,128]{2,1,0:T(8,128)(2,1)S(1)}, u32[]{:S(2)}, u32[]{:S(2)}) collective-permute-start(f16[4,224,128]{2,1,0:T(8,128)(2,1)S(1)} %bitcast_dynamic-update-slice_fusion), channel_id=1, source_target_pairs={{0,32},{1,129},{2,130},{3,35},{4,36},{5,133},{6,134},{7,39},{8,40}... | collective-permute-start | bytes 688136 | tf_op jit(solution)/shard_map/weight_sum/ppermute | solution.py:41
  66.3 3.7 %collective-permute-start.20 = (f16[4,224,128]{2,1,0:T(8,128)(2,1)S(1)}, f16[4,224,128]{2,1,0:T(8,128)(2,1)S(1)}, u32[]{:S(2)}, u32[]{:S(2)}) collective-permute-start(f16[4,224,128]{2,1,0:T(8,128)(2,1)S(1)} %bitcast_dynamic-update-slice_fusion), channel_id=1, source_target_pairs={{0,49},{1,192},{2,195},{3,50},{4,53},{5,196},{6,199},{7,54},{8,57}... | collective-permute-start | bytes 688136 | tf_op jit(solution)/shard_map/weight_sum/ppermute | solution.py:41
  70.0 1.9 %collective-permute-done.21 = f16[4,224,128]{2,1,0:T(8,128)(2,1)S(1)} collective-permute-done((f16[4,224,128]{2,1,0:T(8,128)(2,1)S(1)}, f16[4,224,128]{2,1,0:T(8,128)(2,1)S(1)}, u32[]{:S(2)}, u32[]{:S(2)}) %collective-permute-start.21) | collective-permute-done | bytes 229408 | tf_op jit(solution)/shard_map/weight_sum/ppermute | solution.py:41
  72.0 3.1 %collective-permute-done.20 = f16[4,224,128]{2,1,0:T(8,128)(2,1)S(1)} collective-permute-done((f16[4,224,128]{2,1,0:T(8,128)(2,1)S(1)}, f16[4,224,128]{2,1,0:T(8,128)(2,1)S(1)}, u32[]{:S(2)}, u32[]{:S(2)}) %collective-permute-start.20) | collective-permute-done | bytes 229408 | tf_op jit(solution)/shard_map/weight_sum/ppermute | solution.py:41
  75.1 1.0 %collective-permute-done.18 = f16[4,224,128]{2,1,0:T(8,128)(2,1)S(1)} collective-permute-done((f16[4,224,128]{2,1,0:T(8,128)(2,1)S(1)}, f16[4,224,128]{2,1,0:T(8,128)(2,1)S(1)}, u32[]{:S(2)}, u32[]{:S(2)}) %collective-permute-start.18) | collective-permute-done | bytes 229408 | tf_op jit(solution)/shard_map/weight_sum/ppermute | solution.py:41
  76.2 0.1 pad_maximum_fusion.2
  76.3 1.3 %collective-permute-start.22 = (f16[2,4,224,128]{3,2,1,0:T(8,128)(2,1)S(1)}, f16[2,4,224,128]{3,2,1,0:T(8,128)(2,1)S(1)}, u32[]{:S(2)}, u32[]{:S(2)}) collective-permute-start(f16[2,4,224,128]{3,2,1,0:T(8,128)(2,1)S(1)} %pad_maximum_fusion.2), channel_id=1, source_target_pairs={{0,1},{1,0},{2,3},{3,2},{4,5},{5,4},{6,7},{7,6},{8,9},{9,8},{10,11... | collective-permute-start | bytes 1376264 | tf_op jit(solution)/shard_map/weight_sum/ppermute | solution.py:41
  77.6 0.1 pad_maximum_fusion.1
  77.9 1.3 %weight_sum.4.refs_4_ = f32[2,4,4,216,128]{4,3,2,1,0:T(8,128)} custom-call(f32[4,216,128]{2,1,0:T(8,128)S(1)} %convert_multiply_fusion.4.refs_0_, f32[4,216,128]{2,1,0:T(8,128)S(1)} %convert_multiply_fusion.3.refs_1_, f32[4,216,128]{2,1,0:T(8,128)S(1)} %convert_multiply_fusion.2.refs_2_, f32[4,216,128]{2,1,0:T(8,128)S(1)} %convert_multiply_fusion.1.refs_3_), custom_call_target="tpu_custom_call" | custom-call | bytes 4000000 | tf_op jit(solution)/shard_map/weight_sum/pallas_call | solution.py:301
  79.4 0.3 collective-permute-done.19
  80.0 1.3 %weight_sum.5 = f32[2,4,4,216,128]{4,3,2,1,0:T(8,128)} custom-call(f32[4,216,128]{2,1,0:T(8,128)S(1)} %get-tuple-element.77.refs_0_, f32[4,216,128]{2,1,0:T(8,128)S(1)} %get-tuple-element.76.refs_1_, f32[4,216,128]{2,1,0:T(8,128)S(1)} %get-tuple-element.79.refs_2_, f32[4,216,128]{2,1,0:T(8,128)S(1)} %get-tuple-element.78.refs_3_, ...), custom_call_target="tpu_custom_call", output_to_operand_aliasing={{}: (4, {})} | custom-call | bytes 4000000 | tf_op jit(solution)/shard_map/weight_sum/pallas_call | solution.py:301
  (77 shorter events, 1.9 us)
Async XLA Ops:
  1.3 1.0 %copy-start.1 = (bf16[8,8,32,128]{3,2,1,0:T(8,128)(2,1)S(1)}, bf16[8,8,32,128]{3,2,1,0:T(8,128)(2,1)}, u32[]{:S(2)}) copy-start(bf16[8,8,32,128]{3,2,1,0:T(8,128)(2,1)} %param.5) | copy-start | bytes 1572868
  2.3 0.9 %copy-start.3 = (bf16[8,4,16,256]{3,2,1,0:T(8,128)(2,1)S(1)}, bf16[8,4,16,256]{3,2,1,0:T(8,128)(2,1)}, u32[]{:S(2)}) copy-start(bf16[8,4,16,256]{3,2,1,0:T(8,128)(2,1)} %param.4) | copy-start | bytes 786436
  3.4 8.5 %collective-permute-start = (bf16[2,64,256]{2,1,0:T(8,128)(2,1)S(1)}, bf16[2,64,256]{2,1,0:T(8,128)(2,1)S(1)}, u32[]{:S(2)}, u32[]{:S(2)}) collective-permute-start(bf16[2,64,256]{2,1,0:T(8,128)(2,1)S(1)} %get-tuple-element.18), channel_id=1, source_target_pairs={{0,16},{1,17},{2,18},{3,19},{4,20},{5,21},{6,22},{7,23},{8,24},{9,... | collective-permute-start | bytes 196616 | tf_op jit(solution)/shard_map/edges/ppermute | solution.py:51
  7.3 4.6 %collective-permute-start.1 = (bf16[8,32,128]{2,1,0:T(8,128)(2,1)S(1)}, bf16[8,32,128]{2,1,0:T(8,128)(2,1)S(1)}, u32[]{:S(2)}, u32[]{:S(2)}) collective-permute-start(bf16[8,32,128]{2,1,0:T(8,128)(2,1)S(1)} %get-tuple-element.19), channel_id=1, source_target_pairs={{0,1},{1,0},{2,3},{3,2},{4,5},{5,4},{6,7},{7,6},{8,9},{9,8},{10,11... | collective-permute-start | bytes 196616 | tf_op jit(solution)/shard_map/edges/ppermute | solution.py:41
  8.4 5.6 %collective-permute-start.2 = (bf16[8,32,128]{2,1,0:T(8,128)(2,1)S(1)}, bf16[8,32,128]{2,1,0:T(8,128)(2,1)S(1)}, u32[]{:S(2)}, u32[]{:S(2)}) collective-permute-start(bf16[8,32,128]{2,1,0:T(8,128)(2,1)S(1)} %get-tuple-element.20), channel_id=1, source_target_pairs={{1,2},{2,1},{3,4},{4,3},{5,6},{6,5},{7,8},{8,7},{9,10},{10,9},{11,... | collective-permute-start | bytes 196616 | tf_op jit(solution)/shard_map/edges/ppermute | solution.py:41
  14.0 1.0 %copy-start.2 = (bf16[8,8,32,128]{3,2,1,0:T(8,128)(2,1)S(1)}, bf16[8,8,32,128]{3,2,1,0:T(8,128)(2,1)}, u32[]{:S(2)}) copy-start(bf16[8,8,32,128]{3,2,1,0:T(8,128)(2,1)} %param.5) | copy-start | bytes 1572868
  18.7 2.5 %collective-permute-start.3 = (f16[3464,128]{1,0:T(8,128)(2,1)S(1)}, f16[3464,128]{1,0:T(8,128)(2,1)S(1)}, u32[]{:S(2)}, u32[]{:S(2)}) collective-permute-start(f16[3464,128]{1,0:T(8,128)(2,1)S(1)} %pad_maximum_fusion), channel_id=1, source_target_pairs={{0,1},{1,0},{2,3},{3,2},{4,5},{5,4},{6,7},{7,6},{8,9},{9,8},{10,11... | collective-permute-start | bytes 2660360 | tf_op jit(solution)/shard_map/halves/ppermute | solution.py:41
  21.4 5.8 %copy-start = (bf16[27,256,128]{2,1,0:T(8,128)(2,1)S(1)}, bf16[27,256,128]{2,1,0:T(8,128)(2,1)}, u32[]{:S(2)}) copy-start(bf16[27,256,128]{2,1,0:T(8,128)(2,1)} %weight_ref.3) | copy-start | bytes 5308420
  21.9 7.4 %collective-permute-start.6 = (f16[872,128]{1,0:T(8,128)(2,1)S(1)}, f16[872,128]{1,0:T(8,128)(2,1)S(1)}, u32[]{:S(2)}, u32[]{:S(2)}) collective-permute-start(f16[872,128]{1,0:T(8,128)(2,1)S(1)} %get-tuple-element.69), channel_id=1, source_target_pairs={{0,32},{1,129},{2,130},{3,35},{4,36},{5,133},{6,134},{7,39},{8,40}... | collective-permute-start | bytes 669704 | tf_op jit(solution)/shard_map/weight_sum/ppermute | solution.py:41
  24.9 6.7 %collective-permute-start.5 = (f16[872,128]{1,0:T(8,128)(2,1)S(1)}, f16[872,128]{1,0:T(8,128)(2,1)S(1)}, u32[]{:S(2)}, u32[]{:S(2)}) collective-permute-start(f16[872,128]{1,0:T(8,128)(2,1)S(1)} %get-tuple-element.70), channel_id=1, source_target_pairs={{0,49},{1,192},{2,195},{3,50},{4,53},{5,196},{6,199},{7,54},{8,57}... | collective-permute-start | bytes 669704 | tf_op jit(solution)/shard_map/weight_sum/ppermute | solution.py:41
  26.0 5.9 %collective-permute-start.4 = (f16[872,128]{1,0:T(8,128)(2,1)S(1)}, f16[872,128]{1,0:T(8,128)(2,1)S(1)}, u32[]{:S(2)}, u32[]{:S(2)}) collective-permute-start(f16[872,128]{1,0:T(8,128)(2,1)S(1)} %get-tuple-element.71), channel_id=1, source_target_pairs={{0,17},{1,64},{2,67},{3,18},{4,21},{5,68},{6,71},{7,22},{8,25},{9,... | collective-permute-start | bytes 669704 | tf_op jit(solution)/shard_map/weight_sum/ppermute | solution.py:41
  26.0 10.2 %collective-permute-start.10 = (bf16[2,320,128]{2,1,0:T(8,128)(2,1)S(1)}, bf16[2,320,128]{2,1,0:T(8,128)(2,1)S(1)}, u32[]{:S(2)}, u32[]{:S(2)}) collective-permute-start(bf16[2,320,128]{2,1,0:T(8,128)(2,1)S(1)} %get-tuple-element.28), channel_id=1, source_target_pairs={{16,0},{17,1},{18,2},{19,3},{20,4},{21,5},{22,6},{23,7},{24,8},{25... | collective-permute-start | bytes 491528 | tf_op jit(solution)/shard_map/halves/ppermute | solution.py:51
  32.2 5.6 %collective-permute-start.9 = (f16[224,128]{1,0:T(8,128)(2,1)S(1)}, f16[224,128]{1,0:T(8,128)(2,1)S(1)}, u32[]{:S(2)}, u32[]{:S(2)}) collective-permute-start(f16[224,128]{1,0:T(8,128)(2,1)S(1)} %get-tuple-element.66), channel_id=1, source_target_pairs={{0,128},{1,33},{2,34},{3,131},{4,132},{5,37},{6,38},{7,135},{8,136... | collective-permute-start | bytes 172040 | tf_op jit(solution)/shard_map/weight_sum/ppermute | solution.py:41
  34.8 5.1 %collective-permute-start.8 = (f16[224,128]{1,0:T(8,128)(2,1)S(1)}, f16[224,128]{1,0:T(8,128)(2,1)S(1)}, u32[]{:S(2)}, u32[]{:S(2)}) collective-permute-start(f16[224,128]{1,0:T(8,128)(2,1)S(1)} %get-tuple-element.67), channel_id=1, source_target_pairs={{0,193},{1,48},{2,51},{3,194},{4,197},{5,52},{6,55},{7,198},{8,201... | collective-permute-start | bytes 172040 | tf_op jit(solution)/shard_map/weight_sum/ppermute | solution.py:41
  36.1 3.9 %collective-permute-start.7 = (f16[224,128]{1,0:T(8,128)(2,1)S(1)}, f16[224,128]{1,0:T(8,128)(2,1)S(1)}, u32[]{:S(2)}, u32[]{:S(2)}) collective-permute-start(f16[224,128]{1,0:T(8,128)(2,1)S(1)} %get-tuple-element.68), channel_id=1, source_target_pairs={{0,65},{1,16},{2,19},{3,66},{4,69},{5,20},{6,23},{7,70},{8,73},{9,... | collective-permute-start | bytes 172040 | tf_op jit(solution)/shard_map/weight_sum/ppermute | solution.py:41
  40.2 4.6 %collective-permute-start.11 = (f16[224,128]{1,0:T(8,128)(2,1)S(1)}, f16[224,128]{1,0:T(8,128)(2,1)S(1)}, u32[]{:S(2)}, u32[]{:S(2)}) collective-permute-start(f16[224,128]{1,0:T(8,128)(2,1)S(1)} %pad_maximum_fusion.9), channel_id=1, source_target_pairs={{0,3},{1,2},{2,1},{3,0},{4,7},{5,6},{6,5},{7,4},{8,11},{9,10},{10,... | collective-permute-start | bytes 172040 | tf_op jit(solution)/shard_map/weight_sum/ppermute | solution.py:41
  44.9 9.7 %collective-permute-start.14 = (f16[224,128]{1,0:T(8,128)(2,1)S(1)}, f16[224,128]{1,0:T(8,128)(2,1)S(1)}, u32[]{:S(2)}, u32[]{:S(2)}) collective-permute-start(f16[224,128]{1,0:T(8,128)(2,1)S(1)} %pad_maximum_fusion.10), channel_id=1, source_target_pairs={{0,12},{1,13},{2,6},{3,7},{4,0},{5,1},{6,10},{7,11},{8,4},{9,5},{1... | collective-permute-start | bytes 172040 | tf_op jit(solution)/shard_map/weight_sum/ppermute | solution.py:41
  50.9 5.7 %collective-permute-start.13 = (f16[224,128]{1,0:T(8,128)(2,1)S(1)}, f16[224,128]{1,0:T(8,128)(2,1)S(1)}, u32[]{:S(2)}, u32[]{:S(2)}) collective-permute-start(f16[224,128]{1,0:T(8,128)(2,1)S(1)} %pad_maximum_fusion.10), channel_id=1, source_target_pairs={{0,15},{1,14},{2,5},{3,4},{4,3},{5,2},{6,9},{7,8},{8,7},{9,6},{10,... | collective-permute-start | bytes 172040 | tf_op jit(solution)/shard_map/weight_sum/ppermute | solution.py:41
  50.9 7.7 %collective-permute-start.12 = (f16[224,128]{1,0:T(8,128)(2,1)S(1)}, f16[224,128]{1,0:T(8,128)(2,1)S(1)}, u32[]{:S(2)}, u32[]{:S(2)}) collective-permute-start(f16[224,128]{1,0:T(8,128)(2,1)S(1)} %pad_maximum_fusion.10), channel_id=1, source_target_pairs={{0,11},{1,10},{2,9},{3,8},{4,15},{5,14},{6,13},{7,12},{8,3},{9,2},... | collective-permute-start | bytes 172040 | tf_op jit(solution)/shard_map/weight_sum/ppermute | solution.py:41
  58.7 5.0 %collective-permute-start.16 = (f16[224,128]{1,0:T(8,128)(2,1)S(1)}, f16[224,128]{1,0:T(8,128)(2,1)S(1)}, u32[]{:S(2)}, u32[]{:S(2)}) collective-permute-start(f16[224,128]{1,0:T(8,128)(2,1)S(1)} %pad_maximum_fusion.11), channel_id=1, source_target_pairs={{0,193},{1,48},{2,51},{3,194},{4,197},{5,52},{6,55},{7,198},{8,201... | collective-permute-start | bytes 172040 | tf_op jit(solution)/shard_map/weight_sum/ppermute | solution.py:41
  59.8 3.9 %collective-permute-start.15 = (f16[224,128]{1,0:T(8,128)(2,1)S(1)}, f16[224,128]{1,0:T(8,128)(2,1)S(1)}, u32[]{:S(2)}, u32[]{:S(2)}) collective-permute-start(f16[224,128]{1,0:T(8,128)(2,1)S(1)} %pad_maximum_fusion.11), channel_id=1, source_target_pairs={{0,65},{1,16},{2,19},{3,66},{4,69},{5,20},{6,23},{7,70},{8,73},{9,... | collective-permute-start | bytes 172040 | tf_op jit(solution)/shard_map/weight_sum/ppermute | solution.py:41
  60.0 5.1 %collective-permute-start.17 = (f16[224,128]{1,0:T(8,128)(2,1)S(1)}, f16[224,128]{1,0:T(8,128)(2,1)S(1)}, u32[]{:S(2)}, u32[]{:S(2)}) collective-permute-start(f16[224,128]{1,0:T(8,128)(2,1)S(1)} %pad_maximum_fusion.11), channel_id=1, source_target_pairs={{0,128},{1,33},{2,34},{3,131},{4,132},{5,37},{6,38},{7,135},{8,136... | collective-permute-start | bytes 172040 | tf_op jit(solution)/shard_map/weight_sum/ppermute | solution.py:41
  65.2 6.8 %collective-permute-start.21 = (f16[4,224,128]{2,1,0:T(8,128)(2,1)S(1)}, f16[4,224,128]{2,1,0:T(8,128)(2,1)S(1)}, u32[]{:S(2)}, u32[]{:S(2)}) collective-permute-start(f16[4,224,128]{2,1,0:T(8,128)(2,1)S(1)} %bitcast_dynamic-update-slice_fusion), channel_id=1, source_target_pairs={{0,32},{1,129},{2,130},{3,35},{4,36},{5,133},{6,134},{7,39},{8,40}... | collective-permute-start | bytes 688136 | tf_op jit(solution)/shard_map/weight_sum/ppermute | solution.py:41
  66.3 8.8 %collective-permute-start.20 = (f16[4,224,128]{2,1,0:T(8,128)(2,1)S(1)}, f16[4,224,128]{2,1,0:T(8,128)(2,1)S(1)}, u32[]{:S(2)}, u32[]{:S(2)}) collective-permute-start(f16[4,224,128]{2,1,0:T(8,128)(2,1)S(1)} %bitcast_dynamic-update-slice_fusion), channel_id=1, source_target_pairs={{0,49},{1,192},{2,195},{3,50},{4,53},{5,196},{6,199},{7,54},{8,57}... | collective-permute-start | bytes 688136 | tf_op jit(solution)/shard_map/weight_sum/ppermute | solution.py:41
  70.0 6.1 %collective-permute-start.18 = (f16[4,224,128]{2,1,0:T(8,128)(2,1)S(1)}, f16[4,224,128]{2,1,0:T(8,128)(2,1)S(1)}, u32[]{:S(2)}, u32[]{:S(2)}) collective-permute-start(f16[4,224,128]{2,1,0:T(8,128)(2,1)S(1)} %bitcast_dynamic-update-slice_fusion), channel_id=1, source_target_pairs={{0,17},{1,64},{2,67},{3,18},{4,21},{5,68},{6,71},{7,22},{8,25},{9,... | collective-permute-start | bytes 688136 | tf_op jit(solution)/shard_map/weight_sum/ppermute | solution.py:41
  76.3 2.9 %collective-permute-start.22 = (f16[2,4,224,128]{3,2,1,0:T(8,128)(2,1)S(1)}, f16[2,4,224,128]{3,2,1,0:T(8,128)(2,1)S(1)}, u32[]{:S(2)}, u32[]{:S(2)}) collective-permute-start(f16[2,4,224,128]{3,2,1,0:T(8,128)(2,1)S(1)} %pad_maximum_fusion.2), channel_id=1, source_target_pairs={{0,1},{1,0},{2,3},{3,2},{4,5},{5,4},{6,7},{7,6},{8,9},{9,8},{10,11... | collective-permute-start | bytes 1376264 | tf_op jit(solution)/shard_map/weight_sum/ppermute | solution.py:41
  77.7 2.0 %collective-permute-start.19 = (f16[2,4,224,128]{3,2,1,0:T(8,128)(2,1)S(1)}, f16[2,4,224,128]{3,2,1,0:T(8,128)(2,1)S(1)}, u32[]{:S(2)}, u32[]{:S(2)}) collective-permute-start(f16[2,4,224,128]{3,2,1,0:T(8,128)(2,1)S(1)} %pad_maximum_fusion.1), channel_id=1, source_target_pairs={{0,1},{1,0},{2,3},{3,2},{4,5},{5,4},{6,7},{7,6},{8,9},{9,8},{10,11... | collective-permute-start | bytes 1376264 | tf_op jit(solution)/shard_map/weight_sum/ppermute | solution.py:41
